TPU v7x, 512 devices: a whole 4x8x8 slice. The times are simulated.
512 devices in a mesh: seq: 64 (over z, y), chan: 8 (over x, core).
Axes of the slice: x: 4, y: 8, z: 8, core: 2. Of those that a mesh axis runs over, the one named last changes fastest.
Arguments:
- d_out: bfloat16 [12288, 4096], P('seq', 'chan'), may hold values from -6 to 6
- x_branch: bfloat16 [12288, 4096], P('seq', 'chan'), may hold values from -6 to 6
- gate_branch: bfloat16 [12288, 4096], P('seq', 'chan'), may hold values from -5 to 5
- recurrence_gate: bfloat16 [12288, 4096], P('seq', 'chan'), may hold values from -6 to 6
- input_gate: bfloat16 [12288, 4096], P('seq', 'chan'), may hold values from -6 to 6
- conv_weight: float32 [4, 4096], P(None, 'chan'), may hold values from -3 to 3
- conv_bias: float32 [4096], P('chan'), may hold values from -3 to 3
- decay_level: int32 [4096], P('chan'), may hold values from 0 to 15
- w_in: bfloat16 [4096, 4096], P(('chan', 'seq')), may hold values from -0.09375 to 0.09375
- w_out: bfloat16 [4096, 4096], P(('chan', 'seq')), may hold values from -0.09375 to 0.09375
Outputs:
- d_input: bfloat16 [12288, 4096], P('seq', 'chan')
- d_gate: bfloat16 [12288, 4096], P('seq', 'chan')
- d_recurrence_gate: bfloat16 [12288, 4096], P('seq', 'chan')
- d_input_gate: bfloat16 [12288, 4096], P('seq', 'chan')
All inputs are finite; a program needn't handle non-finite values.
Results may differ from a plain program's by a relative error of at most 0.017.
Values may be sent and summed in bfloat16 or wider, within the bound.
No kernel may reach another device: no remote copies, remote signals or barrier semaphores. Data moves between devices by JAX's collectives and lax.ppermute only.
A program may use at most 64 MiB of HBM per device.

v0:
```python
import jax
import jax.numpy as jnp
from jax import lax
from jax.sharding import PartitionSpec as P

LEVELS = 16


def from_behind(value, axis, steps):
    count = lax.axis_size(axis)
    initial, last = (max(0, -steps), min(count, count - steps))
    return lax.ppermute(value, axis, [(source, source + steps) for source in range(initial, last)])


def prefix(part, axis, combine, identity, reverse):
    count = lax.axis_size(axis)
    place = lax.axis_index(axis)
    ahead = count - 1 - place if reverse else place
    gathered = jax.tree.map(lambda a: lax.all_gather(a, axis), part)
    state = jax.tree.map(lambda a, e: jnp.zeros_like(a) + jnp.asarray(e, a.dtype), part, identity)

    def one(lap, state):
        source = count - 1 - lap if reverse else lap
        return combine(
            state, jax.tree.map(lambda a: lax.dynamic_index_in_dim(a, source, 0, False), gathered)
        )

    return lax.fori_loop(0, ahead, one, state)


def decay_table(length):
    levels = jnp.arange(LEVELS).astype(jnp.float32)
    half = LEVELS // 2
    slow_rates = 0.25 * jnp.power(16.0, levels / (half - 1.0)) / (8.0 * length)
    fast_rates = jnp.power(4.0, (levels - half) / (half - 1.0)) / 640.0
    return -jnp.where(levels < half, slow_rates, fast_rates)


def combine_affine(earlier, later):
    return (earlier[0] * later[0], later[0] * earlier[1] + later[1])


def gelu_parts(gate):
    normal_cdf = 0.5 * (1.0 + lax.erf(gate * 0.7071067811865476))
    density = jnp.exp(-0.5 * gate * gate) * 0.3989422804014327
    return (gate * normal_cdf, normal_cdf + gate * density)


def shards(
    d_out,
    x_branch,
    gate_branch,
    recurrence_gate,
    input_gate,
    conv_weight,
    conv_bias,
    decay_level,
    w_in,
    w_out,
):
    tok_rows, chan_width = x_branch.shape
    seq_count = lax.axis_size("seq")
    chan_count = lax.axis_size("chan")
    log_table = decay_table(tok_rows * seq_count)
    onehot = decay_level[:, None] == jnp.arange(LEVELS)[None, :]
    log_decay = jnp.sum(jnp.where(onehot, log_table[None, :], 0.0), axis=1)
    input_pieces = lax.all_to_all(w_in, "chan", split_axis=1, concat_axis=0, tiled=True)
    out_rows, mixed_rows = (
        lax.all_gather(w_out, "seq", axis=0, tiled=True),
        lax.all_gather(input_pieces, "seq", axis=0, tiled=True),
    )
    in_rows = (
        mixed_rows.reshape(seq_count, chan_count, -1, chan_width)
        .transpose(1, 0, 2, 3)
        .reshape(-1, chan_width)
    )
    full_out = lax.all_gather(d_out, "chan", axis=1, tiled=True)
    d_lru = lax.dot_general(
        full_out, out_rows, (((1,), (1,)), ((), ())), preferred_element_type=jnp.float32
    )
    previous = from_behind(x_branch[tok_rows - 3 :], "seq", 1)
    padded = jnp.concatenate([previous, x_branch], axis=0).astype(jnp.float32)
    conv_out = conv_bias + sum(
        (conv_weight[offset] * padded[3 - offset : 3 - offset + tok_rows] for offset in range(4))
    )
    recur = jax.nn.sigmoid(recurrence_gate.astype(jnp.float32))
    inward = jax.nn.sigmoid(input_gate.astype(jnp.float32))
    log_step = 8.0 * recur * log_decay
    decay = jnp.exp(log_step)
    beta = jnp.sqrt(-jnp.expm1(2.0 * log_step))
    gated_in = inward * conv_out
    gelu_gate, gelu_slope = gelu_parts(gate_branch.astype(jnp.float32))
    d_direct = d_lru * gelu_gate
    cum_decay, local_states = lax.associative_scan(combine_affine, (decay, beta * gated_in), axis=0)
    post_decay, local_kappa = lax.associative_scan(
        combine_affine, (decay, decay * d_direct), axis=0, reverse=True
    )
    block_prod = cum_decay[tok_rows - 1]
    state_end = local_states[tok_rows - 1]
    kappa_first = local_kappa[0]
    ones_row = jnp.ones((chan_width,), jnp.float32)
    zeros_row = jnp.zeros((chan_width,), jnp.float32)
    carried_state = prefix(
        (block_prod, state_end), "seq", combine_affine, (ones_row, zeros_row), False
    )[1]
    carried_kappa = prefix(
        (block_prod, kappa_first), "seq", combine_affine, (ones_row, zeros_row), True
    )[1]
    states = local_states + cum_decay * carried_state[None, :]
    kappa = local_kappa + post_decay * carried_kappa[None, :]
    d_gate = (d_lru * states * gelu_slope).astype(jnp.bfloat16)
    adjoint = d_direct + jnp.concatenate([kappa[1:], carried_kappa[None, :]], axis=0)
    states_prev = jnp.concatenate([carried_state[None, :], states[:-1]], axis=0)
    d_step = adjoint * (decay * states_prev - gated_in * decay * decay / beta)
    d_recurrence_gate = (d_step * 8.0 * log_decay * recur * (1.0 - recur)).astype(jnp.bfloat16)
    d_gated = adjoint * beta
    d_input_gate = (d_gated * conv_out * inward * (1.0 - inward)).astype(jnp.bfloat16)
    d_conv = d_gated * inward
    following = from_behind(d_conv[:3], "seq", -1)
    padded_after = jnp.concatenate([d_conv, following], axis=0)
    d_branch = sum(
        (conv_weight[offset] * padded_after[offset : offset + tok_rows] for offset in range(4))
    ).astype(jnp.bfloat16)
    term = lax.dot_general(
        in_rows, d_branch, (((1,), (1,)), ((), ())), preferred_element_type=jnp.float32
    ).astype(jnp.bfloat16)
    term = lax.optimization_barrier(term)
    summed = lax.psum_scatter(
        term.astype(jnp.float32).astype(jnp.bfloat16), "chan", scatter_dimension=0, tiled=True
    ).astype(jnp.float32)
    d_input = summed.T.astype(jnp.bfloat16)
    return (d_input, d_gate, d_recurrence_gate, d_input_gate)


def solution(mesh):
    in_specs = (
        P("seq", "chan"),
        P("seq", "chan"),
        P("seq", "chan"),
        P("seq", "chan"),
        P("seq", "chan"),
        P(None, "chan"),
        P("chan"),
        P("chan"),
        P(("chan", "seq"), None),
        P(("chan", "seq"), None),
    )
    out_specs = (P("seq", "chan"), P("seq", "chan"), P("seq", "chan"), P("seq", "chan"))
    return jax.shard_map(shards, mesh=mesh, in_specs=in_specs, out_specs=out_specs, check_vma=False)
```

profile of v0, /device:TPU:1, one launch (start us, length us, event | category | flops | bytes accessed | tf_op | source)
XLA Modules:
  0.0 440.4 jit_solution(1875017195785866505)
XLA Ops:
  7.2 0.7 all-gather.7.cloned.1.call-update
  7.9 0.7 all-gather.9.cloned.1.call-update
  8.6 0.7 slice.601
  9.4 4.0 collective-permute-start.1
  13.4 7.4 %all-to-all-start = ((bf16[8,8,512]{2,0,1:T(8,128)(2,1)}), bf16[8,8,512]{2,0,1:T(8,128)(2,1)S(1)}, u32[]{:S(2)}, u32[]{:S(2)}) async-start(bf16[8,8,512]{2,0,1:T(8,128)(2,1)} %bitcast.62), calls=%async_computation | async-start | bytes 131072 | tf_op jit(solution)/shard_map/all_to_all | solution.py:67
  20.8 0.8 select_reduce_fusion
  21.6 1.5 fusion.69
  23.0 1.0 maximum_convert_fusion
  24.0 1.6 all-to-all-done
  26.3 19.4 %all-gather.7.cloned.1.call-done = bf16[192,4096]{1,0:T(8,128)(2,1)} async-done(((bf16[192,512]{1,0:T(8,128)(2,1)}), bf16[192,4096]{1,0:T(8,128)(2,1)}) %all-gather.7.cloned.1.call-update) | async-done | bytes 1572880 | tf_op jit(solution)/shard_map/all_gather | solution.py:77
  45.7 86.4 %all-gather.9.cloned.1.call-done = bf16[512,4096]{1,0:T(8,128)(2,1)} async-done(((bf16[8,4096]{1,0:T(8,128)(2,1)}), bf16[512,4096]{1,0:T(8,128)(2,1)}) %all-gather.9.cloned.1.call-update) | async-done | bytes 4194320 | tf_op jit(solution)/shard_map/all_gather | solution.py:69
  132.1 5.0 %fusion.39 = (f32[192,512]{1,0:T(8,128)S(1)}, f32[192,512]{1,0:T(8,128)S(1)}, f32[192,512]{1,0:T(8,128)S(1)}, f32[192,512]{1,0:T(8,128)}) fusion(f32[512]{0:T(512)S(1)} %broadcast_multiply_fusion, bf16[192,512]{1,0:T(8,128)(2,1)} %param.17, bf16[192,512]{1,0:T(8,128)(2,1)} %param.16, bf16[192,4096]{1,0:T(8,128)(2,1)} %all-gather.7.cloned.1.call-done, ...), kind=kOutput, calls=%fused_computation.84 | convolution fusion | flops 806486016 | bytes 7735296 | tf_op jit(solution)/shard_map/dot_general | solution.py:78
  149.6 0.7 pad_maximum_fusion.9
  150.4 0.7 pad_maximum_fusion.10
  151.9 0.7 pad_maximum_fusion.6
  152.8 0.9 pad.183
  153.7 0.7 add.391
  154.5 0.7 pad_maximum_fusion.1
  155.3 1.0 pad.185
  157.0 0.7 mul.419
  158.3 0.7 fusion.54
  159.0 0.7 pad_maximum_fusion.23
  159.7 0.7 add_multiply_fusion.17
  160.4 0.7 pad_maximum_fusion.19
  161.5 0.7 add.406
  162.4 0.7 pad_maximum_fusion.2
  163.2 0.8 rev.9
  164.0 0.8 rev.8
  164.8 37.0 %all-gather.1 = f32[64,1,512]{2,1,0:T(1,128)S(1)} all-gather(f32[1,1,512]{2,1,0:T(1,128)} %add_bitcast_fusion.1), channel_id=1, replica_groups=mesh['seq'=64,'chan'=8] {'seq'}, dimensions={0}, use_global_device_ids=true | all-gather | bytes 133120 | tf_op jit(solution)/shard_map/all_gather | solution.py:19
  201.8 1.0 pad.212
  202.8 1.0 pad.213
  203.8 37.3 %all-gather = f32[64,1,512]{2,1,0:T(1,128)S(1)} all-gather(f32[1,1,512]{2,1,0:T(1,128)S(1)} %add_bitcast_fusion.2), channel_id=1, replica_groups=mesh['seq'=64,'chan'=8] {'seq'}, dimensions={0}, use_global_device_ids=true | all-gather | bytes 133120 | tf_op jit(solution)/shard_map/all_gather | solution.py:19
  241.1 3.7 while.26
  246.1 0.8 slice_add_fusion
  246.9 2.0 multiply_convert_fusion
  248.9 1.1 fusion.30
  250.0 0.7 slice.607
  250.7 0.7 slice.608
  251.5 1.1 multiply_add_fusion.3
  252.6 0.9 multiply_add_fusion.5
  253.6 0.8 multiply_add_fusion.7
  254.4 0.8 multiply_add_fusion.9
  255.2 0.7 multiply_add_fusion.11
  260.8 0.7 slice.636
  262.9 0.7 multiply_add_fusion.13
  263.6 0.8 slice_add_fusion.1
  264.4 0.7 fusion.57
  265.1 0.7 pad_maximum_fusion.24
  265.8 0.7 fusion.46
  266.6 0.7 pad_maximum_fusion.20
  267.3 0.8 fusion.44
  268.1 0.7 pad_maximum_fusion.16
  268.8 0.8 fusion.42
  269.6 0.7 pad_maximum_fusion.12
  270.4 0.9 fusion.40
  271.4 0.7 pad_maximum_fusion.8
  272.4 34.1 %all-gather.2 = f32[64,1,512]{2,1,0:T(1,128)S(1)} all-gather(f32[1,1,512]{2,1,0:T(1,128)S(1)} %add_bitcast_fusion), channel_id=1, replica_groups=mesh['seq'=64,'chan'=8] {'seq'}, dimensions={0}, use_global_device_ids=true | all-gather | bytes 133120 | tf_op jit(solution)/shard_map/all_gather | solution.py:19
  306.6 2.0 fusion.23
  308.6 2.0 fusion.29
  310.6 1.3 collective-permute-start
  312.0 2.6 copy.16
  314.6 1.6 collective-permute-done
  316.2 2.7 fusion
  318.9 115.0 %reduce-scatter.2.cloned.1.call-done = bf16[512,192]{0,1:T(8,128)(2,1)} async-done(((bf16[4096,192]{0,1:T(8,128)(2,1)}), bf16[512,192]{0,1:T(8,128)(2,1)}) %reduce-scatter.2.cloned.1.call-update) | async-done | bytes 196624 | tf_op jit(solution)/shard_map/reduce_scatter | solution.py:128
  (408 shorter events, 25.2 us)
Async XLA Ops:
  7.2 38.5 %all-gather.7.cloned.1.call-start = ((), (), s32[]{:S(2)}) async-start(), calls=%async_computation.2 | async-start | bytes 1769472 | tf_op jit(solution)/shard_map/all_gather | solution.py:77
  7.9 124.2 %all-gather.9.cloned.1.call-start = ((), (), s32[]{:S(2)}) async-start(), calls=%async_computation.3 | async-start | bytes 4259840 | tf_op jit(solution)/shard_map/all_gather | solution.py:69
  9.4 13.7 %collective-permute-start.1 = (bf16[3,512]{1,0:T(4,128)(2,1)S(1)}, bf16[3,512]{1,0:T(4,128)(2,1)S(1)}, u32[]{:S(2)}, u32[]{:S(2)}) collective-permute-start(bf16[3,512]{1,0:T(4,128)(2,1)S(1)} %slice.601), channel_id=1, source_target_pairs={{0,8},{8,16},{16,24},{24,32},{32,40},{40,48},{48,56},{56,64},{64,7... | collective-permute-start | bytes 9224 | tf_op jit(solution)/shard_map/ppermute | solution.py:12
  13.4 12.3 %all-to-all-start = ((bf16[8,8,512]{2,0,1:T(8,128)(2,1)}), bf16[8,8,512]{2,0,1:T(8,128)(2,1)S(1)}, u32[]{:S(2)}, u32[]{:S(2)}) async-start(bf16[8,8,512]{2,0,1:T(8,128)(2,1)} %bitcast.62), calls=%async_computation | async-start | bytes 131072 | tf_op jit(solution)/shard_map/all_to_all | solution.py:67
  20.8 291.1 %all-gather.11.cloned.1.call-start = ((), (), s32[]{:S(2)}) async-start(), calls=%async_computation.4 | async-start | bytes 4259840 | tf_op jit(solution)/shard_map/all_gather | solution.py:70
  21.6 115.5 %copy-start.17 = (f32[512]{0:T(512)}, f32[512]{0:T(512)S(1)}, u32[]{:S(2)}) copy-start(f32[512]{0:T(512)S(1)} %broadcast_multiply_fusion) | copy-start | bytes 6148
  25.7 0.6 copy-start.12
  26.3 407.6 %reduce-scatter.2.cloned.1.call-start = ((), (), s32[]{:S(2)}) async-start(), calls=%async_computation.5 | async-start | bytes 1769472 | tf_op jit(solution)/shard_map/reduce_scatter | solution.py:128
  141.0 10.8 %copy-start.2 = (f32[96,512]{1,0:T(8,128)}, f32[96,512]{1,0:T(8,128)S(1)}, u32[]{:S(2)}) copy-start(f32[96,512]{1,0:T(8,128)S(1)} %mul.414) | copy-start | bytes 589828
  141.0 5.2 %copy-start.3 = (f32[48,512]{1,0:T(8,128)}, f32[48,512]{1,0:T(8,128)S(1)}, u32[]{:S(2)}) copy-start(f32[48,512]{1,0:T(8,128)S(1)} %slice.563) | copy-start | bytes 294916
  141.1 11.5 %copy-start.6 = (f32[48,512]{1,0:T(8,128)}, f32[48,512]{1,0:T(8,128)S(1)}, u32[]{:S(2)}) copy-start(f32[48,512]{1,0:T(8,128)S(1)} %mul.415) | copy-start | bytes 294916
  141.2 5.1 %copy-start.8 = (f32[24,512]{1,0:T(8,128)}, f32[24,512]{1,0:T(8,128)S(1)}, u32[]{:S(2)}) copy-start(f32[24,512]{1,0:T(8,128)S(1)} %slice.566) | copy-start | bytes 147460
  141.2 5.1 %copy-start.7 = (f32[24,512]{1,0:T(8,128)}, f32[24,512]{1,0:T(8,128)S(1)}, u32[]{:S(2)}) copy-start(f32[24,512]{1,0:T(8,128)S(1)} %mul.416) | copy-start | bytes 147460
  141.2 5.3 %copy-start.11 = (f32[12,512]{1,0:T(8,128)}, f32[12,512]{1,0:T(8,128)S(1)}, u32[]{:S(2)}) copy-start(f32[12,512]{1,0:T(8,128)S(1)} %slice.569) | copy-start | bytes 73732
  141.3 9.8 %copy-start.15 = (f32[6,512]{1,0:T(8,128)}, f32[6,512]{1,0:T(8,128)S(1)}, u32[]{:S(2)}) copy-start(f32[6,512]{1,0:T(8,128)S(1)} %slice.572) | copy-start | bytes 36868
  146.3 15.1 %copy-start.4 = (f32[47,512]{1,0:T(8,128)}, f32[47,512]{1,0:T(8,128)S(1)}, u32[]{:S(2)}) copy-start(f32[47,512]{1,0:T(8,128)S(1)} %slice.588) | copy-start | bytes 288772
  148.8 3.9 copy-start.18
  151.8 9.3 %copy-start.10 = (f32[11,512]{1,0:T(8,128)S(1)}, f32[11,512]{1,0:T(8,128)}, u32[]{:S(2)}) copy-start(f32[11,512]{1,0:T(8,128)} %slice.584) | copy-start | bytes 67588
  151.8 9.4 %slice-start.2 = ((f32[24,512]{1,0:T(8,128)}), f32[1,512]{1,0:T(1,128)S(1)}, s32[]{:S(2)}) async-start(f32[24,512]{1,0:T(8,128)} %copy-done.7), calls=%async_computation.8 | async-start | bytes 4096 | tf_op jit(solution)/shard_map/slice | solution.py:94
  151.8 9.4 %copy-start.9 = (f32[23,512]{1,0:T(8,128)S(1)}, f32[23,512]{1,0:T(8,128)}, u32[]{:S(2)}) copy-start(f32[23,512]{1,0:T(8,128)} %slice.586) | copy-start | bytes 141316
  152.7 8.6 %slice-start.1 = ((f32[48,512]{1,0:T(8,128)}), f32[1,512]{1,0:T(1,128)S(1)}, s32[]{:S(2)}) async-start(f32[48,512]{1,0:T(8,128)} %copy-done.6), calls=%async_computation.7 | async-start | bytes 4096 | tf_op jit(solution)/shard_map/slice | solution.py:94
  152.7 8.8 %slice-start = ((f32[96,512]{1,0:T(8,128)}), f32[1,512]{1,0:T(1,128)S(1)}, s32[]{:S(2)}) async-start(f32[96,512]{1,0:T(8,128)} %copy-done.2), calls=%async_computation.6 | async-start | bytes 4096 | tf_op jit(solution)/shard_map/slice | solution.py:94
  154.5 7.9 %copy-start.20 = (f32[1,512]{1,0:T(1,128)S(1)}, f32[1,512]{1,0:T(1,128)}, u32[]{:S(2)}) copy-start(f32[1,512]{1,0:T(1,128)} %get-tuple-element.174) | copy-start | bytes 6148
  154.5 7.9 %copy-start.21 = (f32[1,512]{1,0:T(1,128)S(1)}, f32[1,512]{1,0:T(1,128)}, u32[]{:S(2)}) copy-start(f32[1,512]{1,0:T(1,128)} %get-tuple-element.175) | copy-start | bytes 6148
  157.7 0.6 copy-start.16
  162.3 84.5 %copy-start = (bf16[192,512]{1,0:T(8,128)(2,1)S(1)}, bf16[192,512]{1,0:T(8,128)(2,1)}, u32[]{:S(2)}) copy-start(bf16[192,512]{1,0:T(8,128)(2,1)} %param.17) | copy-start | bytes 589828
  162.3 84.5 %copy-start.1 = (bf16[192,512]{1,0:T(8,128)(2,1)S(1)}, bf16[192,512]{1,0:T(8,128)(2,1)}, u32[]{:S(2)}) copy-start(bf16[192,512]{1,0:T(8,128)(2,1)} %param.18) | copy-start | bytes 589828
  244.8 0.7 copy-start.13
  245.5 0.6 copy-start.14
  248.9 21.5 %copy-start.5 = (f32[47,512]{1,0:T(8,128)S(1)}, f32[47,512]{1,0:T(8,128)}, u32[]{:S(2)}) copy-start(f32[47,512]{1,0:T(8,128)} %copy-done.4) | copy-start | bytes 288772
  267.2 5.0 %copy-start.19 = (f32[1,512]{1,0:T(1,128)S(1)}, f32[1,512]{1,0:T(1,128)}, u32[]{:S(2)}) copy-start(f32[1,512]{1,0:T(1,128)} %slice.719) | copy-start | bytes 6148
  310.6 5.6 %collective-permute-start = (f32[3,512]{1,0:T(4,128)S(1)}, f32[3,512]{1,0:T(4,128)S(1)}, u32[]{:S(2)}, u32[]{:S(2)}) collective-permute-start(f32[3,512]{1,0:T(4,128)S(1)} %slice.710), channel_id=1, source_target_pairs={{8,0},{16,8},{24,16},{32,24},{40,32},{48,40},{56,48},{64,56},{72,6... | collective-permute-start | bytes 18440 | tf_op jit(solution)/shard_map/ppermute | solution.py:12
  311.9 4.2 copy-start.22
  311.9 4.2 copy-start.23
  311.9 4.2 copy-start.24
  312.0 4.2 copy-start.25
Sparse Core Ops, SparseCore 0:
  10.1 35.5 all-gather.6
  48.8 83.2 all-gather.8
  135.1 83.9 all-gather.10
  319.0 114.8 reduce-scatter.1
where the time goes:
time: 448 us; the launch traced here: 440 us
  waiting for transfers between devices  225 us (50%)
  blocking collectives  108 us (24%)
  other arithmetic  34.4 us (8%)
  local copies, waits for them, and re-layouts  34.3 us (8%)
  between operations  15.3 us (3%)
  starting transfers between devices  12.8 us (3%)
  matrix products  7.73 us (2%)
    reduce_scatter x1, waiting for transfers between devices, shards(): lax.psum_scatter(term.astype(jnp.float32).astype(jnp.bfloat16), 'chan', s...  115 us
    all_gather x3, blocking collectives, prefix(): gathered = jax.tree.map(lambda a: lax.all_gather(a, axis), part)  108 us
    all_gather x1, waiting for transfers between devices, shards(): lax.all_gather(w_out, 'seq', axis=0, tiled=True)  86.4 us
    all_gather x1, waiting for transfers between devices, shards(): full_out = lax.all_gather(d_out, 'chan', axis=1, tiled=True)  19.4 us
    slice x48, local copies, waits for them, and re-layouts, shards(): lax.associative_scan(combine_affine, (decay, beta * gated_in), axis=0)  13.9 us
    add x76, other arithmetic, combine_affine(): return (earlier[0] * later[0], later[0] * earlier[1] + later[1])  10.6 us
  transfers between devices with their start and end apart: 7, of which 5 were waited for; matrix products, arithmetic and copies ran while one was open for 16% of the time, Pallas kernels for 0%

commit v1 on v0

v1 whole, which is shorter than its diff:
```python
import jax
import jax.numpy as jnp
from jax import lax
from jax.experimental import pallas as pl
from jax.experimental.pallas import tpu as pltpu
from jax.sharding import Mesh, PartitionSpec as P

LEVELS = 16
SEQ = ("z", "y")
CHAN = ("x", "k")
SUB = 8
F32 = jnp.float32
BF16 = jnp.bfloat16
VMEM_LIMIT = 48 * 1024 * 1024


def decay_table(length):
    levels = jnp.arange(LEVELS).astype(F32)
    half = LEVELS // 2
    slow_rates = 0.25 * jnp.power(16.0, levels / (half - 1.0)) / (8.0 * length)
    fast_rates = jnp.power(4.0, (levels - half) / (half - 1.0)) / 640.0
    return -jnp.where(levels < half, slow_rates, fast_rates)


def gelu_parts(gate):
    normal_cdf = 0.5 * (1.0 + lax.erf(gate * 0.7071067811865476))
    density = jnp.exp(-0.5 * gate * gate) * 0.3989422804014327
    return (gate * normal_cdf, normal_cdf + gate * density)


def sigmoid(value):
    return 1.0 / (1.0 + jnp.exp(-value))


def expm1(value):
    series = jnp.ones_like(value)
    for term in range(9, 1, -1):
        series = 1.0 + value * (1.0 / term) * series
    return jnp.where(jnp.abs(value) < 0.5, value * series, jnp.exp(value) - 1.0)


def local_scan(a, b, reverse, a_out, b_out):
    rows, width = a.shape
    tiles = rows // SUB
    a = a.reshape(tiles, SUB, width)
    b = b.reshape(tiles, SUB, width)
    row = lax.broadcasted_iota(jnp.int32, a.shape, 1)
    for step in (1, 2, 4):
        shift = SUB - step if reverse else step
        inside = row < SUB - step if reverse else row >= step
        a_from = jnp.where(inside, pltpu.roll(a, shift, 1), 1.0)
        b_from = jnp.where(inside, pltpu.roll(b, shift, 1), 0.0)
        b = b + a * b_from
        a = a * a_from
    prod = jnp.ones((1, width), F32)
    state = jnp.zeros((1, width), F32)
    edge = 0 if reverse else SUB - 1
    for tile in reversed(range(tiles)) if reverse else range(tiles):
        here_b = b[tile] + a[tile] * state
        here_a = a[tile] * prod
        b_out[pl.ds(tile * SUB, SUB), :] = here_b
        a_out[pl.ds(tile * SUB, SUB), :] = here_a
        state = here_b[edge : edge + 1]
        prod = here_a[edge : edge + 1]
    return prod, state


def shift_up(value, last):
    rows = value.shape[0]
    row = lax.broadcasted_iota(jnp.int32, value.shape, 0)
    return jnp.where(row == rows - 1, last, pltpu.roll(value, rows - 1, 0))


def before_kernel(
    x_ref, prev_ref, rec_ref, inw_ref, cw_ref, cb_ref, ld_ref,
    decay_ref, beta_ref, conv_ref, cum_ref, local_ref, post_ref, ends_ref, front_ref,
    padded, scan_a, scan_b,
):
    rows = x_ref.shape[0]
    lead = prev_ref.shape[0]
    padded[pl.ds(0, lead), :] = prev_ref[...].astype(F32)
    padded[pl.ds(lead, rows), :] = x_ref[...].astype(F32)
    conv = jnp.zeros(x_ref.shape, F32)
    for lag in range(4):
        conv = conv + cw_ref[lag : lag + 1, :] * padded[pl.ds(lead - lag, rows), :]
    conv = cb_ref[...] + conv
    recur = sigmoid(rec_ref[...].astype(F32))
    inward = sigmoid(inw_ref[...].astype(F32))
    log_step = 8.0 * recur * ld_ref[...]
    decay = jnp.exp(log_step)
    beta = jnp.sqrt(-expm1(2.0 * log_step))
    decay_ref[...] = decay
    beta_ref[...] = beta
    conv_ref[...] = conv
    prod, state = local_scan(decay, beta * (inward * conv), False, cum_ref, local_ref)
    ends_ref[...] = jnp.concatenate([prod, state], axis=0)
    local_scan(decay, jnp.zeros_like(decay), True, scan_a, scan_b)
    post = shift_up(scan_a[...], 1.0)
    post_ref[...] = post
    front_ref[...] = (post * beta * inward)[:SUB]


def before(x_branch, prev, recurrence_gate, input_gate, conv_weight, conv_bias, log_decay):
    rows, width = x_branch.shape
    full = jax.ShapeDtypeStruct((rows, width), F32)
    return pl.pallas_call(
        before_kernel,
        out_shape=(full,) * 6
        + (jax.ShapeDtypeStruct((2, width), F32), jax.ShapeDtypeStruct((SUB, width), F32)),
        scratch_shapes=[
            pltpu.VMEM((rows + prev.shape[0], width), F32),
            pltpu.VMEM((rows, width), F32),
            pltpu.VMEM((rows, width), F32),
        ],
        compiler_params=pltpu.CompilerParams(vmem_limit_bytes=VMEM_LIMIT),
    )(x_branch, prev, recurrence_gate, input_gate, conv_weight, conv_bias, log_decay)


def adjoint_kernel(
    core_ref, own_ref, other_ref, w_ref, gate_ref, decay_ref, beta_ref, inw_ref, ends_ref,
    dlru_ref, adj_ref, front_ref, carry_ref,
    acc, scan_a, scan_b,
):
    step = pl.program_id(0)
    half = w_ref.shape[1] // 2

    @pl.when(step == 0)
    def _():
        acc[...] = jnp.zeros_like(acc)

    def add(first, second):
        dims = (((1,), (1,)), ((), ()))
        acc[...] += lax.dot_general(
            first[0], w_ref[:, :half], dims, preferred_element_type=F32
        ) + lax.dot_general(second[0], w_ref[:, half:], dims, preferred_element_type=F32)

    @pl.when(core_ref[0] == 0)
    def _():
        add(own_ref[...], other_ref[...])

    @pl.when(core_ref[0] != 0)
    def _():
        add(other_ref[...], own_ref[...])

    @pl.when(step == pl.num_programs(0) - 1)
    def _():
        d_lru = acc[...]
        dlru_ref[...] = d_lru
        d_direct = d_lru * gelu_parts(gate_ref[...].astype(F32))[0]
        decay = decay_ref[...]
        _, first = local_scan(decay, decay * d_direct, True, scan_a, scan_b)
        adj = d_direct + shift_up(scan_b[...], 0.0)
        adj_ref[...] = adj
        inward = sigmoid(inw_ref[:16, :].astype(F32))[:SUB]
        front_ref[...] = adj[:SUB] * beta_ref[:SUB, :] * inward
        mine = jnp.concatenate([ends_ref[...], first], axis=0)
        carry_ref[...] = jnp.broadcast_to(mine[None], carry_ref.shape)


def adjoint(core, own, other, weights, gate, decay, beta, input_gate, ends, seq_count):
    rows, width = gate.shape
    steps = own.shape[0]
    full = jax.ShapeDtypeStruct((rows, width), F32)
    whole = lambda shape: pl.BlockSpec(shape, lambda i: (0,) * len(shape))
    return pl.pallas_call(
        adjoint_kernel,
        grid=(steps,),
        in_specs=[
            pl.BlockSpec(memory_space=pltpu.SMEM),
            pl.BlockSpec((1, rows, width), lambda i: (i, 0, 0)),
            pl.BlockSpec((1, rows, width), lambda i: (i, 0, 0)),
            pl.BlockSpec((width, 2 * width), lambda i: (0, i)),
            whole((rows, width)),
            whole((rows, width)),
            whole((rows, width)),
            whole((rows, width)),
            whole((2, width)),
        ],
        out_specs=[
            whole((rows, width)),
            whole((rows, width)),
            whole((SUB, width)),
            whole((seq_count, 3, width)),
        ],
        out_shape=(
            full,
            full,
            jax.ShapeDtypeStruct((SUB, width), F32),
            jax.ShapeDtypeStruct((seq_count, 3, width), F32),
        ),
        scratch_shapes=[pltpu.VMEM((rows, width), F32)] * 3,
        compiler_params=pltpu.CompilerParams(vmem_limit_bytes=VMEM_LIMIT),
    )(core, own, other, weights, gate, decay, beta, input_gate, ends)


def branch_kernel(
    place_ref, carry_ref, adj_ref, post_ref, beta_ref, inw_ref, cw_ref, front_a_ref, front_b_ref,
    branch_ref, adjoint_ref, state_ref,
    padded,
):
    rows, width = adj_ref.shape
    place = place_ref[0]
    count = carry_ref.shape[0]
    state = jnp.zeros((1, width), F32)
    beyond = jnp.zeros((1, width), F32)
    kappa = jnp.zeros((1, width), F32)
    for i in range(count - 1):
        state = jnp.where(i < place, carry_ref[i, 1:2] + carry_ref[i, 0:1] * state, state)
    for i in reversed(range(1, count)):
        here = carry_ref[i, 2:3] + carry_ref[i, 0:1] * kappa
        beyond = jnp.where(i == place + 1, kappa, beyond)
        kappa = jnp.where(i > place, here, kappa)
    adj = adj_ref[...] + post_ref[...] * kappa
    d_conv = adj * beta_ref[...] * sigmoid(inw_ref[...].astype(F32))
    padded[pl.ds(0, rows), :] = d_conv
    padded[pl.ds(rows, SUB), :] = front_a_ref[...] + front_b_ref[...] * beyond
    total = jnp.zeros((rows, width), F32)
    for lag in range(4):
        total = total + cw_ref[lag : lag + 1, :] * padded[pl.ds(lag, rows), :]
    branch_ref[...] = total.astype(BF16)
    adjoint_ref[...] = adj
    state_ref[...] = state


def branch(place, carry, adj, post, beta, input_gate, conv_weight, front_a, front_b):
    rows, width = adj.shape
    vmem = pl.BlockSpec(memory_space=pltpu.VMEM)
    return pl.pallas_call(
        branch_kernel,
        in_specs=[pl.BlockSpec(memory_space=pltpu.SMEM)] + [vmem] * 8,
        out_shape=(
            jax.ShapeDtypeStruct((rows, width), BF16),
            jax.ShapeDtypeStruct((rows, width), F32),
            jax.ShapeDtypeStruct((1, width), F32),
        ),
        scratch_shapes=[pltpu.VMEM((rows + SUB, width), F32)],
        compiler_params=pltpu.CompilerParams(vmem_limit_bytes=VMEM_LIMIT),
    )(place, carry, adj, post, beta, input_gate, conv_weight, front_a, front_b)


def gates_kernel(
    dlru_ref, adj_ref, state_ref, cum_ref, local_ref, decay_ref, beta_ref, conv_ref,
    gate_ref, rec_ref, inw_ref, ld_ref,
    dgate_ref, drec_ref, dinw_ref,
):
    carried = state_ref[...]
    states = local_ref[...] + cum_ref[...] * carried
    slope = gelu_parts(gate_ref[...].astype(F32))[1]
    dgate_ref[...] = (dlru_ref[...] * states * slope).astype(BF16)
    row = lax.broadcasted_iota(jnp.int32, states.shape, 0)
    states_prev = jnp.where(row == 0, carried, pltpu.roll(states, 1, 0))
    recur = sigmoid(rec_ref[...].astype(F32))
    inward = sigmoid(inw_ref[...].astype(F32))
    decay = decay_ref[...]
    beta = beta_ref[...]
    conv = conv_ref[...]
    adj = adj_ref[...]
    d_step = adj * (decay * states_prev - inward * conv * decay * decay / beta)
    drec_ref[...] = (d_step * 8.0 * ld_ref[...] * recur * (1.0 - recur)).astype(BF16)
    dinw_ref[...] = (adj * beta * conv * inward * (1.0 - inward)).astype(BF16)


def gates(*arrays):
    out = jax.ShapeDtypeStruct(arrays[0].shape, BF16)
    return pl.pallas_call(
        gates_kernel,
        out_shape=(out,) * 3,
        compiler_params=pltpu.CompilerParams(vmem_limit_bytes=VMEM_LIMIT),
    )(*arrays)


def input_kernel(rows_ref, w_ref, out_ref, acc):
    step = pl.program_id(0)
    half = w_ref.shape[1] // 2

    @pl.when(step == 0)
    def _():
        acc[...] = jnp.zeros_like(acc)

    dims = (((1,), (1,)), ((), ()))
    acc[...] += lax.dot_general(
        rows_ref[0], w_ref[:, :half], dims, preferred_element_type=F32
    ) + lax.dot_general(rows_ref[1], w_ref[:, half:], dims, preferred_element_type=F32)

    @pl.when(step == pl.num_programs(0) - 1)
    def _():
        out_ref[...] = acc[...].astype(BF16)


def input_grad(gathered, weights):
    count, rows, width = gathered.shape
    steps = count // 2
    return pl.pallas_call(
        input_kernel,
        grid=(steps,),
        in_specs=[
            pl.BlockSpec((2, rows, width), lambda i: (i, 0, 0)),
            pl.BlockSpec((width, 2 * width), lambda i: (0, steps + i)),
        ],
        out_specs=pl.BlockSpec((rows, width), lambda i: (0, 0)),
        out_shape=jax.ShapeDtypeStruct((rows, width), BF16),
        scratch_shapes=[pltpu.VMEM((rows, width), F32)],
        compiler_params=pltpu.CompilerParams(vmem_limit_bytes=VMEM_LIMIT),
    )(gathered, weights)


def shards(
    d_out,
    x_branch,
    gate_branch,
    recurrence_gate,
    input_gate,
    conv_weight,
    conv_bias,
    decay_level,
    w_in,
    w_out,
):
    tok_rows, chan_width = x_branch.shape
    seq_count = lax.axis_size(SEQ)
    place = lax.axis_index(SEQ).astype(jnp.int32).reshape(1)
    core = lax.axis_index("k").astype(jnp.int32).reshape(1)
    forward = [(i, i + 1) for i in range(seq_count - 1)]
    backward = [(i + 1, i) for i in range(seq_count - 1)]
    weights = lax.all_gather(jnp.concatenate([w_out, w_in], axis=1), SEQ, axis=0, tiled=True)
    prev = lax.ppermute(x_branch[tok_rows - 16 :], SEQ, forward)
    own = lax.all_gather(d_out, "x")
    other = lax.ppermute(own, "k", [(0, 1), (1, 0)])
    log_table = decay_table(tok_rows * seq_count)
    onehot = decay_level[:, None] == jnp.arange(LEVELS)[None, :]
    log_decay = jnp.sum(jnp.where(onehot, log_table[None, :], 0.0), axis=1)[None, :]
    decay, beta, conv_out, cum_decay, local_states, post, ends, front_b = before(
        x_branch, prev, recurrence_gate, input_gate, conv_weight, conv_bias[None, :], log_decay
    )
    next_b = lax.ppermute(front_b, SEQ, backward)
    d_lru, adj_local, front_a, carry = adjoint(
        core, own, other, weights, gate_branch, decay, beta, input_gate, ends, seq_count
    )
    next_a = lax.ppermute(front_a, SEQ, backward)
    carries = lax.all_to_all(carry, SEQ, 0, 0)
    d_branch, adj, state_in = branch(
        place, carries, adj_local, post, beta, input_gate, conv_weight, next_a, next_b
    )
    gathered = lax.all_gather(d_branch, CHAN)
    d_gate, d_recurrence_gate, d_input_gate = gates(
        d_lru, adj, state_in, cum_decay, local_states, decay, beta, conv_out,
        gate_branch, recurrence_gate, input_gate, log_decay,
    )
    d_input = input_grad(gathered, weights)
    return (d_input, d_gate, d_recurrence_gate, d_input_gate)


def solution(mesh):
    fine = Mesh(mesh.devices.reshape(8, 8, 4, 2), SEQ + CHAN)
    tokens = P(SEQ, CHAN)
    rows = P(CHAN + SEQ, None)
    in_specs = (tokens,) * 5 + (P(None, CHAN), P(CHAN), P(CHAN), rows, rows)
    return jax.shard_map(
        shards, mesh=fine, in_specs=in_specs, out_specs=(tokens,) * 4, check_vma=False
    )
```

time: 448 us -> 196 us (0.44); the launches traced: 440 us -> 195 us
  waiting for transfers between devices: 225 us -> 110 us
  blocking collectives: 108 us -> 11.8 us
  other arithmetic: 34.4 us -> 2.46 us
  local copies, waits for them, and re-layouts: 34.3 us -> 16.9 us
  Pallas kernels: 0 us -> 15.2 us
  starting transfers between devices: 12.8 us -> 24.2 us
  matrix products: 7.73 us -> 0 us
    reduce_scatter x1 -> x0, waiting for transfers between devices: 115 us -> none  [shards(): lax.psum_scatter(term.astype(jnp.float32).astype(jnp.bfloat16), 'chan', s...]
    all_gather x3 -> x1, blocking collectives: 108 us -> 11.8 us  [shards(): own = lax.all_gather(d_out, 'x')]
    slice x105 -> x1, local copies, waits for them, and re-layouts: 22 us -> 0.72 us  [shards(): prev = lax.ppermute(x_branch[tok_rows - 16:], SEQ, forward)]
    pallas_call x0 -> x5, Pallas kernels: none -> 15.2 us  [the longest x1 5.46 us: adjoint(): pl.pallas_call(adjoint_kernel, grid=(steps,), in_specs=[pl.BlockSpec(memo...]
    add x103 -> x0, other arithmetic: 13.8 us -> none  [the longest x76 10.6 us: combine_affine(): return (earlier[0] * later[0], later[0] * earlier[1] + later[1])]
    unnamed x55 -> x44, local copies, waits for them, and re-layouts: 2.57 us -> 16.2 us
    all_gather x3 -> x2, waiting for transfers between devices: 106 us -> 96.1 us  [the longest x1 73.7 us: shards(): lax.all_gather(jnp.concatenate([w_out, w_in], axis=1), SEQ, axis=0, tiled...]
    ppermute x2 -> x4, starting transfers between devices: 5.3 us -> 14.4 us  [the longest x1 10.5 us: shards(): other = lax.ppermute(own, 'k', [(0, 1), (1, 0)])]
  transfers between devices with their start and end apart: 7 -> 7, of which waited for: 5 -> 6; matrix products, arithmetic and copies ran while one was open for 16% -> 1% of each run, Pallas kernels for 0% -> 2%
where the time goes in v1:
time: 196 us; the launch traced here: 195 us
  waiting for transfers between devices  110 us (56%)
  starting transfers between devices  24.2 us (12%)
  local copies, waits for them, and re-layouts  16.9 us (9%)
  Pallas kernels  15.2 us (8%)
  between operations  14.2 us (7%)
  blocking collectives  11.8 us (6%)
  other arithmetic  2.46 us (1%)
    all_gather x1, waiting for transfers between devices, shards(): lax.all_gather(jnp.concatenate([w_out, w_in], axis=1), SEQ, axis=0, tiled...  73.7 us
    all_gather x1, waiting for transfers between devices, shards(): gathered = lax.all_gather(d_branch, CHAN)  22.4 us
    unnamed x44, local copies, waits for them, and re-layouts  16.2 us
    all_gather x1, blocking collectives, shards(): own = lax.all_gather(d_out, 'x')  11.8 us
    ppermute x1, starting transfers between devices, shards(): other = lax.ppermute(own, 'k', [(0, 1), (1, 0)])  10.5 us
    all_to_all x1, starting transfers between devices, shards(): carries = lax.all_to_all(carry, SEQ, 0, 0)  9.79 us
    ppermute x1, waiting for transfers between devices, shards(): next_b = lax.ppermute(front_b, SEQ, backward)  8.7 us
    pallas_call x1, Pallas kernels, adjoint(): pl.pallas_call(adjoint_kernel, grid=(steps,), in_specs=[pl.BlockSpec(memo...  5.46 us
  transfers between devices with their start and end apart: 7, of which 6 were waited for; matrix products, arithmetic and copies ran while one was open for 1% of the time, Pallas kernels for 2%

profile of v1, /device:TPU:1, one launch (start us, length us, event | category | flops | bytes accessed | tf_op | source)
XLA Modules:
  0.0 195.3 jit_solution(17202391509862358978)
XLA Ops:
  7.2 0.0 copy-start.2
  7.2 0.0 copy-start.20
  7.2 0.0 copy-start.5
  7.2 0.0 copy-start.7
  7.2 0.0 all-gather.5.cloned.1.call-start
  7.3 1.7 pad_maximum_fusion
  8.9 0.0 all-gather.5.cloned.1.call-update
  9.0 11.8 %all-gather = bf16[768,512]{1,0:T(8,128)(2,1)S(1)} all-gather(bf16[192,512]{1,0:T(8,128)(2,1)} %param.10), channel_id=2, replica_groups=mesh['z'=8,'y'=8,'x'=4,'k'=2] {'x'}, dimensions={0}, use_global_device_ids=true | all-gather | bytes 983040 | tf_op jit(solution)/shard_map/all_gather | solution.py:327
  20.8 10.5 %collective-permute-start = (bf16[4,192,512]{2,1,0:T(8,128)(2,1)S(1)}, bf16[4,192,512]{2,1,0:T(8,128)(2,1)S(1)}, u32[]{:S(2)}, u32[]{:S(2)}) collective-permute-start(bf16[4,192,512]{2,1,0:T(8,128)(2,1)S(1)} %bitcast.6), channel_id=1, source_target_pairs={{0,1},{1,0},{2,3},{3,2},{4,5},{5,4},{6,7},{7,6},{8,9},{9,8},{10,11... | collective-permute-start | bytes 2359304 | tf_op jit(solution)/shard_map/ppermute | solution.py:328
  31.3 0.7 slice.3
  32.0 1.3 collective-permute-start.1
  33.3 0.8 select_reduce_fusion
  34.1 0.1 collective-permute-done.1.prev_ref
  34.1 0.0 copy-start
  34.1 0.9 copy-done
  35.1 0.0 copy-start.4
  35.1 0.9 copy-done.4
  36.0 0.0 copy-start.18
  36.0 0.9 copy-done.18
  36.9 0.0 copy-start.19
  36.9 0.7 copy-done.19
  37.6 0.0 copy-start.21
  37.6 0.7 copy-done.21
  38.3 2.3 %shard_map.129 = (f32[192,512]{1,0:T(8,128)S(1)}, f32[192,512]{1,0:T(8,128)S(1)}, f32[192,512]{1,0:T(8,128)S(1)}, f32[192,512]{1,0:T(8,128)S(1)}, f32[192,512]{1...) custom-call(bf16[192,512]{1,0:T(8,128)(2,1)S(1)} %copy-done.18, ...), custom_call_target="tpu_custom_call" | custom-call | tf_op jit(solution)/shard_map/pallas_call | solution.py:106
  40.6 0.0 copy-start.8
  40.6 0.7 copy-done.8
  41.4 0.0 copy-start.10
  41.4 0.7 copy-done.10
  42.1 0.0 copy-start.14
  42.1 0.7 copy-done.14
  42.9 0.0 collective-permute-done.other_ref
  42.9 73.7 %all-gather.5.cloned.1.call-done.w_ref = bf16[512,8192]{1,0:T(8,128)(2,1)} async-done(((bf16[8,8192]{1,0:T(8,128)(2,1)}), bf16[512,8192]{1,0:T(8,128)(2,1)}) %all-gather.5.cloned.1.call-update) | async-done | bytes 8388624 | tf_op jit(solution)/shard_map/all_gather | solution.py:325
  116.5 0.0 copy-start.1
  116.6 0.9 copy-done.1
  117.5 0.0 copy-start.6
  117.5 0.9 copy-done.6
  118.4 5.5 %shard_map.130 = (f32[192,512]{1,0:T(8,128)S(1)}, f32[192,512]{1,0:T(8,128)S(1)}, f32[8,512]{1,0:T(8,128)S(1)}, f32[64,3,512]{2,1,0:T(4,128)}) custom-call(s32[1]{0:T(128)} %bitcast.1.core_ref, bf16[4,192,512]{2,1,0:T(8,128)(2,1)S(1)} %bitcast.7, bf16[4,192,512]{2,1,0:T(8,128)(2,1)S(1)} %collective-permute-done.other_ref, ...), custom_call_target="tpu_custom_call" | custom-call | tf_op jit(solution)/shard_map/pallas_call | solution.py:165
  123.9 0.0 copy-start.12
  123.9 0.7 copy-done.12
  124.6 0.0 copy-start.16
  124.6 0.8 copy-done.16
  125.4 9.8 %all-to-all-start = ((f32[64,3,512]{2,1,0:T(4,128)}), f32[64,3,512]{2,1,0:T(4,128)S(1)}, u32[]{:S(2)}, u32[]{:S(2)}) async-start(f32[64,3,512]{2,1,0:T(4,128)} %get-tuple-element.25), calls=%async_computation | async-start | bytes 1048576 | tf_op jit(solution)/shard_map/all_to_all | solution.py:340
  135.2 0.0 all-gather.7.cloned.1.call-start
  135.2 1.3 collective-permute-start.3
  136.5 1.3 collective-permute-start.2
  137.8 8.7 %collective-permute-done.3.front_b_ref = f32[8,512]{1,0:T(8,128)S(1)} collective-permute-done((f32[8,512]{1,0:T(8,128)S(1)}, f32[8,512]{1,0:T(8,128)S(1)}, u32[]{:S(2)}, u32[]{:S(2)}) %collective-permute-start.3) | collective-permute-done | bytes 16416 | tf_op jit(solution)/shard_map/ppermute | solution.py:335
  146.5 0.7 collective-permute-done.2.front_a_ref
  147.2 4.9 %all-to-all-done.carry_ref = f32[64,3,512]{2,1,0:T(4,128)S(1)} async-done(((f32[64,3,512]{2,1,0:T(4,128)}), f32[64,3,512]{2,1,0:T(4,128)S(1)}, u32[]{:S(2)}, u32[]{:S(2)}) %all-to-all-start) | async-done | bytes 393248 | tf_op jit(solution)/shard_map/all_to_all | solution.py:340
  152.1 0.0 copy-done.2
  152.1 0.0 copy-done.20
  152.1 1.0 copy-done.15
  153.1 1.0 copy-done.17
  154.1 1.4 shard_map.131
  155.4 0.0 all-gather.7.cloned.1.call-update
  155.5 0.0 copy-done.5
  155.5 0.0 copy-done.7
  155.5 0.0 copy-start.9
  155.5 1.0 copy-done.9
  156.5 1.0 copy-done.11
  157.5 1.0 copy-done.13
  158.5 1.3 shard_map.133
  159.8 22.4 %all-gather.7.cloned.1.call-done = bf16[1536,512]{1,0:T(8,128)(2,1)} async-done(((bf16[192,512]{1,0:T(8,128)(2,1)}), bf16[1536,512]{1,0:T(8,128)(2,1)}) %all-gather.7.cloned.1.call-update) | async-done | bytes 1572880 | tf_op jit(solution)/shard_map/all_gather | solution.py:344
  182.2 1.4 copy-done.3
  183.7 4.8 %shard_map.132 = bf16[192,512]{1,0:T(8,128)(2,1)} custom-call(bf16[8,192,512]{2,1,0:T(8,128)(2,1)S(1)} %bitcast.8, bf16[512,8192]{1,0:T(8,128)(2,1)} %all-gather.5.cloned.1.call-done.w_ref), custom_call_target="tpu_custom_call" | custom-call | tf_op jit(solution)/shard_map/pallas_call | solution.py:293
  (6 shorter events, 0.0 us)
Async XLA Ops:
  7.2 144.9 %copy-start.2 = (bf16[192,512]{1,0:T(8,128)(2,1)S(1)}, bf16[192,512]{1,0:T(8,128)(2,1)}, u32[]{:S(2)}) copy-start(bf16[192,512]{1,0:T(8,128)(2,1)} %inw_ref.7) | copy-start | bytes 589828
  7.2 144.9 %copy-start.20 = (f32[4,512]{1,0:T(4,128)S(1)}, f32[4,512]{1,0:T(4,128)}, u32[]{:S(2)}) copy-start(f32[4,512]{1,0:T(4,128)} %cw_ref.3) | copy-start | bytes 24580
  7.2 148.3 %copy-start.5 = (bf16[192,512]{1,0:T(8,128)(2,1)S(1)}, bf16[192,512]{1,0:T(8,128)(2,1)}, u32[]{:S(2)}) copy-start(bf16[192,512]{1,0:T(8,128)(2,1)} %rec_ref.3) | copy-start | bytes 589828
  7.2 148.3 %copy-start.7 = (bf16[192,512]{1,0:T(8,128)(2,1)S(1)}, bf16[192,512]{1,0:T(8,128)(2,1)}, u32[]{:S(2)}) copy-start(bf16[192,512]{1,0:T(8,128)(2,1)} %gate_ref.3) | copy-start | bytes 589828
  7.2 109.3 %all-gather.5.cloned.1.call-start = ((), (), s32[]{:S(2)}) async-start(), calls=%async_computation.1 | async-start | bytes 8519680 | tf_op jit(solution)/shard_map/all_gather | solution.py:325
  20.8 22.1 %collective-permute-start = (bf16[4,192,512]{2,1,0:T(8,128)(2,1)S(1)}, bf16[4,192,512]{2,1,0:T(8,128)(2,1)S(1)}, u32[]{:S(2)}, u32[]{:S(2)}) collective-permute-start(bf16[4,192,512]{2,1,0:T(8,128)(2,1)S(1)} %bitcast.6), channel_id=1, source_target_pairs={{0,1},{1,0},{2,3},{3,2},{4,5},{5,4},{6,7},{7,6},{8,9},{9,8},{10,11... | collective-permute-start | bytes 2359304 | tf_op jit(solution)/shard_map/ppermute | solution.py:328
  32.0 2.1 %collective-permute-start.1 = (bf16[16,512]{1,0:T(8,128)(2,1)S(1)}, bf16[16,512]{1,0:T(8,128)(2,1)S(1)}, u32[]{:S(2)}, u32[]{:S(2)}) collective-permute-start(bf16[16,512]{1,0:T(8,128)(2,1)S(1)} %slice.3), channel_id=1, source_target_pairs={{0,8},{8,16},{16,24},{24,32},{32,40},{40,48},{48,56},{56,64},{64,7... | collective-permute-start | bytes 49160 | tf_op jit(solution)/shard_map/ppermute | solution.py:326
  34.1 0.9 copy-start
  35.1 0.9 copy-start.4
  36.0 0.9 copy-start.18
  36.9 0.7 copy-start.19
  37.6 0.7 copy-start.21
  40.6 0.8 copy-start.8
  41.4 0.8 copy-start.10
  42.1 0.7 copy-start.14
  116.5 0.9 copy-start.1
  117.5 0.9 copy-start.6
  123.9 0.7 copy-start.12
  124.6 0.8 copy-start.16
  125.4 26.7 %all-to-all-start = ((f32[64,3,512]{2,1,0:T(4,128)}), f32[64,3,512]{2,1,0:T(4,128)S(1)}, u32[]{:S(2)}, u32[]{:S(2)}) async-start(f32[64,3,512]{2,1,0:T(4,128)} %get-tuple-element.25), calls=%async_computation | async-start | bytes 1048576 | tf_op jit(solution)/shard_map/all_to_all | solution.py:340
  135.2 47.1 %all-gather.7.cloned.1.call-start = ((), (), s32[]{:S(2)}) async-start(), calls=%async_computation.2 | async-start | bytes 1769472 | tf_op jit(solution)/shard_map/all_gather | solution.py:344
  135.2 11.3 %collective-permute-start.3 = (f32[8,512]{1,0:T(8,128)S(1)}, f32[8,512]{1,0:T(8,128)S(1)}, u32[]{:S(2)}, u32[]{:S(2)}) collective-permute-start(f32[8,512]{1,0:T(8,128)S(1)} %get-tuple-element.29), channel_id=1, source_target_pairs={{8,0},{16,8},{24,16},{32,24},{40,32},{48,40},{56,48},{64,56},{72,6... | collective-permute-start | bytes 49160 | tf_op jit(solution)/shard_map/ppermute | solution.py:335
  136.5 10.7 %collective-permute-start.2 = (f32[8,512]{1,0:T(8,128)S(1)}, f32[8,512]{1,0:T(8,128)S(1)}, u32[]{:S(2)}, u32[]{:S(2)}) collective-permute-start(f32[8,512]{1,0:T(8,128)S(1)} %get-tuple-element.28), channel_id=1, source_target_pairs={{8,0},{16,8},{24,16},{32,24},{40,32},{48,40},{56,48},{64,56},{72,6... | collective-permute-start | bytes 49160 | tf_op jit(solution)/shard_map/ppermute | solution.py:339
  152.1 1.0 copy-start.15
  153.1 1.0 copy-start.17
  155.5 1.0 copy-start.9
  156.5 1.0 copy-start.11
  157.5 1.0 copy-start.13
  182.2 1.4 copy-start.3
Sparse Core Ops, SparseCore 0:
  11.7 104.8 all-gather.4
  155.6 26.6 all-gather.6

commit v2 on v1

v2 whole, which is shorter than its diff:
```python
import jax
import jax.numpy as jnp
from jax import lax
from jax.experimental import pallas as pl
from jax.experimental.pallas import tpu as pltpu
from jax.sharding import Mesh, PartitionSpec as P

LEVELS = 16
SEQ = ("z", "y")
CHAN = ("x", "k")
SUB = 8
F32 = jnp.float32
BF16 = jnp.bfloat16
VMEM_LIMIT = 24 * 1024 * 1024
VMEM_WHOLE = 61 * 1024 * 1024


def decay_table(length):
    levels = jnp.arange(LEVELS).astype(F32)
    half = LEVELS // 2
    slow_rates = 0.25 * jnp.power(16.0, levels / (half - 1.0)) / (8.0 * length)
    fast_rates = jnp.power(4.0, (levels - half) / (half - 1.0)) / 640.0
    return -jnp.where(levels < half, slow_rates, fast_rates)


def gelu_parts(gate):
    normal_cdf = 0.5 * (1.0 + lax.erf(gate * 0.7071067811865476))
    density = jnp.exp(-0.5 * gate * gate) * 0.3989422804014327
    return (gate * normal_cdf, normal_cdf + gate * density)


def sigmoid(value):
    return 1.0 / (1.0 + jnp.exp(-value))


def expm1(value):
    series = jnp.ones_like(value)
    for term in range(9, 1, -1):
        series = 1.0 + value * (1.0 / term) * series
    return jnp.where(jnp.abs(value) < 0.5, value * series, jnp.exp(value) - 1.0)


def local_scan(a, b, reverse, a_out, b_out):
    rows, width = a.shape
    tiles = rows // SUB
    a = a.reshape(tiles, SUB, width)
    b = b.reshape(tiles, SUB, width)
    row = lax.broadcasted_iota(jnp.int32, a.shape, 1)
    for step in (1, 2, 4):
        shift = SUB - step if reverse else step
        inside = row < SUB - step if reverse else row >= step
        a_from = jnp.where(inside, pltpu.roll(a, shift, 1), 1.0)
        b_from = jnp.where(inside, pltpu.roll(b, shift, 1), 0.0)
        b = b + a * b_from
        a = a * a_from
    prod = jnp.ones((1, width), F32)
    state = jnp.zeros((1, width), F32)
    edge = 0 if reverse else SUB - 1
    for tile in reversed(range(tiles)) if reverse else range(tiles):
        here_b = b[tile] + a[tile] * state
        here_a = a[tile] * prod
        b_out[pl.ds(tile * SUB, SUB), :] = here_b
        a_out[pl.ds(tile * SUB, SUB), :] = here_a
        state = here_b[edge : edge + 1]
        prod = here_a[edge : edge + 1]
    return prod, state


def shift_up(value, last):
    rows = value.shape[0]
    row = lax.broadcasted_iota(jnp.int32, value.shape, 0)
    return jnp.where(row == rows - 1, last, pltpu.roll(value, rows - 1, 0))


def before_kernel(
    x_ref, prev_ref, rec_ref, inw_ref, cw_ref, cb_ref, ld_ref,
    decay_ref, beta_ref, conv_ref, cum_ref, local_ref, post_ref, slope_ref, ends_ref, front_ref,
    padded, scan_a, scan_b,
):
    rows = x_ref.shape[0]
    lead = prev_ref.shape[0]
    padded[pl.ds(0, lead), :] = prev_ref[...].astype(F32)
    padded[pl.ds(lead, rows), :] = x_ref[...].astype(F32)
    conv = jnp.zeros(x_ref.shape, F32)
    for lag in range(4):
        conv = conv + cw_ref[lag : lag + 1, :] * padded[pl.ds(lead - lag, rows), :]
    conv = cb_ref[...] + conv
    recur = sigmoid(rec_ref[...].astype(F32))
    inward = sigmoid(inw_ref[...].astype(F32))
    log_step = 8.0 * recur * ld_ref[...]
    decay = jnp.exp(log_step)
    beta = jnp.sqrt(-expm1(2.0 * log_step))
    decay_ref[...] = decay
    beta_ref[...] = beta
    conv_ref[...] = conv
    prod, state = local_scan(decay, beta * (inward * conv), False, cum_ref, local_ref)
    ends_ref[...] = jnp.concatenate([prod, state], axis=0)
    local_scan(decay, jnp.zeros_like(decay), True, scan_a, scan_b)
    post = shift_up(scan_a[...], 1.0)
    post_ref[...] = post
    slope = post * beta * inward
    slope_ref[...] = slope
    front_ref[...] = slope[:SUB]


def before(
    x_branch, prev, recurrence_gate, input_gate, conv_weight, conv_bias, log_decay
):
    rows, width = x_branch.shape
    full = jax.ShapeDtypeStruct((rows, width), F32)
    return pl.pallas_call(
        before_kernel,
        out_shape=(full,) * 7
        + (
            jax.ShapeDtypeStruct((2, width), F32),
            jax.ShapeDtypeStruct((SUB, width), F32),
        ),
        scratch_shapes=[
            pltpu.VMEM((rows + prev.shape[0], width), F32),
            pltpu.VMEM((rows, width), F32),
            pltpu.VMEM((rows, width), F32),
        ],
        compiler_params=pltpu.CompilerParams(vmem_limit_bytes=VMEM_LIMIT),
    )(x_branch, prev, recurrence_gate, input_gate, conv_weight, conv_bias, log_decay)


def partial_kernel(rows_ref, w_ref, out_ref):
    for i in range(rows_ref.shape[0]):
        out_ref[i] = lax.dot_general(
            rows_ref[i], w_ref[...], (((1,), (1,)), ((), ())), preferred_element_type=F32
        ).astype(BF16)


def partial_products(blocks, weights):
    count, rows, width = blocks.shape
    return pl.pallas_call(
        partial_kernel,
        grid=(count // 2,),
        in_specs=[
            pl.BlockSpec((2, rows, width), lambda i: (i, 0, 0)),
            pl.BlockSpec(weights.shape, lambda i: (0, 0)),
        ],
        out_specs=pl.BlockSpec((2, rows, weights.shape[0]), lambda i: (i, 0, 0)),
        out_shape=jax.ShapeDtypeStruct((count, rows, weights.shape[0]), BF16),
        compiler_params=pltpu.CompilerParams(vmem_limit_bytes=VMEM_WHOLE),
    )(blocks, weights)


def total_kernel(parts_ref, out_ref):
    total = parts_ref[0].astype(F32)
    for i in range(1, parts_ref.shape[0]):
        total = total + parts_ref[i].astype(F32)
    out_ref[...] = total.astype(BF16)


def total_of(parts):
    return pl.pallas_call(
        total_kernel,
        out_shape=jax.ShapeDtypeStruct(parts.shape[1:], BF16),
        compiler_params=pltpu.CompilerParams(vmem_limit_bytes=VMEM_LIMIT),
    )(parts)


def adjoint_kernel(
    dlru_ref, gate_ref, decay_ref, beta_ref, inw_ref, ends_ref,
    adj_ref, offset_ref, front_ref, carry_ref,
    scan_a, scan_b,
):
    d_direct = dlru_ref[...].astype(F32) * gelu_parts(gate_ref[...].astype(F32))[0]
    decay = decay_ref[...]
    _, first = local_scan(decay, decay * d_direct, True, scan_a, scan_b)
    adj = d_direct + shift_up(scan_b[...], 0.0)
    adj_ref[...] = adj
    offset = adj * beta_ref[...] * sigmoid(inw_ref[...].astype(F32))
    offset_ref[...] = offset
    front_ref[...] = offset[:SUB]
    mine = jnp.concatenate([ends_ref[...], first], axis=0)
    carry_ref[...] = jnp.broadcast_to(mine[None], carry_ref.shape)


def adjoint(d_lru, gate, decay, beta, input_gate, ends, seq_count):
    rows, width = gate.shape
    full = jax.ShapeDtypeStruct((rows, width), F32)
    return pl.pallas_call(
        adjoint_kernel,
        out_shape=(
            full,
            full,
            jax.ShapeDtypeStruct((SUB, width), F32),
            jax.ShapeDtypeStruct((seq_count, 3, width), F32),
        ),
        scratch_shapes=[pltpu.VMEM((rows, width), F32)] * 2,
        compiler_params=pltpu.CompilerParams(vmem_limit_bytes=VMEM_LIMIT),
    )(d_lru, gate, decay, beta, input_gate, ends)


def branch_kernel(
    place_ref, carry_ref, offset_ref, slope_ref, cw_ref, front_a_ref, front_b_ref,
    branch_ref, kappa_ref,
    padded,
):
    rows, width = offset_ref.shape
    place = place_ref[0]
    beyond = jnp.zeros((1, width), F32)
    kappa = jnp.zeros((1, width), F32)
    for i in reversed(range(1, carry_ref.shape[0])):
        here = carry_ref[i, 2:3] + carry_ref[i, 0:1] * kappa
        beyond = jnp.where(i == place + 1, kappa, beyond)
        kappa = jnp.where(i > place, here, kappa)
    padded[pl.ds(0, rows), :] = offset_ref[...] + slope_ref[...] * kappa
    padded[pl.ds(rows, SUB), :] = front_a_ref[...] + front_b_ref[...] * beyond
    total = jnp.zeros((rows, width), F32)
    for lag in range(4):
        total = total + cw_ref[lag : lag + 1, :] * padded[pl.ds(lag, rows), :]
    branch_ref[...] = total.astype(BF16)
    kappa_ref[...] = kappa


def branch(place, carry, offset, slope, conv_weight, front_a, front_b):
    rows, width = offset.shape
    vmem = pl.BlockSpec(memory_space=pltpu.VMEM)
    return pl.pallas_call(
        branch_kernel,
        in_specs=[pl.BlockSpec(memory_space=pltpu.SMEM)] + [vmem] * 6,
        out_shape=(
            jax.ShapeDtypeStruct((rows, width), BF16),
            jax.ShapeDtypeStruct((1, width), F32),
        ),
        scratch_shapes=[pltpu.VMEM((rows + SUB, width), F32)],
        compiler_params=pltpu.CompilerParams(vmem_limit_bytes=VMEM_LIMIT),
    )(place, carry, offset, slope, conv_weight, front_a, front_b)


def gates_kernel(
    place_ref, carry_ref, kappa_ref, dlru_ref, adj_ref, post_ref, cum_ref, local_ref, decay_ref,
    beta_ref, conv_ref, gate_ref, rec_ref, inw_ref, ld_ref,
    dgate_ref, drec_ref, dinw_ref,
):
    place = place_ref[0]
    carried = jnp.zeros(kappa_ref.shape, F32)
    for i in range(carry_ref.shape[0] - 1):
        carried = jnp.where(i < place, carry_ref[i, 1:2] + carry_ref[i, 0:1] * carried, carried)
    states = local_ref[...] + cum_ref[...] * carried
    slope = gelu_parts(gate_ref[...].astype(F32))[1]
    dgate_ref[...] = (dlru_ref[...].astype(F32) * states * slope).astype(BF16)
    row = lax.broadcasted_iota(jnp.int32, states.shape, 0)
    states_prev = jnp.where(row == 0, carried, pltpu.roll(states, 1, 0))
    recur = sigmoid(rec_ref[...].astype(F32))
    inward = sigmoid(inw_ref[...].astype(F32))
    decay = decay_ref[...]
    beta = beta_ref[...]
    conv = conv_ref[...]
    adj = adj_ref[...] + post_ref[...] * kappa_ref[...]
    d_step = adj * (decay * states_prev - inward * conv * decay * decay / beta)
    drec_ref[...] = (d_step * 8.0 * ld_ref[...] * recur * (1.0 - recur)).astype(BF16)
    dinw_ref[...] = (adj * beta * conv * inward * (1.0 - inward)).astype(BF16)


def gates(place, carry, kappa, d_lru, *arrays):
    out = jax.ShapeDtypeStruct(d_lru.shape, BF16)
    vmem = pl.BlockSpec(memory_space=pltpu.VMEM)
    return pl.pallas_call(
        gates_kernel,
        in_specs=[pl.BlockSpec(memory_space=pltpu.SMEM)] + [vmem] * (3 + len(arrays)),
        out_shape=(out,) * 3,
        compiler_params=pltpu.CompilerParams(vmem_limit_bytes=VMEM_LIMIT),
    )(place, carry, kappa, d_lru, *arrays)


def input_kernel(core_ref, own_ref, other_ref, w_ref, out_ref, acc):
    step = pl.program_id(0)
    half = w_ref.shape[1] // 2

    @pl.when(step == 0)
    def _():
        acc[...] = jnp.zeros_like(acc)

    def add(first, second):
        dims = (((1,), (1,)), ((), ()))
        acc[...] += lax.dot_general(
            first, w_ref[:, :half], dims, preferred_element_type=F32
        ) + lax.dot_general(second, w_ref[:, half:], dims, preferred_element_type=F32)

    @pl.when(core_ref[0] == 0)
    def _():
        add(own_ref[0], other_ref[0])

    @pl.when(core_ref[0] != 0)
    def _():
        add(other_ref[0], own_ref[0])

    @pl.when(step == pl.num_programs(0) - 1)
    def _():
        out_ref[...] = acc[...].astype(BF16)


def input_grad(core, own, other, weights):
    steps, rows, width = own.shape
    return pl.pallas_call(
        input_kernel,
        grid=(steps,),
        in_specs=[
            pl.BlockSpec(memory_space=pltpu.SMEM),
            pl.BlockSpec((1, rows, width), lambda i: (i, 0, 0)),
            pl.BlockSpec((1, rows, width), lambda i: (i, 0, 0)),
            pl.BlockSpec((weights.shape[0], 2 * width), lambda i: (0, i)),
        ],
        out_specs=pl.BlockSpec((rows, weights.shape[0]), lambda i: (0, 0)),
        out_shape=jax.ShapeDtypeStruct((rows, weights.shape[0]), BF16),
        scratch_shapes=[pltpu.VMEM((rows, weights.shape[0]), F32)],
        compiler_params=pltpu.CompilerParams(vmem_limit_bytes=VMEM_WHOLE),
    )(core, own, other, weights)


def shards(
    d_out,
    x_branch,
    gate_branch,
    recurrence_gate,
    input_gate,
    conv_weight,
    conv_bias,
    decay_level,
    w_in,
    w_out,
):
    tok_rows, width = x_branch.shape
    z_count, y_count = lax.axis_size("z"), lax.axis_size("y")
    seq_count, chan_count = lax.axis_size(SEQ), lax.axis_size(CHAN)
    w_rows = w_out.shape[0]
    place = lax.axis_index(SEQ).astype(jnp.int32).reshape(1)
    core = lax.axis_index("k").astype(jnp.int32).reshape(1)
    forward = [(i, i + 1) for i in range(seq_count - 1)]
    backward = [(i + 1, i) for i in range(seq_count - 1)]
    swap = [(y * chan_count + c, c * chan_count + y) for y in range(y_count) for c in range(chan_count)]

    blocks = lax.all_gather(d_out, "y")
    pieces = lax.all_to_all(w_out.reshape(w_rows, chan_count, width), CHAN, 1, 0)
    spread = jnp.broadcast_to(pieces[None], (z_count,) + pieces.shape)
    out_block = lax.all_to_all(spread.reshape(seq_count, w_rows, width), SEQ, 0, 0)
    prev = lax.ppermute(x_branch[tok_rows - 16 :], SEQ, forward)
    log_table = decay_table(tok_rows * seq_count)
    onehot = decay_level[:, None] == jnp.arange(LEVELS)[None, :]
    log_decay = jnp.sum(jnp.where(onehot, log_table[None, :], 0.0), axis=1)[None, :]
    decay, beta, conv_out, cum_decay, local_states, post, slope, ends, front_b = before(
        x_branch, prev, recurrence_gate, input_gate, conv_weight, conv_bias[None, :], log_decay
    )

    next_b = lax.ppermute(front_b, SEQ, backward)

    blocks, w_in, out_block, ends, next_b = lax.optimization_barrier(
        (blocks, w_in, out_block, ends, next_b)
    )
    in_rows = lax.all_gather(w_in, SEQ, axis=0, tiled=True)
    partial = partial_products(blocks, out_block.reshape(seq_count * w_rows, width))
    total = total_of(lax.all_to_all(partial, CHAN, 0, 0))
    d_lru = lax.ppermute(total, ("y",) + CHAN, swap)
    adj_local, offset, front_a, carry = adjoint(
        d_lru, gate_branch, decay, beta, input_gate, ends, seq_count
    )
    next_a = lax.ppermute(front_a, SEQ, backward)
    carries = lax.all_to_all(carry, SEQ, 0, 0)
    d_branch, kappa = branch(place, carries, offset, slope, conv_weight, next_a, next_b)
    own = lax.all_gather(d_branch, "x")
    other = lax.ppermute(own, "k", [(0, 1), (1, 0)])
    d_gate, d_recurrence_gate, d_input_gate = gates(
        place, carries, kappa, d_lru, adj_local, post, cum_decay, local_states, decay,
        beta, conv_out, gate_branch, recurrence_gate, input_gate, log_decay,
    )
    d_input = input_grad(core, own, other, in_rows)
    return (d_input, d_gate, d_recurrence_gate, d_input_gate)


def solution(mesh):
    fine = Mesh(mesh.devices.reshape(8, 8, 4, 2), SEQ + CHAN)
    tokens = P(SEQ, CHAN)
    rows = P(CHAN + SEQ, None)
    in_specs = (tokens,) * 5 + (P(None, CHAN), P(CHAN), P(CHAN), rows, rows)
    return jax.shard_map(
        shards, mesh=fine, in_specs=in_specs, out_specs=(tokens,) * 4, check_vma=False
    )
```

time: 196 us -> 191 us (0.974)
  waiting for transfers between devices: 110 us -> 45 us
  blocking collectives: 11.8 us -> 56.8 us
  starting transfers between devices: 24.2 us -> 50.6 us
  local copies, waits for them, and re-layouts: 16.9 us -> 7.16 us
  other arithmetic: 2.46 us -> 0.1 us
    all_gather x2, waiting for transfers between devices: 96.1 us -> 1.05 us  [the longest x1 1.05 us: shards(): blocks = lax.all_gather(d_out, 'y')]
    all_to_all x0 -> x2, blocking collectives: none -> 43.7 us  [the longest x1 28.7 us: shards(): total = total_of(lax.all_to_all(partial, CHAN, 0, 0))]
    ppermute x1, waiting for transfers between devices: 0.7 us -> 15.6 us  [shards(): next_a = lax.ppermute(front_a, SEQ, backward)]
    ppermute x1, waiting for transfers between devices: 0.06 us -> 13.3 us  [shards(): prev = lax.ppermute(x_branch[tok_rows - 16:], SEQ, forward)]
    all_to_all x0 -> x1, starting transfers between devices: none -> 12.2 us  [shards(): lax.all_to_all(spread.reshape(seq_count, w_rows, width), SEQ, 0, 0)]
    unnamed x44 -> x30, local copies, waits for them, and re-layouts: 16.2 us -> 6.31 us
    all_to_all x1, starting transfers between devices: 9.79 us -> 19.1 us  [shards(): carries = lax.all_to_all(carry, SEQ, 0, 0)]
    ppermute x0 -> x1, waiting for transfers between devices: none -> 5.47 us  [shards(): d_lru = lax.ppermute(total, ('y',) + CHAN, swap)]
  transfers between devices with their start and end apart: 7 -> 9, of which waited for: 6 -> 6; matrix products, arithmetic and copies ran while one was open for 1% -> 1% of each run, Pallas kernels for 2% -> 6%
where the time goes in v2:
time: 191 us; the launch traced here: 190 us
  blocking collectives  56.8 us (30%)
  starting transfers between devices  50.6 us (26%)
  waiting for transfers between devices  45 us (24%)
  Pallas kernels  16.1 us (8%)
  between operations  14.2 us (7%)
  local copies, waits for them, and re-layouts  7.16 us (4%)
    all_to_all x1, blocking collectives, shards(): total = total_of(lax.all_to_all(partial, CHAN, 0, 0))  28.7 us
    all_to_all x1, starting transfers between devices, shards(): carries = lax.all_to_all(carry, SEQ, 0, 0)  19.1 us
    ppermute x1, waiting for transfers between devices, shards(): next_a = lax.ppermute(front_a, SEQ, backward)  15.6 us
    all_to_all x1, blocking collectives, shards(): lax.all_to_all(w_out.reshape(w_rows, chan_count, width), CHAN, 1, 0)  15 us
    ppermute x1, waiting for transfers between devices, shards(): prev = lax.ppermute(x_branch[tok_rows - 16:], SEQ, forward)  13.3 us
    all_gather x1, blocking collectives, shards(): own = lax.all_gather(d_branch, 'x')  13.2 us
    all_to_all x1, starting transfers between devices, shards(): lax.all_to_all(spread.reshape(seq_count, w_rows, width), SEQ, 0, 0)  12.2 us
    ppermute x1, starting transfers between devices, shards(): other = lax.ppermute(own, 'k', [(0, 1), (1, 0)])  9.14 us
  transfers between devices with their start and end apart: 9, of which 6 were waited for; matrix products, arithmetic and copies ran while one was open for 1% of the time, Pallas kernels for 6%

profile of v2, /device:TPU:1, one launch (start us, length us, event | category | flops | bytes accessed | tf_op | source)
XLA Modules:
  0.0 190.0 jit_solution(1075225409714021311)
XLA Ops:
  7.2 0.0 copy-start.11
  7.2 0.0 copy-start.14
  7.2 0.0 copy-start.13
  7.2 0.0 copy-start.1
  7.2 0.0 copy-start
  7.2 0.0 copy-start.12
  7.2 0.0 all-gather.7.cloned.1.call-start
  7.3 0.7 all-gather.7.cloned.1.call-update
  8.0 15.0 %all_to_all.30 = bf16[1,8,8,512]{3,1,0,2:T(8,128)(2,1)S(1)} all-to-all(bf16[1,8,8,512]{3,1,0,2:T(8,128)(2,1)} %bitcast.19), channel_id=1, replica_groups=mesh['z'=8,'y'=8,'x'=4,'k'=2] {'x','k'}, dimensions={2} | all-to-all | bytes 131072 | tf_op jit(solution)/shard_map/all_to_all | solution.py:338
  22.9 0.9 broadcast_in_dim.29
  23.8 12.2 %all-to-all-start.1 = ((bf16[64,8,512]{2,1,0:T(8,128)(2,1)}), bf16[64,8,512]{2,1,0:T(8,128)(2,1)}, u32[]{:S(2)}, u32[]{:S(2)}) async-start(bf16[64,8,512]{2,1,0:T(8,128)(2,1)} %bitcast.7), calls=%async_computation.1 | async-start | bytes 1048576 | tf_op jit(solution)/shard_map/all_to_all | solution.py:340
  36.0 0.0 all-gather.5.cloned.1.call-start
  36.1 0.0 copy-done.11
  36.1 2.8 %collective-permute-start = (bf16[16,512]{1,0:T(8,128)(2,1)S(1)}, bf16[16,512]{1,0:T(8,128)(2,1)S(1)}, u32[]{:S(2)}, u32[]{:S(2)}) collective-permute-start(bf16[16,512]{1,0:T(8,128)(2,1)S(1)} %slice.3), channel_id=1, source_target_pairs={{0,8},{8,16},{16,24},{24,32},{32,40},{40,48},{48,56},{56,64},{64,7... | collective-permute-start | bytes 49160 | tf_op jit(solution)/shard_map/ppermute | solution.py:341
  39.0 0.0 copy-done.14
  39.0 0.1 select_reduce_fusion
  39.1 13.3 %collective-permute-done.prev_ref = bf16[16,512]{1,0:T(8,128)(2,1)S(1)} collective-permute-done((bf16[16,512]{1,0:T(8,128)(2,1)S(1)}, bf16[16,512]{1,0:T(8,128)(2,1)S(1)}, u32[]{:S(2)}, u32[]{:S(2)}) %collective-permute-start) | collective-permute-done | bytes 16416 | tf_op jit(solution)/shard_map/ppermute | solution.py:341
  52.4 0.0 copy-done.13
  52.4 0.0 copy-done.1
  52.4 0.0 copy-done
  52.4 0.0 copy-done.12
  52.4 2.4 %shard_map.129 = (f32[192,512]{1,0:T(8,128)S(1)}, f32[192,512]{1,0:T(8,128)S(1)}, f32[192,512]{1,0:T(8,128)S(1)}, f32[192,512]{1,0:T(8,128)S(1)}, f32[192,512]{1...) custom-call(bf16[192,512]{1,0:T(8,128)(2,1)S(1)} %copy-done.11, ...), custom_call_target="tpu_custom_call" | custom-call | tf_op jit(solution)/shard_map/pallas_call | solution.py:111
  54.8 0.0 copy-start.3
  54.8 0.8 copy-done.3
  55.6 0.0 copy-start.7
  55.6 1.3 collective-permute-start.1
  56.9 4.5 %collective-permute-done.1.front_b_ref = f32[8,512]{1,0:T(8,128)S(1)} collective-permute-done((f32[8,512]{1,0:T(8,128)S(1)}, f32[8,512]{1,0:T(8,128)S(1)}, u32[]{:S(2)}, u32[]{:S(2)}) %collective-permute-start.1) | collective-permute-done | bytes 16416 | tf_op jit(solution)/shard_map/ppermute | solution.py:349
  61.4 0.0 all-to-all-done.1
  61.4 1.1 all-gather.7.cloned.1.call-done
  62.5 0.0 all-gather.5.cloned.1.call-update
  62.5 4.7 %shard_map.130 = bf16[8,192,512]{2,1,0:T(8,128)(2,1)} custom-call(bf16[8,192,512]{2,1,0:T(8,128)(2,1)} %bitcast.17, bf16[512,512]{1,0:T(8,128)(2,1)} %bitcast.10.w_ref), custom_call_target="tpu_custom_call" | custom-call | tf_op jit(solution)/shard_map/pallas_call | solution.py:136
  67.2 0.0 copy-done.7
  67.2 28.7 %all_to_all.31.parts_ref = bf16[8,192,512]{2,1,0:T(8,128)(2,1)S(1)} all-to-all(bf16[8,192,512]{2,1,0:T(8,128)(2,1)} %shard_map.130), channel_id=1, replica_groups=mesh['z'=8,'y'=8,'x'=4,'k'=2] {'x','k'}, dimensions={0} | all-to-all | bytes 3145728 | tf_op jit(solution)/shard_map/all_to_all | solution.py:356
  95.9 0.0 copy-start.2
  95.9 0.2 shard_map.131
  96.1 4.5 %collective-permute-start.2 = (bf16[192,512]{1,0:T(8,128)(2,1)S(1)}, bf16[192,512]{1,0:T(8,128)(2,1)S(1)}, u32[]{:S(2)}, u32[]{:S(2)}) collective-permute-start(bf16[192,512]{1,0:T(8,128)(2,1)S(1)} %shard_map.131), channel_id=1, source_target_pairs={{0,0},{1,8},{2,16},{3,24},{4,32},{5,40},{6,48},{7,56},{8,1},{9,9},... | collective-permute-start | bytes 589832 | tf_op jit(solution)/shard_map/ppermute | solution.py:357
  100.6 5.5 %collective-permute-done.2.dlru_ref = bf16[192,512]{1,0:T(8,128)(2,1)S(1)} collective-permute-done((bf16[192,512]{1,0:T(8,128)(2,1)S(1)}, bf16[192,512]{1,0:T(8,128)(2,1)S(1)}, u32[]{:S(2)}, u32[]{:S(2)}) %collective-permute-start.2) | collective-permute-done | bytes 196640 | tf_op jit(solution)/shard_map/ppermute | solution.py:357
  106.1 0.0 copy-done.2
  106.1 1.5 shard_map.132
  107.7 0.0 copy-start.5
  107.7 0.8 copy-done.5
  108.4 0.0 copy-start.9
  108.4 0.7 copy-done.9
  109.2 19.1 %all-to-all-start.3 = ((f32[64,3,512]{2,1,0:T(4,128)}), f32[64,3,512]{2,1,0:T(4,128)S(1)}, u32[]{:S(2)}, u32[]{:S(2)}) async-start(f32[64,3,512]{2,1,0:T(4,128)} %get-tuple-element.34), calls=%async_computation.3 | async-start | bytes 1048576 | tf_op jit(solution)/shard_map/all_to_all | solution.py:362
  128.3 1.3 collective-permute-start.3
  129.6 15.6 %collective-permute-done.3.front_a_ref = f32[8,512]{1,0:T(8,128)S(1)} collective-permute-done((f32[8,512]{1,0:T(8,128)S(1)}, f32[8,512]{1,0:T(8,128)S(1)}, u32[]{:S(2)}, u32[]{:S(2)}) %collective-permute-start.3) | collective-permute-done | bytes 16416 | tf_op jit(solution)/shard_map/ppermute | solution.py:361
  145.2 4.3 %all-to-all-done.3.carry_ref = f32[64,3,512]{2,1,0:T(4,128)S(1)} async-done(((f32[64,3,512]{2,1,0:T(4,128)}), f32[64,3,512]{2,1,0:T(4,128)S(1)}, u32[]{:S(2)}, u32[]{:S(2)}) %all-to-all-start.3) | async-done | bytes 393248 | tf_op jit(solution)/shard_map/all_to_all | solution.py:362
  149.5 0.0 copy-start.8
  149.6 1.0 copy-done.8
  150.5 0.0 copy-start.10
  150.5 1.0 copy-done.10
  151.5 0.5 shard_map.133
  152.1 13.2 %all-gather.1 = bf16[768,512]{1,0:T(8,128)(2,1)} all-gather(bf16[192,512]{1,0:T(8,128)(2,1)S(1)} %get-tuple-element.39), channel_id=3, replica_groups=mesh['z'=8,'y'=8,'x'=4,'k'=2] {'x'}, dimensions={0}, use_global_device_ids=true | all-gather | bytes 983040 | tf_op jit(solution)/shard_map/all_gather | solution.py:364
  165.2 9.1 %collective-permute-start.4 = (bf16[4,192,512]{2,1,0:T(8,128)(2,1)}, bf16[4,192,512]{2,1,0:T(8,128)(2,1)}, u32[]{:S(2)}, u32[]{:S(2)}) collective-permute-start(bf16[4,192,512]{2,1,0:T(8,128)(2,1)} %bitcast.11.own_ref), channel_id=1, source_target_pairs={{0,1},{1,0},{2,3},{3,2},{4,5},{5,4},{6,7},{7,6},{8,9},{9,8},{10,11... | collective-permute-start | bytes 2359304 | tf_op jit(solution)/shard_map/ppermute | solution.py:365
  174.4 0.0 copy-start.4
  174.4 1.0 copy-done.4
  175.4 0.0 copy-start.6
  175.4 1.0 copy-done.6
  176.4 1.5 shard_map.135
  177.9 0.0 collective-permute-done.4.other_ref
  177.9 0.0 all-gather.5.cloned.1.call-done.w_ref
  177.9 5.2 %shard_map.134 = bf16[192,512]{1,0:T(8,128)(2,1)} custom-call(s32[1]{0:T(128)} %bitcast.core_ref, bf16[4,192,512]{2,1,0:T(8,128)(2,1)} %bitcast.11.own_ref, bf16[4,192,512]{2,1,0:T(8,128)(2,1)} %collective-permute-done.4.other_ref, bf16[512,4096]{1,0:T(8,128)(2,1)} %all-gather.5.cloned.1.call-done.w_ref), custom_call_target="tpu_custom_call" | custom-call | tf_op jit(solution)/shard_map/pallas_call | solution.py:299
  (2 shorter events, 0.0 us)
Async XLA Ops:
  7.2 28.9 %copy-start.11 = (bf16[192,512]{1,0:T(8,128)(2,1)S(1)}, bf16[192,512]{1,0:T(8,128)(2,1)}, u32[]{:S(2)}) copy-start(bf16[192,512]{1,0:T(8,128)(2,1)} %x_ref.1) | copy-start | bytes 589828
  7.2 31.8 %copy-start.14 = (s32[512]{0:T(512)S(1)}, s32[512]{0:T(512)}, u32[]{:S(2)}) copy-start(s32[512]{0:T(512)} %param.17) | copy-start | bytes 6148
  7.2 45.2 %copy-start.13 = (f32[512]{0:T(512)S(1)}, f32[512]{0:T(512)}, u32[]{:S(2)}) copy-start(f32[512]{0:T(512)} %param.16) | copy-start | bytes 6148
  7.2 45.2 %copy-start.1 = (bf16[192,512]{1,0:T(8,128)(2,1)S(1)}, bf16[192,512]{1,0:T(8,128)(2,1)}, u32[]{:S(2)}) copy-start(bf16[192,512]{1,0:T(8,128)(2,1)} %rec_ref.3) | copy-start | bytes 589828
  7.2 45.2 %copy-start = (bf16[192,512]{1,0:T(8,128)(2,1)S(1)}, bf16[192,512]{1,0:T(8,128)(2,1)}, u32[]{:S(2)}) copy-start(bf16[192,512]{1,0:T(8,128)(2,1)} %inw_ref.5) | copy-start | bytes 589828
  7.2 45.2 %copy-start.12 = (f32[4,512]{1,0:T(4,128)S(1)}, f32[4,512]{1,0:T(4,128)}, u32[]{:S(2)}) copy-start(f32[4,512]{1,0:T(4,128)} %cw_ref.3) | copy-start | bytes 24580
  7.2 55.2 %all-gather.7.cloned.1.call-start = ((), (), s32[]{:S(2)}) async-start(), calls=%async_computation.5 | async-start | bytes 1769472 | tf_op jit(solution)/shard_map/all_gather | solution.py:337
  23.8 37.6 %all-to-all-start.1 = ((bf16[64,8,512]{2,1,0:T(8,128)(2,1)}), bf16[64,8,512]{2,1,0:T(8,128)(2,1)}, u32[]{:S(2)}, u32[]{:S(2)}) async-start(bf16[64,8,512]{2,1,0:T(8,128)(2,1)} %bitcast.7), calls=%async_computation.1 | async-start | bytes 1048576 | tf_op jit(solution)/shard_map/all_to_all | solution.py:340
  36.0 141.9 %all-gather.5.cloned.1.call-start = ((), (), s32[]{:S(2)}) async-start(), calls=%async_computation.4 | async-start | bytes 4259840 | tf_op jit(solution)/shard_map/all_gather | solution.py:354
  36.1 16.3 %collective-permute-start = (bf16[16,512]{1,0:T(8,128)(2,1)S(1)}, bf16[16,512]{1,0:T(8,128)(2,1)S(1)}, u32[]{:S(2)}, u32[]{:S(2)}) collective-permute-start(bf16[16,512]{1,0:T(8,128)(2,1)S(1)} %slice.3), channel_id=1, source_target_pairs={{0,8},{8,16},{16,24},{24,32},{32,40},{40,48},{48,56},{56,64},{64,7... | collective-permute-start | bytes 49160 | tf_op jit(solution)/shard_map/ppermute | solution.py:341
  54.8 0.8 copy-start.3
  55.6 11.6 %copy-start.7 = (f32[192,512]{1,0:T(8,128)}, f32[192,512]{1,0:T(8,128)S(1)}, u32[]{:S(2)}) copy-start(f32[192,512]{1,0:T(8,128)S(1)} %get-tuple-element.36.slope_ref) | copy-start | bytes 1179652
  55.6 5.8 %collective-permute-start.1 = (f32[8,512]{1,0:T(8,128)S(1)}, f32[8,512]{1,0:T(8,128)S(1)}, u32[]{:S(2)}, u32[]{:S(2)}) collective-permute-start(f32[8,512]{1,0:T(8,128)S(1)} %get-tuple-element.28), channel_id=1, source_target_pairs={{8,0},{16,8},{24,16},{32,24},{40,32},{48,40},{56,48},{64,56},{72,6... | collective-permute-start | bytes 49160 | tf_op jit(solution)/shard_map/ppermute | solution.py:349
  95.9 10.2 %copy-start.2 = (bf16[192,512]{1,0:T(8,128)(2,1)S(1)}, bf16[192,512]{1,0:T(8,128)(2,1)}, u32[]{:S(2)}) copy-start(bf16[192,512]{1,0:T(8,128)(2,1)} %gate_ref.3) | copy-start | bytes 589828
  96.1 10.0 %collective-permute-start.2 = (bf16[192,512]{1,0:T(8,128)(2,1)S(1)}, bf16[192,512]{1,0:T(8,128)(2,1)S(1)}, u32[]{:S(2)}, u32[]{:S(2)}) collective-permute-start(bf16[192,512]{1,0:T(8,128)(2,1)S(1)} %shard_map.131), channel_id=1, source_target_pairs={{0,0},{1,8},{2,16},{3,24},{4,32},{5,40},{6,48},{7,56},{8,1},{9,9},... | collective-permute-start | bytes 589832 | tf_op jit(solution)/shard_map/ppermute | solution.py:357
  107.7 0.8 copy-start.5
  108.4 0.7 copy-start.9
  109.2 40.4 %all-to-all-start.3 = ((f32[64,3,512]{2,1,0:T(4,128)}), f32[64,3,512]{2,1,0:T(4,128)S(1)}, u32[]{:S(2)}, u32[]{:S(2)}) async-start(f32[64,3,512]{2,1,0:T(4,128)} %get-tuple-element.34), calls=%async_computation.3 | async-start | bytes 1048576 | tf_op jit(solution)/shard_map/all_to_all | solution.py:362
  128.3 16.9 %collective-permute-start.3 = (f32[8,512]{1,0:T(8,128)S(1)}, f32[8,512]{1,0:T(8,128)S(1)}, u32[]{:S(2)}, u32[]{:S(2)}) collective-permute-start(f32[8,512]{1,0:T(8,128)S(1)} %get-tuple-element.37), channel_id=1, source_target_pairs={{8,0},{16,8},{24,16},{32,24},{40,32},{48,40},{56,48},{64,56},{72,6... | collective-permute-start | bytes 49160 | tf_op jit(solution)/shard_map/ppermute | solution.py:361
  149.5 1.0 copy-start.8
  150.5 1.0 copy-start.10
  165.2 12.7 %collective-permute-start.4 = (bf16[4,192,512]{2,1,0:T(8,128)(2,1)}, bf16[4,192,512]{2,1,0:T(8,128)(2,1)}, u32[]{:S(2)}, u32[]{:S(2)}) collective-permute-start(bf16[4,192,512]{2,1,0:T(8,128)(2,1)} %bitcast.11.own_ref), channel_id=1, source_target_pairs={{0,1},{1,0},{2,3},{3,2},{4,5},{5,4},{6,7},{7,6},{8,9},{9,8},{10,11... | collective-permute-start | bytes 2359304 | tf_op jit(solution)/shard_map/ppermute | solution.py:365
  174.4 1.0 copy-start.4
  175.4 1.0 copy-start.6
Sparse Core Ops, SparseCore 0:
  10.1 52.2 all-gather.6
  65.5 101.1 all-gather.4

commit v3 on v2

--- a/solution.py
+++ b/solution.py
@@ -124,74 +124,84 @@
     )(x_branch, prev, recurrence_gate, input_gate, conv_weight, conv_bias, log_decay)
 
 
-def partial_kernel(rows_ref, w_ref, out_ref):
-    for i in range(rows_ref.shape[0]):
-        out_ref[i] = lax.dot_general(
-            rows_ref[i], w_ref[...], (((1,), (1,)), ((), ())), preferred_element_type=F32
-        ).astype(BF16)
-
-
-def partial_products(blocks, weights):
-    count, rows, width = blocks.shape
-    return pl.pallas_call(
-        partial_kernel,
-        grid=(count // 2,),
+def adjoint_kernel(
+    core_ref, own_ref, other_ref, w_ref, gate_ref, decay_ref, beta_ref, inw_ref, ends_ref,
+    dlru_ref, adj_ref, offset_ref, front_ref, carry_ref,
+    acc, scan_a, scan_b,
+):
+    step = pl.program_id(0)
+    half = w_ref.shape[1] // 2
+
+    @pl.when(step == 0)
+    def _():
+        acc[...] = jnp.zeros_like(acc)
+
+    def add(first, second):
+        dims = (((1,), (1,)), ((), ()))
+        acc[...] += lax.dot_general(
+            first, w_ref[:, :half], dims, preferred_element_type=F32
+        ) + lax.dot_general(second, w_ref[:, half:], dims, preferred_element_type=F32)
+
+    @pl.when(core_ref[0] == 0)
+    def _():
+        add(own_ref[0], other_ref[0])
+
+    @pl.when(core_ref[0] != 0)
+    def _():
+        add(other_ref[0], own_ref[0])
+
+    @pl.when(step == pl.num_programs(0) - 1)
+    def _():
+        d_lru = acc[...]
+        dlru_ref[...] = d_lru
+        d_direct = d_lru * gelu_parts(gate_ref[...].astype(F32))[0]
+        decay = decay_ref[...]
+        _, first = local_scan(decay, decay * d_direct, True, scan_a, scan_b)
+        adj = d_direct + shift_up(scan_b[...], 0.0)
+        adj_ref[...] = adj
+        offset = adj * beta_ref[...] * sigmoid(inw_ref[...].astype(F32))
+        offset_ref[...] = offset
+        front_ref[...] = offset[:SUB]
+        mine = jnp.concatenate([ends_ref[...], first], axis=0)
+        carry_ref[...] = jnp.broadcast_to(mine[None], carry_ref.shape)
+
+
+def adjoint(core, own, other, weights, gate, decay, beta, input_gate, ends, seq_count):
+    rows, width = gate.shape
+    steps = own.shape[0]
+    full = jax.ShapeDtypeStruct((rows, width), F32)
+    whole = lambda shape: pl.BlockSpec(shape, lambda i: (0,) * len(shape))
+    return pl.pallas_call(
+        adjoint_kernel,
+        grid=(steps,),
         in_specs=[
-            pl.BlockSpec((2, rows, width), lambda i: (i, 0, 0)),
-            pl.BlockSpec(weights.shape, lambda i: (0, 0)),
+            pl.BlockSpec(memory_space=pltpu.SMEM),
+            pl.BlockSpec((1, rows, width), lambda i: (i, 0, 0)),
+            pl.BlockSpec((1, rows, width), lambda i: (i, 0, 0)),
+            pl.BlockSpec((width, 2 * width), lambda i: (0, i)),
+            whole((rows, width)),
+            whole((rows, width)),
+            whole((rows, width)),
+            whole((rows, width)),
+            whole((2, width)),
         ],
-        out_specs=pl.BlockSpec((2, rows, weights.shape[0]), lambda i: (i, 0, 0)),
-        out_shape=jax.ShapeDtypeStruct((count, rows, weights.shape[0]), BF16),
-        compiler_params=pltpu.CompilerParams(vmem_limit_bytes=VMEM_WHOLE),
-    )(blocks, weights)
-
-
-def total_kernel(parts_ref, out_ref):
-    total = parts_ref[0].astype(F32)
-    for i in range(1, parts_ref.shape[0]):
-        total = total + parts_ref[i].astype(F32)
-    out_ref[...] = total.astype(BF16)
-
-
-def total_of(parts):
-    return pl.pallas_call(
-        total_kernel,
-        out_shape=jax.ShapeDtypeStruct(parts.shape[1:], BF16),
-        compiler_params=pltpu.CompilerParams(vmem_limit_bytes=VMEM_LIMIT),
-    )(parts)
-
-
-def adjoint_kernel(
-    dlru_ref, gate_ref, decay_ref, beta_ref, inw_ref, ends_ref,
-    adj_ref, offset_ref, front_ref, carry_ref,
-    scan_a, scan_b,
-):
-    d_direct = dlru_ref[...].astype(F32) * gelu_parts(gate_ref[...].astype(F32))[0]
-    decay = decay_ref[...]
-    _, first = local_scan(decay, decay * d_direct, True, scan_a, scan_b)
-    adj = d_direct + shift_up(scan_b[...], 0.0)
-    adj_ref[...] = adj
-    offset = adj * beta_ref[...] * sigmoid(inw_ref[...].astype(F32))
-    offset_ref[...] = offset
-    front_ref[...] = offset[:SUB]
-    mine = jnp.concatenate([ends_ref[...], first], axis=0)
-    carry_ref[...] = jnp.broadcast_to(mine[None], carry_ref.shape)
-
-
-def adjoint(d_lru, gate, decay, beta, input_gate, ends, seq_count):
-    rows, width = gate.shape
-    full = jax.ShapeDtypeStruct((rows, width), F32)
-    return pl.pallas_call(
-        adjoint_kernel,
+        out_specs=[
+            whole((rows, width)),
+            whole((rows, width)),
+            whole((rows, width)),
+            whole((SUB, width)),
+            whole((seq_count, 3, width)),
+        ],
         out_shape=(
+            full,
             full,
             full,
             jax.ShapeDtypeStruct((SUB, width), F32),
             jax.ShapeDtypeStruct((seq_count, 3, width), F32),
         ),
-        scratch_shapes=[pltpu.VMEM((rows, width), F32)] * 2,
-        compiler_params=pltpu.CompilerParams(vmem_limit_bytes=VMEM_LIMIT),
-    )(d_lru, gate, decay, beta, input_gate, ends)
+        scratch_shapes=[pltpu.VMEM((rows, width), F32)] * 3,
+        compiler_params=pltpu.CompilerParams(vmem_limit_bytes=VMEM_WHOLE),
+    )(core, own, other, weights, gate, decay, beta, input_gate, ends)
 
 
 def branch_kernel(
@@ -325,19 +335,18 @@
     w_out,
 ):
     tok_rows, width = x_branch.shape
-    z_count, y_count = lax.axis_size("z"), lax.axis_size("y")
-    seq_count, chan_count = lax.axis_size(SEQ), lax.axis_size(CHAN)
-    w_rows = w_out.shape[0]
+    seq_count = lax.axis_size(SEQ)
     place = lax.axis_index(SEQ).astype(jnp.int32).reshape(1)
     core = lax.axis_index("k").astype(jnp.int32).reshape(1)
     forward = [(i, i + 1) for i in range(seq_count - 1)]
     backward = [(i + 1, i) for i in range(seq_count - 1)]
-    swap = [(y * chan_count + c, c * chan_count + y) for y in range(y_count) for c in range(chan_count)]
-
-    blocks = lax.all_gather(d_out, "y")
-    pieces = lax.all_to_all(w_out.reshape(w_rows, chan_count, width), CHAN, 1, 0)
-    spread = jnp.broadcast_to(pieces[None], (z_count,) + pieces.shape)
-    out_block = lax.all_to_all(spread.reshape(seq_count, w_rows, width), SEQ, 0, 0)
+    cores = [(0, 1), (1, 0)]
+
+    out_rows = lax.all_gather(w_out, SEQ, axis=0, tiled=True)
+    in_part = lax.all_gather(w_in, "y", axis=0, tiled=True)
+    in_rows = lax.all_gather(in_part, "z", axis=0, tiled=True)
+    out_own = lax.all_gather(d_out, "x")
+    out_other = lax.ppermute(out_own, "k", cores)
     prev = lax.ppermute(x_branch[tok_rows - 16 :], SEQ, forward)
     log_table = decay_table(tok_rows * seq_count)
     onehot = decay_level[:, None] == jnp.arange(LEVELS)[None, :]
@@ -348,21 +357,15 @@
 
     next_b = lax.ppermute(front_b, SEQ, backward)
 
-    blocks, w_in, out_block, ends, next_b = lax.optimization_barrier(
-        (blocks, w_in, out_block, ends, next_b)
-    )
-    in_rows = lax.all_gather(w_in, SEQ, axis=0, tiled=True)
-    partial = partial_products(blocks, out_block.reshape(seq_count * w_rows, width))
-    total = total_of(lax.all_to_all(partial, CHAN, 0, 0))
-    d_lru = lax.ppermute(total, ("y",) + CHAN, swap)
-    adj_local, offset, front_a, carry = adjoint(
-        d_lru, gate_branch, decay, beta, input_gate, ends, seq_count
+    ends, next_b, in_part = lax.optimization_barrier((ends, next_b, in_part))
+    d_lru, adj_local, offset, front_a, carry = adjoint(
+        core, out_own, out_other, out_rows, gate_branch, decay, beta, input_gate, ends, seq_count
     )
     next_a = lax.ppermute(front_a, SEQ, backward)
     carries = lax.all_to_all(carry, SEQ, 0, 0)
     d_branch, kappa = branch(place, carries, offset, slope, conv_weight, next_a, next_b)
     own = lax.all_gather(d_branch, "x")
-    other = lax.ppermute(own, "k", [(0, 1), (1, 0)])
+    other = lax.ppermute(own, "k", cores)
     d_gate, d_recurrence_gate, d_input_gate = gates(
         place, carries, kappa, d_lru, adj_local, post, cum_decay, local_states, decay,
         beta, conv_out, gate_branch, recurrence_gate, input_gate, log_decay,

time: 191 us -> 184 us (0.963)
  starting transfers between devices: 50.6 us -> 36.8 us
  waiting for transfers between devices: 45 us -> 54.4 us
  blocking collectives: 56.8 us -> 49 us
  local copies, waits for them, and re-layouts: 7.16 us -> 11.7 us
    all_to_all x2 -> x0, blocking collectives: 43.7 us -> none  [the longest x1 28.7 us: shards(): total = total_of(lax.all_to_all(partial, CHAN, 0, 0))]
    all_gather x0 -> x2, blocking collectives: none -> 35.7 us  [the longest x1 23.9 us: shards(): in_part = lax.all_gather(w_in, 'y', axis=0, tiled=True)]
    all_gather x2, waiting for transfers between devices: 1.05 us -> 35.9 us  [the longest x1 24.4 us: shards(): out_rows = lax.all_gather(w_out, SEQ, axis=0, tiled=True)]
    ppermute x1, waiting for transfers between devices: 13.3 us -> 0.06 us  [shards(): prev = lax.ppermute(x_branch[tok_rows - 16:], SEQ, forward)]
    all_to_all x1 -> x0, starting transfers between devices: 12.2 us -> none  [shards(): lax.all_to_all(spread.reshape(seq_count, w_rows, width), SEQ, 0, 0)]
    ppermute x2, starting transfers between devices: 13.7 us -> 24 us  [the longest x1 14.1 us: shards(): out_other = lax.ppermute(out_own, 'k', cores)]
    all_to_all x1, starting transfers between devices: 19.1 us -> 8.88 us  [shards(): carries = lax.all_to_all(carry, SEQ, 0, 0)]
    ppermute x1, waiting for transfers between devices: 15.6 us -> 7.98 us  [shards(): next_a = lax.ppermute(front_a, SEQ, backward)]
  transfers between devices with their start and end apart: 9 -> 8, of which waited for: 6 -> 6; matrix products, arithmetic and copies ran while one was open for 1% -> 1% of each run, Pallas kernels for 6% -> 6%
where the time goes in v3:
time: 184 us; the launch traced here: 183 us
  waiting for transfers between devices  54.4 us (30%)
  blocking collectives  49 us (27%)
  starting transfers between devices  36.8 us (20%)
  Pallas kernels  16.5 us (9%)
  between operations  14.2 us (8%)
  local copies, waits for them, and re-layouts  11.7 us (6%)
    all_gather x1, waiting for transfers between devices, shards(): out_rows = lax.all_gather(w_out, SEQ, axis=0, tiled=True)  24.4 us
    all_gather x1, blocking collectives, shards(): in_part = lax.all_gather(w_in, 'y', axis=0, tiled=True)  23.9 us
    ppermute x1, starting transfers between devices, shards(): out_other = lax.ppermute(out_own, 'k', cores)  14.1 us
    all_gather x1, blocking collectives, shards(): own = lax.all_gather(d_branch, 'x')  13.2 us
    all_gather x1, blocking collectives, shards(): out_own = lax.all_gather(d_out, 'x')  11.8 us
    all_gather x1, waiting for transfers between devices, shards(): in_rows = lax.all_gather(in_part, 'z', axis=0, tiled=True)  11.6 us
    unnamed x42, local copies, waits for them, and re-layouts  11 us
    ppermute x1, starting transfers between devices, shards(): other = lax.ppermute(own, 'k', cores)  9.87 us
  transfers between devices with their start and end apart: 8, of which 6 were waited for; matrix products, arithmetic and copies ran while one was open for 1% of the time, Pallas kernels for 6%

profile of v3, /device:TPU:1, one launch (start us, length us, event | category | flops | bytes accessed | tf_op | source)
XLA Modules:
  0.0 183.4 jit_solution(13956657140691942976)
XLA Ops:
  7.2 0.0 all-gather.5.cloned.1.call-start
  7.2 0.7 all-gather.5.cloned.1.call-update
  7.9 0.0 all-gather.7.cloned.1.call-start
  7.9 23.9 %all_gather.24 = bf16[64,4096]{1,0:T(8,128)(2,1)} all-gather(bf16[8,4096]{1,0:T(8,128)(2,1)} %param.18), channel_id=1, replica_groups=mesh['z'=8,'y'=8,'x'=4,'k'=2] {'y'}, dimensions={0}, use_global_device_ids=true | all-gather | bytes 589824 | tf_op jit(solution)/shard_map/all_gather | solution.py:346
  31.9 0.0 all-gather.7.cloned.1.call-update
  31.9 11.8 %all-gather = bf16[768,512]{1,0:T(8,128)(2,1)S(1)} all-gather(bf16[192,512]{1,0:T(8,128)(2,1)} %param.10), channel_id=2, replica_groups=mesh['z'=8,'y'=8,'x'=4,'k'=2] {'x'}, dimensions={0}, use_global_device_ids=true | all-gather | bytes 983040 | tf_op jit(solution)/shard_map/all_gather | solution.py:348
  43.7 0.0 copy-start.19
  43.7 14.1 %collective-permute-start = (bf16[4,192,512]{2,1,0:T(8,128)(2,1)S(1)}, bf16[4,192,512]{2,1,0:T(8,128)(2,1)S(1)}, u32[]{:S(2)}, u32[]{:S(2)}) collective-permute-start(bf16[4,192,512]{2,1,0:T(8,128)(2,1)S(1)} %bitcast.9), channel_id=1, source_target_pairs={{0,1},{1,0},{2,3},{3,2},{4,5},{5,4},{6,7},{7,6},{8,9},{9,8},{10,11... | collective-permute-start | bytes 2359304 | tf_op jit(solution)/shard_map/ppermute | solution.py:349
  57.8 0.7 slice.3
  58.5 1.3 collective-permute-start.1
  59.8 0.8 select_reduce_fusion
  60.6 0.1 collective-permute-done.1.prev_ref
  60.7 0.0 copy-start
  60.7 0.9 copy-done
  61.6 0.0 copy-start.7
  61.6 0.9 copy-done.7
  62.5 0.0 copy-start.14
  62.5 0.9 copy-done.14
  63.5 0.0 copy-start.15
  63.5 0.7 copy-done.15
  64.2 0.0 copy-start.18
  64.2 0.7 copy-done.18
  64.8 0.0 copy-start.16
  64.8 2.4 %shard_map.129 = (f32[192,512]{1,0:T(8,128)S(1)}, f32[192,512]{1,0:T(8,128)S(1)}, f32[192,512]{1,0:T(8,128)S(1)}, f32[192,512]{1,0:T(8,128)S(1)}, f32[192,512]{1...) custom-call(bf16[192,512]{1,0:T(8,128)(2,1)S(1)} %copy-done.14, ...), custom_call_target="tpu_custom_call" | custom-call | tf_op jit(solution)/shard_map/pallas_call | solution.py:111
  67.2 0.0 copy-start.2
  67.2 0.7 copy-done.2
  68.0 0.0 copy-start.4
  68.0 0.7 copy-done.4
  68.7 0.0 copy-start.10
  68.7 0.7 copy-done.10
  69.4 0.0 copy-start.17
  69.4 0.6 copy-done.17
  70.0 1.3 collective-permute-start.2
  71.3 4.1 %collective-permute-done.2.front_b_ref = f32[8,512]{1,0:T(8,128)S(1)} collective-permute-done((f32[8,512]{1,0:T(8,128)S(1)}, f32[8,512]{1,0:T(8,128)S(1)}, u32[]{:S(2)}, u32[]{:S(2)}) %collective-permute-start.2) | collective-permute-done | bytes 16416 | tf_op jit(solution)/shard_map/ppermute | solution.py:358
  75.4 0.0 collective-permute-done.other_ref
  75.4 24.4 %all-gather.5.cloned.1.call-done.w_ref = bf16[512,4096]{1,0:T(8,128)(2,1)} async-done(((bf16[8,4096]{1,0:T(8,128)(2,1)}), bf16[512,4096]{1,0:T(8,128)(2,1)}) %all-gather.5.cloned.1.call-update) | async-done | bytes 4194320 | tf_op jit(solution)/shard_map/all_gather | solution.py:345
  99.8 0.0 copy-done.19
  99.8 0.0 copy-done.20
  99.8 0.0 copy-start.5
  99.8 0.0 copy-start.6
  99.9 0.0 copy-start.8
  99.9 7.0 %shard_map.130 = (f32[192,512]{1,0:T(8,128)}, f32[192,512]{1,0:T(8,128)}, f32[192,512]{1,0:T(8,128)}, f32[8,512]{1,0:T(8,128)}, f32[64,3,512]{2,1,0:T(4,128)}) custom-call(s32[1]{0:T(128)} %bitcast.core_ref, bf16[4,192,512]{2,1,0:T(8,128)(2,1)} %bitcast.10, bf16[4,192,512]{2,1,0:T(8,128)(2,1)} %copy-done.20, ...), custom_call_target="tpu_custom_call" | custom-call | tf_op jit(solution)/shard_map/pallas_call | solution.py:174
  106.9 8.9 %all-to-all-start = ((f32[64,3,512]{2,1,0:T(4,128)}), f32[64,3,512]{2,1,0:T(4,128)S(1)}, u32[]{:S(2)}, u32[]{:S(2)}) async-start(f32[64,3,512]{2,1,0:T(4,128)} %get-tuple-element.30), calls=%async_computation | async-start | bytes 1048576 | tf_op jit(solution)/shard_map/all_to_all | solution.py:365
  115.8 1.3 collective-permute-start.3
  117.1 8.0 %collective-permute-done.3.front_a_ref = f32[8,512]{1,0:T(8,128)S(1)} collective-permute-done((f32[8,512]{1,0:T(8,128)}, f32[8,512]{1,0:T(8,128)S(1)}, u32[]{:S(2)}, u32[]{:S(2)}) %collective-permute-start.3) | collective-permute-done | bytes 16416 | tf_op jit(solution)/shard_map/ppermute | solution.py:364
  125.1 5.6 %all-to-all-done.carry_ref = f32[64,3,512]{2,1,0:T(4,128)S(1)} async-done(((f32[64,3,512]{2,1,0:T(4,128)}), f32[64,3,512]{2,1,0:T(4,128)S(1)}, u32[]{:S(2)}, u32[]{:S(2)}) %all-to-all-start) | async-done | bytes 393248 | tf_op jit(solution)/shard_map/all_to_all | solution.py:365
  130.7 0.0 copy-done.16
  130.7 1.0 copy-done.9
  131.7 0.5 shard_map.131
  132.2 13.2 %all-gather.1 = bf16[768,512]{1,0:T(8,128)(2,1)} all-gather(bf16[192,512]{1,0:T(8,128)(2,1)S(1)} %get-tuple-element.35), channel_id=3, replica_groups=mesh['z'=8,'y'=8,'x'=4,'k'=2] {'x'}, dimensions={0}, use_global_device_ids=true | all-gather | bytes 983040 | tf_op jit(solution)/shard_map/all_gather | solution.py:367
  145.4 9.9 %collective-permute-start.4 = (bf16[4,192,512]{2,1,0:T(8,128)(2,1)}, bf16[4,192,512]{2,1,0:T(8,128)(2,1)}, u32[]{:S(2)}, u32[]{:S(2)}) collective-permute-start(bf16[4,192,512]{2,1,0:T(8,128)(2,1)} %bitcast.5.own_ref), channel_id=1, source_target_pairs={{0,1},{1,0},{2,3},{3,2},{4,5},{5,4},{6,7},{7,6},{8,9},{9,8},{10,11... | collective-permute-start | bytes 2359304 | tf_op jit(solution)/shard_map/ppermute | solution.py:368
  155.3 0.0 copy-done.1
  155.3 0.0 copy-done.3
  155.3 0.0 copy-done.5
  155.3 0.0 copy-done.6
  155.3 0.0 copy-done.8
  155.3 0.0 copy-start.11
  155.4 1.0 copy-done.11
  156.3 1.0 copy-done.12
  157.4 1.0 copy-done.13
  158.4 1.5 shard_map.133
  159.8 11.6 %all-gather.7.cloned.1.call-done.w_ref = bf16[512,4096]{1,0:T(8,128)(2,1)} async-done(((bf16[64,4096]{1,0:T(8,128)(2,1)}), bf16[512,4096]{1,0:T(8,128)(2,1)}) %all-gather.7.cloned.1.call-update) | async-done | bytes 4194320 | tf_op jit(solution)/shard_map/all_gather | solution.py:347
  171.4 0.0 collective-permute-done.4.other_ref
  171.4 5.2 %shard_map.132 = bf16[192,512]{1,0:T(8,128)(2,1)} custom-call(s32[1]{0:T(128)} %bitcast.core_ref, bf16[4,192,512]{2,1,0:T(8,128)(2,1)} %bitcast.5.own_ref, bf16[4,192,512]{2,1,0:T(8,128)(2,1)} %collective-permute-done.4.other_ref, bf16[512,4096]{1,0:T(8,128)(2,1)} %all-gather.7.cloned.1.call-done.w_ref), custom_call_target="tpu_custom_call" | custom-call | tf_op jit(solution)/shard_map/pallas_call | solution.py:309
  (7 shorter events, 0.0 us)
Async XLA Ops:
  7.2 92.7 %all-gather.5.cloned.1.call-start = ((), (), s32[]{:S(2)}) async-start(), calls=%async_computation.1 | async-start | bytes 4259840 | tf_op jit(solution)/shard_map/all_gather | solution.py:345
  7.9 163.5 %all-gather.7.cloned.1.call-start = ((), (), s32[]{:S(2)}) async-start(), calls=%async_computation.2 | async-start | bytes 4718592 | tf_op jit(solution)/shard_map/all_gather | solution.py:347
  43.7 56.1 %copy-start.19 = (bf16[768,512]{1,0:T(8,128)(2,1)}, bf16[768,512]{1,0:T(8,128)(2,1)S(1)}, u32[]{:S(2)}) copy-start(bf16[768,512]{1,0:T(8,128)(2,1)S(1)} %all-gather) | copy-start | bytes 2359300
  43.7 31.7 %collective-permute-start = (bf16[4,192,512]{2,1,0:T(8,128)(2,1)S(1)}, bf16[4,192,512]{2,1,0:T(8,128)(2,1)S(1)}, u32[]{:S(2)}, u32[]{:S(2)}) collective-permute-start(bf16[4,192,512]{2,1,0:T(8,128)(2,1)S(1)} %bitcast.9), channel_id=1, source_target_pairs={{0,1},{1,0},{2,3},{3,2},{4,5},{5,4},{6,7},{7,6},{8,9},{9,8},{10,11... | collective-permute-start | bytes 2359304 | tf_op jit(solution)/shard_map/ppermute | solution.py:349
  58.5 2.1 %collective-permute-start.1 = (bf16[16,512]{1,0:T(8,128)(2,1)S(1)}, bf16[16,512]{1,0:T(8,128)(2,1)S(1)}, u32[]{:S(2)}, u32[]{:S(2)}) collective-permute-start(bf16[16,512]{1,0:T(8,128)(2,1)S(1)} %slice.3), channel_id=1, source_target_pairs={{0,8},{8,16},{16,24},{24,32},{32,40},{40,48},{48,56},{56,64},{64,7... | collective-permute-start | bytes 49160 | tf_op jit(solution)/shard_map/ppermute | solution.py:350
  60.7 0.9 copy-start
  61.6 0.9 copy-start.7
  62.5 0.9 copy-start.14
  63.5 0.7 copy-start.15
  64.2 0.7 copy-start.18
  64.8 65.8 %copy-start.16 = (f32[4,512]{1,0:T(4,128)S(1)}, f32[4,512]{1,0:T(4,128)}, u32[]{:S(2)}) copy-start(f32[4,512]{1,0:T(4,128)} %cw_ref.3) | copy-start | bytes 24580
  67.2 0.8 copy-start.2
  68.0 0.7 copy-start.4
  68.7 0.8 copy-start.10
  69.4 0.6 copy-start.17
  70.0 5.4 %collective-permute-start.2 = (f32[8,512]{1,0:T(8,128)S(1)}, f32[8,512]{1,0:T(8,128)S(1)}, u32[]{:S(2)}, u32[]{:S(2)}) collective-permute-start(f32[8,512]{1,0:T(8,128)S(1)} %get-tuple-element.28), channel_id=1, source_target_pairs={{8,0},{16,8},{24,16},{32,24},{40,32},{48,40},{56,48},{64,56},{72,6... | collective-permute-start | bytes 49160 | tf_op jit(solution)/shard_map/ppermute | solution.py:358
  75.4 24.4 %copy-start.20 = (bf16[4,192,512]{2,1,0:T(8,128)(2,1)}, bf16[4,192,512]{2,1,0:T(8,128)(2,1)S(1)}, u32[]{:S(2)}) copy-start(bf16[4,192,512]{2,1,0:T(8,128)(2,1)S(1)} %collective-permute-done.other_ref) | copy-start | bytes 2359300
  99.8 55.5 %copy-start.1 = (bf16[192,512]{1,0:T(8,128)(2,1)S(1)}, bf16[192,512]{1,0:T(8,128)(2,1)}, u32[]{:S(2)}) copy-start(bf16[192,512]{1,0:T(8,128)(2,1)} %inw_ref.5) | copy-start | bytes 589828
  99.8 55.5 %copy-start.3 = (f32[192,512]{1,0:T(8,128)S(1)}, f32[192,512]{1,0:T(8,128)}, u32[]{:S(2)}) copy-start(f32[192,512]{1,0:T(8,128)} %copy-done.2) | copy-start | bytes 1179652
  99.8 55.5 %copy-start.5 = (f32[192,512]{1,0:T(8,128)S(1)}, f32[192,512]{1,0:T(8,128)}, u32[]{:S(2)}) copy-start(f32[192,512]{1,0:T(8,128)} %copy-done.4) | copy-start | bytes 1179652
  99.8 55.5 %copy-start.6 = (bf16[192,512]{1,0:T(8,128)(2,1)S(1)}, bf16[192,512]{1,0:T(8,128)(2,1)}, u32[]{:S(2)}) copy-start(bf16[192,512]{1,0:T(8,128)(2,1)} %gate_ref.3) | copy-start | bytes 589828
  99.9 55.5 %copy-start.8 = (bf16[192,512]{1,0:T(8,128)(2,1)S(1)}, bf16[192,512]{1,0:T(8,128)(2,1)}, u32[]{:S(2)}) copy-start(bf16[192,512]{1,0:T(8,128)(2,1)} %rec_ref.3) | copy-start | bytes 589828
  106.9 23.8 %all-to-all-start = ((f32[64,3,512]{2,1,0:T(4,128)}), f32[64,3,512]{2,1,0:T(4,128)S(1)}, u32[]{:S(2)}, u32[]{:S(2)}) async-start(f32[64,3,512]{2,1,0:T(4,128)} %get-tuple-element.30), calls=%async_computation | async-start | bytes 1048576 | tf_op jit(solution)/shard_map/all_to_all | solution.py:365
  115.8 9.3 %collective-permute-start.3 = (f32[8,512]{1,0:T(8,128)}, f32[8,512]{1,0:T(8,128)S(1)}, u32[]{:S(2)}, u32[]{:S(2)}) collective-permute-start(f32[8,512]{1,0:T(8,128)} %get-tuple-element.33), channel_id=1, source_target_pairs={{8,0},{16,8},{24,16},{32,24},{40,32},{48,40},{56,48},{64,56},{72,6... | collective-permute-start | bytes 49160 | tf_op jit(solution)/shard_map/ppermute | solution.py:364
  130.7 1.0 copy-start.9
  145.4 26.0 %collective-permute-start.4 = (bf16[4,192,512]{2,1,0:T(8,128)(2,1)}, bf16[4,192,512]{2,1,0:T(8,128)(2,1)}, u32[]{:S(2)}, u32[]{:S(2)}) collective-permute-start(bf16[4,192,512]{2,1,0:T(8,128)(2,1)} %bitcast.5.own_ref), channel_id=1, source_target_pairs={{0,1},{1,0},{2,3},{3,2},{4,5},{5,4},{6,7},{7,6},{8,9},{9,8},{10,11... | collective-permute-start | bytes 2359304 | tf_op jit(solution)/shard_map/ppermute | solution.py:368
  155.3 1.0 copy-start.11
  156.3 1.0 copy-start.12
  157.4 1.0 copy-start.13
Sparse Core Ops, SparseCore 0:
  11.1 88.7 all-gather.4
  101.9 69.4 all-gather.6

commit v4 on v3

--- a/solution.py
+++ b/solution.py
@@ -277,35 +277,42 @@
     )(place, carry, kappa, d_lru, *arrays)
 
 
-def input_kernel(core_ref, own_ref, other_ref, w_ref, out_ref, acc):
+def input_kernel(core_ref, own_ref, other_ref, first_ref, rest_ref, out_ref, acc):
     step = pl.program_id(0)
-    half = w_ref.shape[1] // 2
-
-    @pl.when(step == 0)
-    def _():
-        acc[...] = jnp.zeros_like(acc)
-
-    def add(first, second):
+    half = first_ref.shape[1] // 2
+
+    def product(left, right, w_ref):
         dims = (((1,), (1,)), ((), ()))
-        acc[...] += lax.dot_general(
-            first, w_ref[:, :half], dims, preferred_element_type=F32
-        ) + lax.dot_general(second, w_ref[:, half:], dims, preferred_element_type=F32)
+        return lax.dot_general(
+            left, w_ref[:, :half], dims, preferred_element_type=F32
+        ) + lax.dot_general(right, w_ref[:, half:], dims, preferred_element_type=F32)
+
+    def add(left, right):
+        @pl.when(step == 0)
+        def _():
+            acc[...] = product(left[0], right[0], first_ref)
+
+        @pl.when(step != 0)
+        def _():
+            acc[...] += product(left[0], right[0], rest_ref)
 
     @pl.when(core_ref[0] == 0)
     def _():
-        add(own_ref[0], other_ref[0])
+        add(own_ref, other_ref)
 
     @pl.when(core_ref[0] != 0)
     def _():
-        add(other_ref[0], own_ref[0])
+        add(other_ref, own_ref)
 
     @pl.when(step == pl.num_programs(0) - 1)
     def _():
         out_ref[...] = acc[...].astype(BF16)
 
 
-def input_grad(core, own, other, weights):
+def input_grad(core, own, other, first, rest):
     steps, rows, width = own.shape
+    feats = first.shape[0]
+    at = first.shape[1] // (2 * width) - 1
     return pl.pallas_call(
         input_kernel,
         grid=(steps,),
@@ -313,13 +320,14 @@
             pl.BlockSpec(memory_space=pltpu.SMEM),
             pl.BlockSpec((1, rows, width), lambda i: (i, 0, 0)),
             pl.BlockSpec((1, rows, width), lambda i: (i, 0, 0)),
-            pl.BlockSpec((weights.shape[0], 2 * width), lambda i: (0, i)),
+            pl.BlockSpec((feats, 2 * width), lambda i: (0, at)),
+            pl.BlockSpec((feats, 2 * width), lambda i: (0, jnp.maximum(i - 1, 0))),
         ],
-        out_specs=pl.BlockSpec((rows, weights.shape[0]), lambda i: (0, 0)),
-        out_shape=jax.ShapeDtypeStruct((rows, weights.shape[0]), BF16),
-        scratch_shapes=[pltpu.VMEM((rows, weights.shape[0]), F32)],
+        out_specs=pl.BlockSpec((rows, feats), lambda i: (0, 0)),
+        out_shape=jax.ShapeDtypeStruct((rows, feats), BF16),
+        scratch_shapes=[pltpu.VMEM((rows, feats), F32)],
         compiler_params=pltpu.CompilerParams(vmem_limit_bytes=VMEM_WHOLE),
-    )(core, own, other, weights)
+    )(core, own, other, first, rest)
 
 
 def shards(
@@ -342,9 +350,10 @@
     backward = [(i + 1, i) for i in range(seq_count - 1)]
     cores = [(0, 1), (1, 0)]
 
-    out_rows = lax.all_gather(w_out, SEQ, axis=0, tiled=True)
-    in_part = lax.all_gather(w_in, "y", axis=0, tiled=True)
-    in_rows = lax.all_gather(in_part, "z", axis=0, tiled=True)
+    first = jnp.concatenate([w_out, w_in[:, : 2 * width]], axis=1)
+    first = lax.all_gather(first, SEQ, axis=0, tiled=True)
+    rest = lax.all_gather(w_in[:, 2 * width :], "y", axis=0, tiled=True)
+    in_rows = lax.all_gather(rest, "z", axis=0, tiled=True)
     out_own = lax.all_gather(d_out, "x")
     out_other = lax.ppermute(out_own, "k", cores)
     prev = lax.ppermute(x_branch[tok_rows - 16 :], SEQ, forward)
@@ -357,9 +366,9 @@
 
     next_b = lax.ppermute(front_b, SEQ, backward)
 
-    ends, next_b, in_part = lax.optimization_barrier((ends, next_b, in_part))
+    ends, next_b = lax.optimization_barrier((ends, next_b))
     d_lru, adj_local, offset, front_a, carry = adjoint(
-        core, out_own, out_other, out_rows, gate_branch, decay, beta, input_gate, ends, seq_count
+        core, out_own, out_other, first, gate_branch, decay, beta, input_gate, ends, seq_count
     )
     next_a = lax.ppermute(front_a, SEQ, backward)
     carries = lax.all_to_all(carry, SEQ, 0, 0)
@@ -370,7 +379,7 @@
         place, carries, kappa, d_lru, adj_local, post, cum_decay, local_states, decay,
         beta, conv_out, gate_branch, recurrence_gate, input_gate, log_decay,
     )
-    d_input = input_grad(core, own, other, in_rows)
+    d_input = input_grad(core, own, other, first, in_rows)
     return (d_input, d_gate, d_recurrence_gate, d_input_gate)
 
 

time: 184 us -> 177 us (0.962)
  waiting for transfers between devices: 54.4 us -> 44.1 us
    all_gather x2, waiting for transfers between devices: 35.9 us -> 26.3 us  [the longest x1 25.1 us: shards(): first = lax.all_gather(first, SEQ, axis=0, tiled=True)]
where the time goes in v4:
time: 177 us; the launch traced here: 176 us
  blocking collectives  48.5 us (27%)
  waiting for transfers between devices  44.1 us (25%)
  starting transfers between devices  37 us (21%)
  Pallas kernels  16.8 us (9%)
  between operations  14.2 us (8%)
  local copies, waits for them, and re-layouts  13.2 us (7%)
  other arithmetic  2.26 us (1%)
    all_gather x1, waiting for transfers between devices, shards(): first = lax.all_gather(first, SEQ, axis=0, tiled=True)  25.1 us
    all_gather x1, blocking collectives, shards(): rest = lax.all_gather(w_in[:, 2 * width:], 'y', axis=0, tiled=True)  23.2 us
    ppermute x1, starting transfers between devices, shards(): out_other = lax.ppermute(out_own, 'k', cores)  14.8 us
    all_gather x1, blocking collectives, shards(): own = lax.all_gather(d_branch, 'x')  13.9 us
    all_gather x1, blocking collectives, shards(): out_own = lax.all_gather(d_out, 'x')  11.3 us
    unnamed x42, local copies, waits for them, and re-layouts  11 us
    ppermute x1, starting transfers between devices, shards(): other = lax.ppermute(own, 'k', cores)  9.57 us
    all_to_all x1, starting transfers between devices, shards(): carries = lax.all_to_all(carry, SEQ, 0, 0)  8.75 us
  transfers between devices with their start and end apart: 8, of which 6 were waited for; matrix products, arithmetic and copies ran while one was open for 1% of the time, Pallas kernels for 6%

profile of v4, /device:TPU:1, one launch (start us, length us, event | category | flops | bytes accessed | tf_op | source)
XLA Modules:
  0.0 176.1 jit_solution(9607305243150717385)
XLA Ops:
  7.2 0.0 all-gather.5.cloned.1.call-start
  7.2 0.7 slice.9
  7.9 1.5 pad_maximum_fusion
  9.4 0.0 all-gather.5.cloned.1.call-update
  9.4 0.0 all-gather.7.cloned.1.call-start
  9.5 0.8 slice.11
  10.3 23.2 %all_gather.26 = bf16[64,3072]{1,0:T(8,128)(2,1)} all-gather(bf16[8,3072]{1,0:T(8,128)(2,1)S(1)} %slice.11), channel_id=1, replica_groups=mesh['z'=8,'y'=8,'x'=4,'k'=2] {'y'}, dimensions={0}, use_global_device_ids=true | all-gather | bytes 442368 | tf_op jit(solution)/shard_map/all_gather | solution.py:355
  33.5 0.0 all-gather.7.cloned.1.call-update
  33.6 0.0 copy-start.16
  33.6 11.3 %all-gather = bf16[768,512]{1,0:T(8,128)(2,1)S(1)} all-gather(bf16[192,512]{1,0:T(8,128)(2,1)} %param.10), channel_id=2, replica_groups=mesh['z'=8,'y'=8,'x'=4,'k'=2] {'x'}, dimensions={0}, use_global_device_ids=true | all-gather | bytes 983040 | tf_op jit(solution)/shard_map/all_gather | solution.py:357
  44.9 0.0 copy-start.19
  44.9 14.8 %collective-permute-start = (bf16[4,192,512]{2,1,0:T(8,128)(2,1)S(1)}, bf16[4,192,512]{2,1,0:T(8,128)(2,1)S(1)}, u32[]{:S(2)}, u32[]{:S(2)}) collective-permute-start(bf16[4,192,512]{2,1,0:T(8,128)(2,1)S(1)} %bitcast.9), channel_id=1, source_target_pairs={{0,1},{1,0},{2,3},{3,2},{4,5},{5,4},{6,7},{7,6},{8,9},{9,8},{10,11... | collective-permute-start | bytes 2359304 | tf_op jit(solution)/shard_map/ppermute | solution.py:358
  59.7 0.7 slice.10
  60.4 1.3 collective-permute-start.1
  61.7 0.8 select_reduce_fusion
  62.5 0.1 collective-permute-done.1.prev_ref
  62.6 0.0 copy-start
  62.6 0.9 copy-done
  63.5 0.9 copy-done.6
  64.4 0.0 copy-start.14
  64.4 0.9 copy-done.14
  65.3 0.0 copy-start.15
  65.3 0.7 copy-done.15
  66.0 0.0 copy-start.18
  66.0 0.7 copy-done.18
  66.7 2.4 %shard_map.129 = (f32[192,512]{1,0:T(8,128)S(1)}, f32[192,512]{1,0:T(8,128)S(1)}, f32[192,512]{1,0:T(8,128)S(1)}, f32[192,512]{1,0:T(8,128)S(1)}, f32[192,512]{1...) custom-call(bf16[192,512]{1,0:T(8,128)(2,1)S(1)} %copy-done.14, ...), custom_call_target="tpu_custom_call" | custom-call | tf_op jit(solution)/shard_map/pallas_call | solution.py:111
  69.1 0.0 copy-start.2
  69.1 0.7 copy-done.2
  69.8 0.0 copy-start.4
  69.8 0.8 copy-done.4
  70.6 0.7 copy-done.10
  71.3 0.6 copy-done.17
  71.9 1.3 collective-permute-start.2
  73.2 4.2 %collective-permute-done.2.front_b_ref = f32[8,512]{1,0:T(8,128)S(1)} collective-permute-done((f32[8,512]{1,0:T(8,128)S(1)}, f32[8,512]{1,0:T(8,128)S(1)}, u32[]{:S(2)}, u32[]{:S(2)}) %collective-permute-start.2) | collective-permute-done | bytes 16416 | tf_op jit(solution)/shard_map/ppermute | solution.py:367
  77.4 0.0 collective-permute-done.other_ref
  77.4 25.1 %all-gather.5.cloned.1.call-done.w_ref.first_ref = bf16[512,5120]{1,0:T(8,128)(2,1)} async-done(((bf16[8,5120]{1,0:T(8,128)(2,1)}), bf16[512,5120]{1,0:T(8,128)(2,1)}) %all-gather.5.cloned.1.call-update) | async-done | bytes 5242896 | tf_op jit(solution)/shard_map/all_gather | solution.py:354
  102.5 0.0 copy-done.19
  102.5 0.0 copy-done.20
  102.5 0.0 copy-start.5
  102.5 0.0 copy-start.7
  102.5 0.0 copy-start.8
  102.6 6.9 %shard_map.130 = (f32[192,512]{1,0:T(8,128)}, f32[192,512]{1,0:T(8,128)}, f32[192,512]{1,0:T(8,128)}, f32[8,512]{1,0:T(8,128)}, f32[64,3,512]{2,1,0:T(4,128)}) custom-call(s32[1]{0:T(128)} %bitcast.core_ref, bf16[4,192,512]{2,1,0:T(8,128)(2,1)} %bitcast.10, bf16[4,192,512]{2,1,0:T(8,128)(2,1)} %copy-done.20, ...), custom_call_target="tpu_custom_call" | custom-call | tf_op jit(solution)/shard_map/pallas_call | solution.py:174
  109.4 8.8 %all-to-all-start = ((f32[64,3,512]{2,1,0:T(4,128)}), f32[64,3,512]{2,1,0:T(4,128)S(1)}, u32[]{:S(2)}, u32[]{:S(2)}) async-start(f32[64,3,512]{2,1,0:T(4,128)} %get-tuple-element.30), calls=%async_computation | async-start | bytes 1048576 | tf_op jit(solution)/shard_map/all_to_all | solution.py:374
  118.2 1.3 collective-permute-start.3
  119.5 8.6 %collective-permute-done.3.front_a_ref = f32[8,512]{1,0:T(8,128)S(1)} collective-permute-done((f32[8,512]{1,0:T(8,128)}, f32[8,512]{1,0:T(8,128)S(1)}, u32[]{:S(2)}, u32[]{:S(2)}) %collective-permute-start.3) | collective-permute-done | bytes 16416 | tf_op jit(solution)/shard_map/ppermute | solution.py:373
  128.1 4.9 %all-to-all-done.carry_ref = f32[64,3,512]{2,1,0:T(4,128)S(1)} async-done(((f32[64,3,512]{2,1,0:T(4,128)}), f32[64,3,512]{2,1,0:T(4,128)S(1)}, u32[]{:S(2)}, u32[]{:S(2)}) %all-to-all-start) | async-done | bytes 393248 | tf_op jit(solution)/shard_map/all_to_all | solution.py:374
  133.0 0.0 copy-done.16
  133.1 1.0 copy-done.9
  134.0 0.5 shard_map.131
  134.6 13.9 %all-gather.1 = bf16[768,512]{1,0:T(8,128)(2,1)} all-gather(bf16[192,512]{1,0:T(8,128)(2,1)S(1)} %get-tuple-element.35), channel_id=3, replica_groups=mesh['z'=8,'y'=8,'x'=4,'k'=2] {'x'}, dimensions={0}, use_global_device_ids=true | all-gather | bytes 983040 | tf_op jit(solution)/shard_map/all_gather | solution.py:376
  148.4 9.6 %collective-permute-start.4 = (bf16[4,192,512]{2,1,0:T(8,128)(2,1)}, bf16[4,192,512]{2,1,0:T(8,128)(2,1)}, u32[]{:S(2)}, u32[]{:S(2)}) collective-permute-start(bf16[4,192,512]{2,1,0:T(8,128)(2,1)} %bitcast.5.own_ref), channel_id=1, source_target_pairs={{0,1},{1,0},{2,3},{3,2},{4,5},{5,4},{6,7},{7,6},{8,9},{9,8},{10,11... | collective-permute-start | bytes 2359304 | tf_op jit(solution)/shard_map/ppermute | solution.py:377
  158.0 0.0 copy-done.1
  158.0 0.0 copy-done.3
  158.0 0.0 copy-done.5
  158.1 0.0 copy-done.7
  158.1 0.0 copy-done.8
  158.1 0.0 copy-start.11
  158.1 1.0 copy-done.11
  159.1 1.0 copy-done.12
  160.1 1.0 copy-done.13
  161.1 1.5 shard_map.133
  162.5 1.1 all-gather.7.cloned.1.call-done.rest_ref
  163.7 0.0 collective-permute-done.4.other_ref
  163.7 5.6 %shard_map.132 = bf16[192,512]{1,0:T(8,128)(2,1)} custom-call(s32[1]{0:T(128)} %bitcast.core_ref, bf16[4,192,512]{2,1,0:T(8,128)(2,1)} %bitcast.5.own_ref, bf16[4,192,512]{2,1,0:T(8,128)(2,1)} %collective-permute-done.4.other_ref, bf16[512,5120]{1,0:T(8,128)(2,1)} %all-gather.5.cloned.1.call-done.w_ref.first_ref, ...), custom_call_target="tpu_custom_call" | custom-call | tf_op jit(solution)/shard_map/pallas_call | solution.py:316
  (10 shorter events, 0.0 us)
Async XLA Ops:
  7.2 95.3 %all-gather.5.cloned.1.call-start = ((), (), s32[]{:S(2)}) async-start(), calls=%async_computation.1 | async-start | bytes 5324800 | tf_op jit(solution)/shard_map/all_gather | solution.py:354
  9.4 154.2 %all-gather.7.cloned.1.call-start = ((), (), s32[]{:S(2)}) async-start(), calls=%async_computation.2 | async-start | bytes 3538944 | tf_op jit(solution)/shard_map/all_gather | solution.py:356
  33.6 99.5 %copy-start.16 = (f32[4,512]{1,0:T(4,128)S(1)}, f32[4,512]{1,0:T(4,128)}, u32[]{:S(2)}) copy-start(f32[4,512]{1,0:T(4,128)} %cw_ref.3) | copy-start | bytes 24580
  44.9 57.6 %copy-start.19 = (bf16[768,512]{1,0:T(8,128)(2,1)}, bf16[768,512]{1,0:T(8,128)(2,1)S(1)}, u32[]{:S(2)}) copy-start(bf16[768,512]{1,0:T(8,128)(2,1)S(1)} %all-gather) | copy-start | bytes 2359300
  44.9 32.5 %collective-permute-start = (bf16[4,192,512]{2,1,0:T(8,128)(2,1)S(1)}, bf16[4,192,512]{2,1,0:T(8,128)(2,1)S(1)}, u32[]{:S(2)}, u32[]{:S(2)}) collective-permute-start(bf16[4,192,512]{2,1,0:T(8,128)(2,1)S(1)} %bitcast.9), channel_id=1, source_target_pairs={{0,1},{1,0},{2,3},{3,2},{4,5},{5,4},{6,7},{7,6},{8,9},{9,8},{10,11... | collective-permute-start | bytes 2359304 | tf_op jit(solution)/shard_map/ppermute | solution.py:358
  60.4 2.1 %collective-permute-start.1 = (bf16[16,512]{1,0:T(8,128)(2,1)S(1)}, bf16[16,512]{1,0:T(8,128)(2,1)S(1)}, u32[]{:S(2)}, u32[]{:S(2)}) collective-permute-start(bf16[16,512]{1,0:T(8,128)(2,1)S(1)} %slice.10), channel_id=1, source_target_pairs={{0,8},{8,16},{16,24},{24,32},{32,40},{40,48},{48,56},{56,64},{64,7... | collective-permute-start | bytes 49160 | tf_op jit(solution)/shard_map/ppermute | solution.py:359
  62.6 0.9 copy-start
  63.5 0.9 copy-start.6
  64.4 0.9 copy-start.14
  65.3 0.7 copy-start.15
  66.0 0.7 copy-start.18
  69.1 0.7 copy-start.2
  69.8 0.8 copy-start.4
  70.6 0.7 copy-start.10
  71.3 0.6 copy-start.17
  71.9 5.5 %collective-permute-start.2 = (f32[8,512]{1,0:T(8,128)S(1)}, f32[8,512]{1,0:T(8,128)S(1)}, u32[]{:S(2)}, u32[]{:S(2)}) collective-permute-start(f32[8,512]{1,0:T(8,128)S(1)} %get-tuple-element.28), channel_id=1, source_target_pairs={{8,0},{16,8},{24,16},{32,24},{40,32},{48,40},{56,48},{64,56},{72,6... | collective-permute-start | bytes 49160 | tf_op jit(solution)/shard_map/ppermute | solution.py:367
  77.4 25.1 %copy-start.20 = (bf16[4,192,512]{2,1,0:T(8,128)(2,1)}, bf16[4,192,512]{2,1,0:T(8,128)(2,1)S(1)}, u32[]{:S(2)}) copy-start(bf16[4,192,512]{2,1,0:T(8,128)(2,1)S(1)} %collective-permute-done.other_ref) | copy-start | bytes 2359300
  102.5 55.5 %copy-start.1 = (bf16[192,512]{1,0:T(8,128)(2,1)S(1)}, bf16[192,512]{1,0:T(8,128)(2,1)}, u32[]{:S(2)}) copy-start(bf16[192,512]{1,0:T(8,128)(2,1)} %inw_ref.5) | copy-start | bytes 589828
  102.5 55.5 %copy-start.3 = (f32[192,512]{1,0:T(8,128)S(1)}, f32[192,512]{1,0:T(8,128)}, u32[]{:S(2)}) copy-start(f32[192,512]{1,0:T(8,128)} %copy-done.2) | copy-start | bytes 1179652
  102.5 55.5 %copy-start.5 = (f32[192,512]{1,0:T(8,128)S(1)}, f32[192,512]{1,0:T(8,128)}, u32[]{:S(2)}) copy-start(f32[192,512]{1,0:T(8,128)} %copy-done.4) | copy-start | bytes 1179652
  102.5 55.5 %copy-start.7 = (bf16[192,512]{1,0:T(8,128)(2,1)S(1)}, bf16[192,512]{1,0:T(8,128)(2,1)}, u32[]{:S(2)}) copy-start(bf16[192,512]{1,0:T(8,128)(2,1)} %rec_ref.3) | copy-start | bytes 589828
  102.5 55.5 %copy-start.8 = (bf16[192,512]{1,0:T(8,128)(2,1)S(1)}, bf16[192,512]{1,0:T(8,128)(2,1)}, u32[]{:S(2)}) copy-start(bf16[192,512]{1,0:T(8,128)(2,1)} %gate_ref.3) | copy-start | bytes 589828
  109.4 23.6 %all-to-all-start = ((f32[64,3,512]{2,1,0:T(4,128)}), f32[64,3,512]{2,1,0:T(4,128)S(1)}, u32[]{:S(2)}, u32[]{:S(2)}) async-start(f32[64,3,512]{2,1,0:T(4,128)} %get-tuple-element.30), calls=%async_computation | async-start | bytes 1048576 | tf_op jit(solution)/shard_map/all_to_all | solution.py:374
  118.2 9.9 %collective-permute-start.3 = (f32[8,512]{1,0:T(8,128)}, f32[8,512]{1,0:T(8,128)S(1)}, u32[]{:S(2)}, u32[]{:S(2)}) collective-permute-start(f32[8,512]{1,0:T(8,128)} %get-tuple-element.33), channel_id=1, source_target_pairs={{8,0},{16,8},{24,16},{32,24},{40,32},{48,40},{56,48},{64,56},{72,6... | collective-permute-start | bytes 49160 | tf_op jit(solution)/shard_map/ppermute | solution.py:373
  133.1 1.0 copy-start.9
  148.4 15.2 %collective-permute-start.4 = (bf16[4,192,512]{2,1,0:T(8,128)(2,1)}, bf16[4,192,512]{2,1,0:T(8,128)(2,1)}, u32[]{:S(2)}, u32[]{:S(2)}) collective-permute-start(bf16[4,192,512]{2,1,0:T(8,128)(2,1)} %bitcast.5.own_ref), channel_id=1, source_target_pairs={{0,1},{1,0},{2,3},{3,2},{4,5},{5,4},{6,7},{7,6},{8,9},{9,8},{10,11... | collective-permute-start | bytes 2359304 | tf_op jit(solution)/shard_map/ppermute | solution.py:377
  158.1 1.0 copy-start.11
  159.1 1.0 copy-start.12
  160.1 1.0 copy-start.13
Sparse Core Ops, SparseCore 0:
  11.6 90.8 all-gather.4
  104.6 59.0 all-gather.6

commit v5 on v3

--- a/solution.py
+++ b/solution.py
@@ -342,7 +342,10 @@
     backward = [(i + 1, i) for i in range(seq_count - 1)]
     cores = [(0, 1), (1, 0)]
 
-    out_rows = lax.all_gather(w_out, SEQ, axis=0, tiled=True)
+    spread = jnp.broadcast_to(w_out[None], (lax.axis_size("y"),) + w_out.shape)
+    out_part = lax.all_to_all(spread, "y", 0, 0).reshape(-1, w_out.shape[1])
+    out_part, w_in = lax.optimization_barrier((out_part, w_in))
+    out_rows = lax.all_gather(out_part, "z", axis=0, tiled=True)
     in_part = lax.all_gather(w_in, "y", axis=0, tiled=True)
     in_rows = lax.all_gather(in_part, "z", axis=0, tiled=True)
     out_own = lax.all_gather(d_out, "x")

time: 184 us -> 174 us (0.946)
  waiting for transfers between devices: 54.4 us -> 24 us
  blocking collectives: 49 us -> 70.3 us
  local copies, waits for them, and re-layouts: 11.7 us -> 7.92 us
  starting transfers between devices: 36.8 us -> 40.2 us
    all_gather x1, waiting for transfers between devices: 24.4 us -> 0.73 us  [shards(): out_rows = lax.all_gather(out_part, 'z', axis=0, tiled=True)]
    all_to_all x0 -> x1, blocking collectives: none -> 22 us  [shards(): out_part = lax.all_to_all(spread, 'y', 0, 0).reshape(-1, w_out.shape[1])]
    all_gather x1, waiting for transfers between devices: 11.6 us -> 3.89 us  [shards(): in_rows = lax.all_gather(in_part, 'z', axis=0, tiled=True)]
    all_to_all x1, starting transfers between devices: 8.88 us -> 15.9 us  [shards(): carries = lax.all_to_all(carry, SEQ, 0, 0)]
    unnamed x42 -> x38, local copies, waits for them, and re-layouts: 11 us -> 6.86 us
    ppermute x1, starting transfers between devices: 14.1 us -> 11.4 us  [shards(): out_other = lax.ppermute(out_own, 'k', cores)]
    all_gather x1, blocking collectives: 11.8 us -> 13.7 us  [shards(): out_own = lax.all_gather(d_out, 'x')]
  transfers between devices with their start and end apart: 8 -> 8, of which waited for: 6 -> 6; matrix products, arithmetic and copies ran while one was open for 1% -> 0% of each run, Pallas kernels for 6% -> 6%
where the time goes in v5:
time: 174 us; the launch traced here: 173 us
  blocking collectives  70.3 us (40%)
  starting transfers between devices  40.2 us (23%)
  waiting for transfers between devices  24 us (14%)
  Pallas kernels  16.4 us (9%)
  between operations  14.3 us (8%)
  local copies, waits for them, and re-layouts  7.92 us (5%)
    all_gather x1, blocking collectives, shards(): in_part = lax.all_gather(w_in, 'y', axis=0, tiled=True)  22.3 us
    all_to_all x1, blocking collectives, shards(): out_part = lax.all_to_all(spread, 'y', 0, 0).reshape(-1, w_out.shape[1])  22 us
    all_to_all x1, starting transfers between devices, shards(): carries = lax.all_to_all(carry, SEQ, 0, 0)  15.9 us
    all_gather x1, blocking collectives, shards(): out_own = lax.all_gather(d_out, 'x')  13.7 us
    all_gather x1, blocking collectives, shards(): own = lax.all_gather(d_branch, 'x')  12.3 us
    ppermute x1, starting transfers between devices, shards(): out_other = lax.ppermute(out_own, 'k', cores)  11.4 us
    ppermute x1, waiting for transfers between devices, shards(): next_a = lax.ppermute(front_a, SEQ, backward)  9.68 us
    ppermute x1, starting transfers between devices, shards(): other = lax.ppermute(own, 'k', cores)  8.96 us
  transfers between devices with their start and end apart: 8, of which 6 were waited for; matrix products, arithmetic and copies ran while one was open for 0% of the time, Pallas kernels for 6%

profile of v5, /device:TPU:1, one launch (start us, length us, event | category | flops | bytes accessed | tf_op | source)
XLA Modules:
  0.0 173.2 jit_solution(527596160967482010)
XLA Ops:
  7.2 0.0 copy-start.13
  7.2 0.0 copy-start.18
  7.2 0.0 copy-start.16
  7.2 0.0 copy-start.7
  7.2 0.0 copy-start
  7.2 0.0 copy-start.14
  7.2 0.0 all-gather.5.cloned.1.call-start
  7.3 1.1 broadcast_in_dim.27
  8.3 22.0 %all_to_all.10 = bf16[8,8,4096]{2,1,0:T(8,128)(2,1)} all-to-all(bf16[8,8,4096]{2,1,0:T(8,128)(2,1)S(1)} %broadcast_in_dim.27), channel_id=1, replica_groups=mesh['z'=8,'y'=8,'x'=4,'k'=2] {'y'}, dimensions={0} | all-to-all | bytes 1048576 | tf_op jit(solution)/shard_map/all_to_all | solution.py:346
  30.3 0.0 all-gather.5.cloned.1.call-update
  30.4 0.0 all-gather.7.cloned.1.call-start
  30.4 22.3 %all_gather.24 = bf16[64,4096]{1,0:T(8,128)(2,1)} all-gather(bf16[8,4096]{1,0:T(8,128)(2,1)} %param.18), channel_id=1, replica_groups=mesh['z'=8,'y'=8,'x'=4,'k'=2] {'y'}, dimensions={0}, use_global_device_ids=true | all-gather | bytes 589824 | tf_op jit(solution)/shard_map/all_gather | solution.py:349
  52.7 0.0 all-gather.7.cloned.1.call-update
  52.7 13.7 %all-gather = bf16[768,512]{1,0:T(8,128)(2,1)S(1)} all-gather(bf16[192,512]{1,0:T(8,128)(2,1)} %param.10), channel_id=2, replica_groups=mesh['z'=8,'y'=8,'x'=4,'k'=2] {'x'}, dimensions={0}, use_global_device_ids=true | all-gather | bytes 983040 | tf_op jit(solution)/shard_map/all_gather | solution.py:351
  66.4 0.0 copy-start.17
  66.4 11.4 %collective-permute-start = (bf16[4,192,512]{2,1,0:T(8,128)(2,1)S(1)}, bf16[4,192,512]{2,1,0:T(8,128)(2,1)}, u32[]{:S(2)}, u32[]{:S(2)}) collective-permute-start(bf16[4,192,512]{2,1,0:T(8,128)(2,1)S(1)} %bitcast.10), channel_id=1, source_target_pairs={{0,1},{1,0},{2,3},{3,2},{4,5},{5,4},{6,7},{7,6},{8,9},{9,8},{10,11... | collective-permute-start | bytes 2359304 | tf_op jit(solution)/shard_map/ppermute | solution.py:352
  77.8 0.0 copy-done.13
  77.8 1.3 collective-permute-start.1
  79.2 0.0 copy-done.18
  79.2 0.1 select_reduce_fusion
  79.2 0.7 collective-permute-done.1.prev_ref
  80.0 0.0 copy-done.16
  80.0 0.0 copy-done.7
  80.0 0.0 copy-done
  80.0 0.0 copy-done.14
  80.0 2.4 %shard_map.129 = (f32[192,512]{1,0:T(8,128)S(1)}, f32[192,512]{1,0:T(8,128)S(1)}, f32[192,512]{1,0:T(8,128)S(1)}, f32[192,512]{1,0:T(8,128)S(1)}, f32[192,512]{1...) custom-call(bf16[192,512]{1,0:T(8,128)(2,1)S(1)} %copy-done.13, ...), custom_call_target="tpu_custom_call" | custom-call | tf_op jit(solution)/shard_map/pallas_call | solution.py:111
  82.4 0.0 copy-start.2
  82.4 0.7 copy-done.2
  83.1 0.0 copy-start.4
  83.1 0.7 copy-done.4
  83.9 0.0 copy-start.9
  83.9 0.8 copy-done.9
  84.6 0.0 copy-start.15
  84.6 0.6 copy-done.15
  85.2 1.3 collective-permute-start.2
  86.5 4.3 %collective-permute-done.2.front_b_ref = f32[8,512]{1,0:T(8,128)S(1)} collective-permute-done((f32[8,512]{1,0:T(8,128)S(1)}, f32[8,512]{1,0:T(8,128)S(1)}, u32[]{:S(2)}, u32[]{:S(2)}) %collective-permute-start.2) | collective-permute-done | bytes 16416 | tf_op jit(solution)/shard_map/ppermute | solution.py:361
  90.8 0.0 collective-permute-done.other_ref
  90.8 0.7 all-gather.5.cloned.1.call-done.w_ref
  91.5 0.0 copy-done.17
  91.5 0.0 copy-start.1
  91.5 0.0 copy-start.3
  91.5 0.0 copy-start.5
  91.5 0.0 copy-start.6
  91.5 6.9 %shard_map.130 = (f32[192,512]{1,0:T(8,128)}, f32[192,512]{1,0:T(8,128)}, f32[192,512]{1,0:T(8,128)}, f32[8,512]{1,0:T(8,128)}, f32[64,3,512]{2,1,0:T(4,128)}) custom-call(s32[1]{0:T(128)} %bitcast.core_ref, bf16[4,192,512]{2,1,0:T(8,128)(2,1)} %bitcast.11, bf16[4,192,512]{2,1,0:T(8,128)(2,1)} %collective-permute-done.other_ref, ...), custom_call_target="tpu_custom_call" | custom-call | tf_op jit(solution)/shard_map/pallas_call | solution.py:174
  98.4 15.9 %all-to-all-start.1 = ((f32[64,3,512]{2,1,0:T(4,128)}), f32[64,3,512]{2,1,0:T(4,128)S(1)}, u32[]{:S(2)}, u32[]{:S(2)}) async-start(f32[64,3,512]{2,1,0:T(4,128)} %get-tuple-element.34), calls=%async_computation.1 | async-start | bytes 1048576 | tf_op jit(solution)/shard_map/all_to_all | solution.py:368
  114.4 1.3 collective-permute-start.3
  115.7 9.7 %collective-permute-done.3.front_a_ref = f32[8,512]{1,0:T(8,128)S(1)} collective-permute-done((f32[8,512]{1,0:T(8,128)}, f32[8,512]{1,0:T(8,128)S(1)}, u32[]{:S(2)}, u32[]{:S(2)}) %collective-permute-start.3) | collective-permute-done | bytes 16416 | tf_op jit(solution)/shard_map/ppermute | solution.py:367
  125.4 4.7 %all-to-all-done.1.carry_ref = f32[64,3,512]{2,1,0:T(4,128)S(1)} async-done(((f32[64,3,512]{2,1,0:T(4,128)}), f32[64,3,512]{2,1,0:T(4,128)S(1)}, u32[]{:S(2)}, u32[]{:S(2)}) %all-to-all-start.1) | async-done | bytes 393248 | tf_op jit(solution)/shard_map/all_to_all | solution.py:368
  130.0 1.0 copy-done.8
  131.0 0.5 shard_map.131
  131.5 12.3 %all-gather.1 = bf16[768,512]{1,0:T(8,128)(2,1)} all-gather(bf16[192,512]{1,0:T(8,128)(2,1)S(1)} %get-tuple-element.39), channel_id=3, replica_groups=mesh['z'=8,'y'=8,'x'=4,'k'=2] {'x'}, dimensions={0}, use_global_device_ids=true | all-gather | bytes 983040 | tf_op jit(solution)/shard_map/all_gather | solution.py:370
  143.8 9.0 %collective-permute-start.4 = (bf16[4,192,512]{2,1,0:T(8,128)(2,1)}, bf16[4,192,512]{2,1,0:T(8,128)(2,1)}, u32[]{:S(2)}, u32[]{:S(2)}) collective-permute-start(bf16[4,192,512]{2,1,0:T(8,128)(2,1)} %bitcast.6.own_ref), channel_id=1, source_target_pairs={{0,1},{1,0},{2,3},{3,2},{4,5},{5,4},{6,7},{7,6},{8,9},{9,8},{10,11... | collective-permute-start | bytes 2359304 | tf_op jit(solution)/shard_map/ppermute | solution.py:371
  152.8 0.0 copy-done.1
  152.8 0.0 copy-done.3
  152.8 0.0 copy-done.5
  152.8 0.0 copy-done.6
  152.8 0.0 copy-start.10
  152.8 1.0 copy-done.10
  153.8 1.0 copy-done.11
  154.8 1.0 copy-done.12
  155.8 1.5 shard_map.133
  157.3 3.9 %all-gather.7.cloned.1.call-done.w_ref = bf16[512,4096]{1,0:T(8,128)(2,1)} async-done(((bf16[64,4096]{1,0:T(8,128)(2,1)}), bf16[512,4096]{1,0:T(8,128)(2,1)}) %all-gather.7.cloned.1.call-update) | async-done | bytes 4194320 | tf_op jit(solution)/shard_map/all_gather | solution.py:350
  161.2 0.0 collective-permute-done.4.other_ref
  161.2 5.2 %shard_map.132 = bf16[192,512]{1,0:T(8,128)(2,1)} custom-call(s32[1]{0:T(128)} %bitcast.core_ref, bf16[4,192,512]{2,1,0:T(8,128)(2,1)} %bitcast.6.own_ref, bf16[4,192,512]{2,1,0:T(8,128)(2,1)} %collective-permute-done.4.other_ref, bf16[512,4096]{1,0:T(8,128)(2,1)} %all-gather.7.cloned.1.call-done.w_ref), custom_call_target="tpu_custom_call" | custom-call | tf_op jit(solution)/shard_map/pallas_call | solution.py:309
  (5 shorter events, 0.0 us)
Async XLA Ops:
  7.2 70.7 %copy-start.13 = (bf16[192,512]{1,0:T(8,128)(2,1)S(1)}, bf16[192,512]{1,0:T(8,128)(2,1)}, u32[]{:S(2)}) copy-start(bf16[192,512]{1,0:T(8,128)(2,1)} %x_ref.1) | copy-start | bytes 589828
  7.2 72.0 %copy-start.18 = (s32[512]{0:T(512)S(1)}, s32[512]{0:T(512)}, u32[]{:S(2)}) copy-start(s32[512]{0:T(512)} %param.17) | copy-start | bytes 6148
  7.2 72.8 %copy-start.16 = (f32[512]{0:T(512)S(1)}, f32[512]{0:T(512)}, u32[]{:S(2)}) copy-start(f32[512]{0:T(512)} %param.16) | copy-start | bytes 6148
  7.2 72.8 %copy-start.7 = (bf16[192,512]{1,0:T(8,128)(2,1)S(1)}, bf16[192,512]{1,0:T(8,128)(2,1)}, u32[]{:S(2)}) copy-start(bf16[192,512]{1,0:T(8,128)(2,1)} %rec_ref.3) | copy-start | bytes 589828
  7.2 72.8 %copy-start = (bf16[192,512]{1,0:T(8,128)(2,1)S(1)}, bf16[192,512]{1,0:T(8,128)(2,1)}, u32[]{:S(2)}) copy-start(bf16[192,512]{1,0:T(8,128)(2,1)} %inw_ref.5) | copy-start | bytes 589828
  7.2 72.8 %copy-start.14 = (f32[4,512]{1,0:T(4,128)S(1)}, f32[4,512]{1,0:T(4,128)}, u32[]{:S(2)}) copy-start(f32[4,512]{1,0:T(4,128)} %cw_ref.3) | copy-start | bytes 24580
  7.2 84.3 %all-gather.5.cloned.1.call-start = ((), (), s32[]{:S(2)}) async-start(), calls=%async_computation.2 | async-start | bytes 4718592 | tf_op jit(solution)/shard_map/all_gather | solution.py:348
  30.4 130.8 %all-gather.7.cloned.1.call-start = ((), (), s32[]{:S(2)}) async-start(), calls=%async_computation.3 | async-start | bytes 4718592 | tf_op jit(solution)/shard_map/all_gather | solution.py:350
  66.4 25.1 %copy-start.17 = (bf16[768,512]{1,0:T(8,128)(2,1)}, bf16[768,512]{1,0:T(8,128)(2,1)S(1)}, u32[]{:S(2)}) copy-start(bf16[768,512]{1,0:T(8,128)(2,1)S(1)} %all-gather) | copy-start | bytes 2359300
  66.4 24.3 %collective-permute-start = (bf16[4,192,512]{2,1,0:T(8,128)(2,1)S(1)}, bf16[4,192,512]{2,1,0:T(8,128)(2,1)}, u32[]{:S(2)}, u32[]{:S(2)}) collective-permute-start(bf16[4,192,512]{2,1,0:T(8,128)(2,1)S(1)} %bitcast.10), channel_id=1, source_target_pairs={{0,1},{1,0},{2,3},{3,2},{4,5},{5,4},{6,7},{7,6},{8,9},{9,8},{10,11... | collective-permute-start | bytes 2359304 | tf_op jit(solution)/shard_map/ppermute | solution.py:352
  77.8 2.1 %collective-permute-start.1 = (bf16[16,512]{1,0:T(8,128)(2,1)S(1)}, bf16[16,512]{1,0:T(8,128)(2,1)S(1)}, u32[]{:S(2)}, u32[]{:S(2)}) collective-permute-start(bf16[16,512]{1,0:T(8,128)(2,1)S(1)} %slice.3), channel_id=1, source_target_pairs={{0,8},{8,16},{16,24},{24,32},{32,40},{40,48},{48,56},{56,64},{64,7... | collective-permute-start | bytes 49160 | tf_op jit(solution)/shard_map/ppermute | solution.py:353
  82.4 0.7 copy-start.2
  83.1 0.7 copy-start.4
  83.9 0.8 copy-start.9
  84.6 0.6 copy-start.15
  85.2 5.5 %collective-permute-start.2 = (f32[8,512]{1,0:T(8,128)S(1)}, f32[8,512]{1,0:T(8,128)S(1)}, u32[]{:S(2)}, u32[]{:S(2)}) collective-permute-start(f32[8,512]{1,0:T(8,128)S(1)} %get-tuple-element.31), channel_id=1, source_target_pairs={{8,0},{16,8},{24,16},{32,24},{40,32},{48,40},{56,48},{64,56},{72,6... | collective-permute-start | bytes 49160 | tf_op jit(solution)/shard_map/ppermute | solution.py:361
  91.5 61.3 %copy-start.1 = (bf16[192,512]{1,0:T(8,128)(2,1)S(1)}, bf16[192,512]{1,0:T(8,128)(2,1)}, u32[]{:S(2)}) copy-start(bf16[192,512]{1,0:T(8,128)(2,1)} %inw_ref.5) | copy-start | bytes 589828
  91.5 61.3 %copy-start.3 = (f32[192,512]{1,0:T(8,128)S(1)}, f32[192,512]{1,0:T(8,128)}, u32[]{:S(2)}) copy-start(f32[192,512]{1,0:T(8,128)} %copy-done.2) | copy-start | bytes 1179652
  91.5 61.3 %copy-start.5 = (f32[192,512]{1,0:T(8,128)S(1)}, f32[192,512]{1,0:T(8,128)}, u32[]{:S(2)}) copy-start(f32[192,512]{1,0:T(8,128)} %copy-done.4) | copy-start | bytes 1179652
  91.5 61.3 %copy-start.6 = (bf16[192,512]{1,0:T(8,128)(2,1)S(1)}, bf16[192,512]{1,0:T(8,128)(2,1)}, u32[]{:S(2)}) copy-start(bf16[192,512]{1,0:T(8,128)(2,1)} %gate_ref.3) | copy-start | bytes 589828
  98.4 31.6 %all-to-all-start.1 = ((f32[64,3,512]{2,1,0:T(4,128)}), f32[64,3,512]{2,1,0:T(4,128)S(1)}, u32[]{:S(2)}, u32[]{:S(2)}) async-start(f32[64,3,512]{2,1,0:T(4,128)} %get-tuple-element.34), calls=%async_computation.1 | async-start | bytes 1048576 | tf_op jit(solution)/shard_map/all_to_all | solution.py:368
  114.4 11.0 %collective-permute-start.3 = (f32[8,512]{1,0:T(8,128)}, f32[8,512]{1,0:T(8,128)S(1)}, u32[]{:S(2)}, u32[]{:S(2)}) collective-permute-start(f32[8,512]{1,0:T(8,128)} %get-tuple-element.37), channel_id=1, source_target_pairs={{8,0},{16,8},{24,16},{32,24},{40,32},{48,40},{56,48},{64,56},{72,6... | collective-permute-start | bytes 49160 | tf_op jit(solution)/shard_map/ppermute | solution.py:367
  130.0 1.0 copy-start.8
  143.8 17.4 %collective-permute-start.4 = (bf16[4,192,512]{2,1,0:T(8,128)(2,1)}, bf16[4,192,512]{2,1,0:T(8,128)(2,1)}, u32[]{:S(2)}, u32[]{:S(2)}) collective-permute-start(bf16[4,192,512]{2,1,0:T(8,128)(2,1)} %bitcast.6.own_ref), channel_id=1, source_target_pairs={{0,1},{1,0},{2,3},{3,2},{4,5},{5,4},{6,7},{7,6},{8,9},{9,8},{10,11... | collective-permute-start | bytes 2359304 | tf_op jit(solution)/shard_map/ppermute | solution.py:371
  152.8 1.0 copy-start.10
  153.8 1.0 copy-start.11
  154.8 1.0 copy-start.12
Sparse Core Ops, SparseCore 0:
  30.5 60.9 all-gather.4
  93.6 67.5 all-gather.6

commit v6 on v4

--- a/solution.py
+++ b/solution.py
@@ -1,3 +1,5 @@
+import functools
+
 import jax
 import jax.numpy as jnp
 from jax import lax
@@ -94,7 +96,8 @@
     beta_ref[...] = beta
     conv_ref[...] = conv
     prod, state = local_scan(decay, beta * (inward * conv), False, cum_ref, local_ref)
-    ends_ref[...] = jnp.concatenate([prod, state], axis=0)
+    ends = jnp.concatenate([prod, state], axis=0)
+    ends_ref[...] = jnp.broadcast_to(ends[None], ends_ref.shape)
     local_scan(decay, jnp.zeros_like(decay), True, scan_a, scan_b)
     post = shift_up(scan_a[...], 1.0)
     post_ref[...] = post
@@ -104,7 +107,7 @@
 
 
 def before(
-    x_branch, prev, recurrence_gate, input_gate, conv_weight, conv_bias, log_decay
+    x_branch, prev, recurrence_gate, input_gate, conv_weight, conv_bias, log_decay, seq_count
 ):
     rows, width = x_branch.shape
     full = jax.ShapeDtypeStruct((rows, width), F32)
@@ -112,7 +115,7 @@
         before_kernel,
         out_shape=(full,) * 7
         + (
-            jax.ShapeDtypeStruct((2, width), F32),
+            jax.ShapeDtypeStruct((seq_count, 2, width), F32),
             jax.ShapeDtypeStruct((SUB, width), F32),
         ),
         scratch_shapes=[
@@ -125,8 +128,8 @@
 
 
 def adjoint_kernel(
-    core_ref, own_ref, other_ref, w_ref, gate_ref, decay_ref, beta_ref, inw_ref, ends_ref,
-    dlru_ref, adj_ref, offset_ref, front_ref, carry_ref,
+    core_ref, own_ref, other_ref, w_ref, gate_ref, decay_ref, beta_ref, inw_ref,
+    dlru_ref, adj_ref, offset_ref, front_ref, edge_ref,
     acc, scan_a, scan_b,
 ):
     step = pl.program_id(0)
@@ -162,11 +165,10 @@
         offset = adj * beta_ref[...] * sigmoid(inw_ref[...].astype(F32))
         offset_ref[...] = offset
         front_ref[...] = offset[:SUB]
-        mine = jnp.concatenate([ends_ref[...], first], axis=0)
-        carry_ref[...] = jnp.broadcast_to(mine[None], carry_ref.shape)
-
-
-def adjoint(core, own, other, weights, gate, decay, beta, input_gate, ends, seq_count):
+        edge_ref[...] = jnp.broadcast_to(first[None], edge_ref.shape)
+
+
+def adjoint(core, own, other, weights, gate, decay, beta, input_gate, seq_count):
     rows, width = gate.shape
     steps = own.shape[0]
     full = jax.ShapeDtypeStruct((rows, width), F32)
@@ -183,29 +185,28 @@
             whole((rows, width)),
             whole((rows, width)),
             whole((rows, width)),
-            whole((2, width)),
         ],
         out_specs=[
             whole((rows, width)),
             whole((rows, width)),
             whole((rows, width)),
             whole((SUB, width)),
-            whole((seq_count, 3, width)),
+            whole((seq_count, 1, width)),
         ],
         out_shape=(
             full,
             full,
             full,
             jax.ShapeDtypeStruct((SUB, width), F32),
-            jax.ShapeDtypeStruct((seq_count, 3, width), F32),
+            jax.ShapeDtypeStruct((seq_count, 1, width), F32),
         ),
         scratch_shapes=[pltpu.VMEM((rows, width), F32)] * 3,
         compiler_params=pltpu.CompilerParams(vmem_limit_bytes=VMEM_WHOLE),
-    )(core, own, other, weights, gate, decay, beta, input_gate, ends)
+    )(core, own, other, weights, gate, decay, beta, input_gate)
 
 
 def branch_kernel(
-    place_ref, carry_ref, offset_ref, slope_ref, cw_ref, front_a_ref, front_b_ref,
+    place_ref, ends_ref, edge_ref, offset_ref, slope_ref, cw_ref, front_a_ref, front_b_ref,
     branch_ref, kappa_ref,
     padded,
 ):
@@ -213,8 +214,8 @@
     place = place_ref[0]
     beyond = jnp.zeros((1, width), F32)
     kappa = jnp.zeros((1, width), F32)
-    for i in reversed(range(1, carry_ref.shape[0])):
-        here = carry_ref[i, 2:3] + carry_ref[i, 0:1] * kappa
+    for i in reversed(range(1, ends_ref.shape[0])):
+        here = edge_ref[i] + ends_ref[i, 0:1] * kappa
         beyond = jnp.where(i == place + 1, kappa, beyond)
         kappa = jnp.where(i > place, here, kappa)
     padded[pl.ds(0, rows), :] = offset_ref[...] + slope_ref[...] * kappa
@@ -226,19 +227,19 @@
     kappa_ref[...] = kappa
 
 
-def branch(place, carry, offset, slope, conv_weight, front_a, front_b):
+def branch(place, ends, edges, offset, slope, conv_weight, front_a, front_b):
     rows, width = offset.shape
     vmem = pl.BlockSpec(memory_space=pltpu.VMEM)
     return pl.pallas_call(
         branch_kernel,
-        in_specs=[pl.BlockSpec(memory_space=pltpu.SMEM)] + [vmem] * 6,
+        in_specs=[pl.BlockSpec(memory_space=pltpu.SMEM)] + [vmem] * 7,
         out_shape=(
             jax.ShapeDtypeStruct((rows, width), BF16),
             jax.ShapeDtypeStruct((1, width), F32),
         ),
         scratch_shapes=[pltpu.VMEM((rows + SUB, width), F32)],
         compiler_params=pltpu.CompilerParams(vmem_limit_bytes=VMEM_LIMIT),
-    )(place, carry, offset, slope, conv_weight, front_a, front_b)
+    )(place, ends, edges, offset, slope, conv_weight, front_a, front_b)
 
 
 def gates_kernel(
@@ -277,9 +278,13 @@
     )(place, carry, kappa, d_lru, *arrays)
 
 
-def input_kernel(core_ref, own_ref, other_ref, first_ref, rest_ref, out_ref, acc):
+def input_kernel(lead, core_ref, own_ref, other_ref, first_ref, rest_ref, out_ref, acc):
     step = pl.program_id(0)
     half = first_ref.shape[1] // 2
+
+    @pl.when(step == 0)
+    def _():
+        acc[...] = jnp.zeros_like(acc)
 
     def product(left, right, w_ref):
         dims = (((1,), (1,)), ((), ()))
@@ -288,11 +293,11 @@
         ) + lax.dot_general(right, w_ref[:, half:], dims, preferred_element_type=F32)
 
     def add(left, right):
-        @pl.when(step == 0)
+        @pl.when(step < lead)
         def _():
-            acc[...] = product(left[0], right[0], first_ref)
-
-        @pl.when(step != 0)
+            acc[...] += product(left[0], right[0], first_ref)
+
+        @pl.when(step >= lead)
         def _():
             acc[...] += product(left[0], right[0], rest_ref)
 
@@ -312,16 +317,17 @@
 def input_grad(core, own, other, first, rest):
     steps, rows, width = own.shape
     feats = first.shape[0]
-    at = first.shape[1] // (2 * width) - 1
+    lead = steps - rest.shape[1] // (2 * width)
+    at = first.shape[1] // (2 * width) - lead
     return pl.pallas_call(
-        input_kernel,
+        functools.partial(input_kernel, lead),
         grid=(steps,),
         in_specs=[
             pl.BlockSpec(memory_space=pltpu.SMEM),
             pl.BlockSpec((1, rows, width), lambda i: (i, 0, 0)),
             pl.BlockSpec((1, rows, width), lambda i: (i, 0, 0)),
-            pl.BlockSpec((feats, 2 * width), lambda i: (0, at)),
-            pl.BlockSpec((feats, 2 * width), lambda i: (0, jnp.maximum(i - 1, 0))),
+            pl.BlockSpec((feats, 2 * width), lambda i: (0, at + jnp.minimum(i, lead - 1))),
+            pl.BlockSpec((feats, 2 * width), lambda i: (0, jnp.maximum(i - lead, 0))),
         ],
         out_specs=pl.BlockSpec((rows, feats), lambda i: (0, 0)),
         out_shape=jax.ShapeDtypeStruct((rows, feats), BF16),
@@ -350,9 +356,10 @@
     backward = [(i + 1, i) for i in range(seq_count - 1)]
     cores = [(0, 1), (1, 0)]
 
-    first = jnp.concatenate([w_out, w_in[:, : 2 * width]], axis=1)
+    half = w_in.shape[1] // 2
+    first = jnp.concatenate([w_out, w_in[:, :half]], axis=1)
     first = lax.all_gather(first, SEQ, axis=0, tiled=True)
-    rest = lax.all_gather(w_in[:, 2 * width :], "y", axis=0, tiled=True)
+    rest = lax.all_gather(w_in[:, half:], "y", axis=0, tiled=True)
     in_rows = lax.all_gather(rest, "z", axis=0, tiled=True)
     out_own = lax.all_gather(d_out, "x")
     out_other = lax.ppermute(out_own, "k", cores)
@@ -361,22 +368,24 @@
     onehot = decay_level[:, None] == jnp.arange(LEVELS)[None, :]
     log_decay = jnp.sum(jnp.where(onehot, log_table[None, :], 0.0), axis=1)[None, :]
     decay, beta, conv_out, cum_decay, local_states, post, slope, ends, front_b = before(
-        x_branch, prev, recurrence_gate, input_gate, conv_weight, conv_bias[None, :], log_decay
+        x_branch, prev, recurrence_gate, input_gate, conv_weight, conv_bias[None, :], log_decay,
+        seq_count,
     )
 
     next_b = lax.ppermute(front_b, SEQ, backward)
 
-    ends, next_b = lax.optimization_barrier((ends, next_b))
-    d_lru, adj_local, offset, front_a, carry = adjoint(
-        core, out_own, out_other, first, gate_branch, decay, beta, input_gate, ends, seq_count
+    all_ends = lax.all_to_all(ends, SEQ, 0, 0)
+    decay, all_ends, next_b = lax.optimization_barrier((decay, all_ends, next_b))
+    d_lru, adj_local, offset, front_a, edge = adjoint(
+        core, out_own, out_other, first, gate_branch, decay, beta, input_gate, seq_count
     )
     next_a = lax.ppermute(front_a, SEQ, backward)
-    carries = lax.all_to_all(carry, SEQ, 0, 0)
-    d_branch, kappa = branch(place, carries, offset, slope, conv_weight, next_a, next_b)
+    edges = lax.all_to_all(edge, SEQ, 0, 0)
+    d_branch, kappa = branch(place, all_ends, edges, offset, slope, conv_weight, next_a, next_b)
     own = lax.all_gather(d_branch, "x")
     other = lax.ppermute(own, "k", cores)
     d_gate, d_recurrence_gate, d_input_gate = gates(
-        place, carries, kappa, d_lru, adj_local, post, cum_decay, local_states, decay,
+        place, all_ends, kappa, d_lru, adj_local, post, cum_decay, local_states, decay,
         beta, conv_out, gate_branch, recurrence_gate, input_gate, log_decay,
     )
     d_input = input_grad(core, own, other, first, in_rows)

time: 177 us -> 180 us (1.017)
  starting transfers between devices: 37 us -> 49.9 us
  waiting for transfers between devices: 44.1 us -> 33.2 us
    all_gather x1, waiting for transfers between devices: 25.1 us -> 8.29 us  [shards(): first = lax.all_gather(first, SEQ, axis=0, tiled=True)]
    all_to_all x1 -> x2, starting transfers between devices: 8.75 us -> 25.6 us  [the longest x1 16.1 us: shards(): all_ends = lax.all_to_all(ends, SEQ, 0, 0)]
    all_to_all x1 -> x2, waiting for transfers between devices: 4.92 us -> 12.1 us  [the longest x1 6.21 us: shards(): edges = lax.all_to_all(edge, SEQ, 0, 0)]
    ppermute x1, waiting for transfers between devices: 8.63 us -> 4.13 us  [shards(): next_a = lax.ppermute(front_a, SEQ, backward)]
    ppermute x1, waiting for transfers between devices: 4.17 us -> 8.66 us  [shards(): next_b = lax.ppermute(front_b, SEQ, backward)]
    ppermute x1, starting transfers between devices: 9.57 us -> 6.23 us  [shards(): other = lax.ppermute(own, 'k', cores)]
    unnamed x42 -> x40, local copies, waits for them, and re-layouts: 11 us -> 12.2 us
  transfers between devices with their start and end apart: 8 -> 9, of which waited for: 6 -> 6; matrix products, arithmetic and copies ran while one was open for 1% -> 1% of each run, Pallas kernels for 6% -> 6%
where the time goes in v6:
time: 180 us; the launch traced here: 179 us
  starting transfers between devices  49.9 us (28%)
  blocking collectives  48.7 us (27%)
  waiting for transfers between devices  33.2 us (18%)
  Pallas kernels  17 us (9%)
  between operations  14.2 us (8%)
  local copies, waits for them, and re-layouts  13.7 us (8%)
  other arithmetic  2.27 us (1%)
    all_gather x1, blocking collectives, shards(): rest = lax.all_gather(w_in[:, half:], 'y', axis=0, tiled=True)  22.9 us
    all_to_all x1, starting transfers between devices, shards(): all_ends = lax.all_to_all(ends, SEQ, 0, 0)  16.1 us
    ppermute x1, starting transfers between devices, shards(): out_other = lax.ppermute(out_own, 'k', cores)  14.1 us
    all_gather x1, blocking collectives, shards(): own = lax.all_gather(d_branch, 'x')  13.1 us
    all_gather x1, blocking collectives, shards(): out_own = lax.all_gather(d_out, 'x')  12.8 us
    unnamed x40, local copies, waits for them, and re-layouts  12.2 us
    all_to_all x1, starting transfers between devices, shards(): edges = lax.all_to_all(edge, SEQ, 0, 0)  9.42 us
    ppermute x1, waiting for transfers between devices, shards(): next_b = lax.ppermute(front_b, SEQ, backward)  8.66 us
  transfers between devices with their start and end apart: 9, of which 6 were waited for; matrix products, arithmetic and copies ran while one was open for 1% of the time, Pallas kernels for 6%

profile of v6, /device:TPU:1, one launch (start us, length us, event | category | flops | bytes accessed | tf_op | source)
XLA Modules:
  0.0 179.0 jit_solution(3673112595225646302)
XLA Ops:
  7.2 0.0 copy-start.18
  7.2 0.0 all-gather.5.cloned.1.call-start
  7.2 0.8 fusion.1
  8.0 1.5 pad_maximum_fusion
  9.5 0.0 all-gather.5.cloned.1.call-update
  9.5 0.0 all-gather.7.cloned.1.call-start
  9.6 22.9 %all_gather.26 = bf16[64,2048]{1,0:T(8,128)(2,1)} all-gather(bf16[8,2048]{1,0:T(8,128)(2,1)S(1)} %get-tuple-element.48), channel_id=1, replica_groups=mesh['z'=8,'y'=8,'x'=4,'k'=2] {'y'}, dimensions={0}, use_global_device_ids=true | all-gather | bytes 294912 | tf_op jit(solution)/shard_map/all_gather | solution.py:362
  32.5 0.0 all-gather.7.cloned.1.call-update
  32.5 12.8 %all-gather = bf16[768,512]{1,0:T(8,128)(2,1)} all-gather(bf16[192,512]{1,0:T(8,128)(2,1)} %param.10), channel_id=2, replica_groups=mesh['z'=8,'y'=8,'x'=4,'k'=2] {'x'}, dimensions={0}, use_global_device_ids=true | all-gather | bytes 983040 | tf_op jit(solution)/shard_map/all_gather | solution.py:364
  45.3 14.1 %collective-permute-start.2 = (bf16[4,192,512]{2,1,0:T(8,128)(2,1)}, bf16[4,192,512]{2,1,0:T(8,128)(2,1)}, u32[]{:S(2)}, u32[]{:S(2)}) collective-permute-start(bf16[4,192,512]{2,1,0:T(8,128)(2,1)} %bitcast.4.own_ref), channel_id=1, source_target_pairs={{0,1},{1,0},{2,3},{3,2},{4,5},{5,4},{6,7},{7,6},{8,9},{9,8},{10,11... | collective-permute-start | bytes 2359304 | tf_op jit(solution)/shard_map/ppermute | solution.py:365
  59.4 0.7 slice.9
  60.2 1.3 collective-permute-start
  61.5 0.8 select_reduce_fusion
  62.2 0.1 collective-permute-done.prev_ref
  62.3 0.0 copy-start
  62.3 0.9 copy-done
  63.2 0.0 copy-start.6
  63.2 0.9 copy-done.6
  64.2 0.9 copy-done.16
  65.1 0.0 copy-start.17
  65.1 0.7 copy-done.17
  65.8 0.0 copy-start.19
  65.8 0.7 copy-done.19
  66.5 0.0 copy-start.1
  66.5 0.0 copy-start.7
  66.5 0.0 copy-start.8
  66.5 2.8 %shard_map.129 = (f32[192,512]{1,0:T(8,128)S(1)}, f32[192,512]{1,0:T(8,128)S(1)}, f32[192,512]{1,0:T(8,128)S(1)}, f32[192,512]{1,0:T(8,128)S(1)}, f32[192,512]{1...) custom-call(bf16[192,512]{1,0:T(8,128)(2,1)S(1)} %copy-done.16, ...), custom_call_target="tpu_custom_call" | custom-call | tf_op jit(solution)/shard_map/pallas_call | solution.py:114
  69.3 0.0 copy-start.2
  69.3 0.8 copy-done.2
  70.1 0.0 copy-start.4
  70.1 0.8 copy-done.4
  70.8 0.0 copy-start.9
  70.8 0.7 copy-done.9
  71.6 0.0 copy-start.13
  71.6 0.8 copy-done.13
  72.3 16.1 %all-to-all-start = ((f32[64,2,512]{2,1,0:T(2,128)}), f32[64,2,512]{2,1,0:T(2,128)S(1)}, u32[]{:S(2)}, u32[]{:S(2)}) async-start(f32[64,2,512]{2,1,0:T(2,128)} %get-tuple-element.27), calls=%async_computation | async-start | bytes 524288 | tf_op jit(solution)/shard_map/all_to_all | solution.py:377
  88.5 1.3 collective-permute-start.1
  89.8 8.7 %collective-permute-done.1.front_b_ref = f32[8,512]{1,0:T(8,128)S(1)} collective-permute-done((f32[8,512]{1,0:T(8,128)S(1)}, f32[8,512]{1,0:T(8,128)S(1)}, u32[]{:S(2)}, u32[]{:S(2)}) %collective-permute-start.1) | collective-permute-done | bytes 16416 | tf_op jit(solution)/shard_map/ppermute | solution.py:375
  98.5 5.8 %all-to-all-done.ends_ref.carry_ref = f32[64,2,512]{2,1,0:T(2,128)S(1)} async-done(((f32[64,2,512]{2,1,0:T(2,128)}), f32[64,2,512]{2,1,0:T(2,128)S(1)}, u32[]{:S(2)}, u32[]{:S(2)}) %all-to-all-start) | async-done | bytes 262176 | tf_op jit(solution)/shard_map/all_to_all | solution.py:377
  104.3 0.0 collective-permute-done.2.other_ref
  104.3 8.3 %all-gather.5.cloned.1.call-done.w_ref.first_ref = bf16[512,6144]{1,0:T(8,128)(2,1)} async-done(((bf16[8,6144]{1,0:T(8,128)(2,1)}), bf16[512,6144]{1,0:T(8,128)(2,1)}) %all-gather.5.cloned.1.call-update) | async-done | bytes 6291472 | tf_op jit(solution)/shard_map/all_gather | solution.py:361
  112.6 6.6 %shard_map.130 = (f32[192,512]{1,0:T(8,128)}, f32[192,512]{1,0:T(8,128)}, f32[192,512]{1,0:T(8,128)}, f32[8,512]{1,0:T(8,128)}, f32[64,1,512]{2,1,0:T(1,128)}) custom-call(s32[1]{0:T(128)} %bitcast.core_ref, bf16[4,192,512]{2,1,0:T(8,128)(2,1)} %bitcast.4.own_ref, bf16[4,192,512]{2,1,0:T(8,128)(2,1)} %collective-permute-done.2.other_ref, ...), custom_call_target="tpu_custom_call" | custom-call | tf_op jit(solution)/shard_map/pallas_call | solution.py:176
  119.2 9.4 %all-to-all-start.1 = ((f32[64,1,512]{2,1,0:T(1,128)}), f32[64,1,512]{2,1,0:T(1,128)S(1)}, u32[]{:S(2)}, u32[]{:S(2)}) async-start(f32[64,1,512]{2,1,0:T(1,128)} %get-tuple-element.32), calls=%async_computation.1 | async-start | bytes 262144 | tf_op jit(solution)/shard_map/all_to_all | solution.py:383
  128.6 1.3 collective-permute-start.3
  129.9 4.1 %collective-permute-done.3.front_a_ref = f32[8,512]{1,0:T(8,128)S(1)} collective-permute-done((f32[8,512]{1,0:T(8,128)}, f32[8,512]{1,0:T(8,128)S(1)}, u32[]{:S(2)}, u32[]{:S(2)}) %collective-permute-start.3) | collective-permute-done | bytes 16416 | tf_op jit(solution)/shard_map/ppermute | solution.py:382
  134.0 6.2 %all-to-all-done.1.edge_ref = f32[64,1,512]{2,1,0:T(1,128)S(1)} async-done(((f32[64,1,512]{2,1,0:T(1,128)}), f32[64,1,512]{2,1,0:T(1,128)S(1)}, u32[]{:S(2)}, u32[]{:S(2)}) %all-to-all-start.1) | async-done | bytes 131104 | tf_op jit(solution)/shard_map/all_to_all | solution.py:383
  140.2 0.0 copy-done.18
  140.2 1.0 copy-done.14
  141.2 1.0 copy-done.15
  142.2 0.5 shard_map.131
  142.8 13.1 %all-gather.1 = bf16[768,512]{1,0:T(8,128)(2,1)} all-gather(bf16[192,512]{1,0:T(8,128)(2,1)S(1)} %get-tuple-element.37), channel_id=3, replica_groups=mesh['z'=8,'y'=8,'x'=4,'k'=2] {'x'}, dimensions={0}, use_global_device_ids=true | all-gather | bytes 983040 | tf_op jit(solution)/shard_map/all_gather | solution.py:385
  155.8 6.2 %collective-permute-start.4 = (bf16[4,192,512]{2,1,0:T(8,128)(2,1)}, bf16[4,192,512]{2,1,0:T(8,128)(2,1)}, u32[]{:S(2)}, u32[]{:S(2)}) collective-permute-start(bf16[4,192,512]{2,1,0:T(8,128)(2,1)} %bitcast.5.own_ref), channel_id=1, source_target_pairs={{0,1},{1,0},{2,3},{3,2},{4,5},{5,4},{6,7},{7,6},{8,9},{9,8},{10,11... | collective-permute-start | bytes 2359304 | tf_op jit(solution)/shard_map/ppermute | solution.py:386
  162.0 0.0 copy-done.1
  162.1 0.0 copy-done.7
  162.1 0.0 copy-done.8
  162.1 0.0 copy-done.3
  162.1 0.0 copy-done.5
  162.1 0.0 copy-start.10
  162.1 1.0 copy-done.10
  163.1 1.0 copy-done.11
  164.1 1.0 copy-done.12
  165.1 1.5 shard_map.133
  166.6 0.0 collective-permute-done.4.other_ref
  166.6 5.5 %shard_map.132 = bf16[192,512]{1,0:T(8,128)(2,1)} custom-call(s32[1]{0:T(128)} %bitcast.core_ref, bf16[4,192,512]{2,1,0:T(8,128)(2,1)} %bitcast.5.own_ref, bf16[4,192,512]{2,1,0:T(8,128)(2,1)} %collective-permute-done.4.other_ref, bf16[512,6144]{1,0:T(8,128)(2,1)} %all-gather.5.cloned.1.call-done.w_ref.first_ref, ...), custom_call_target="tpu_custom_call" | custom-call | tf_op jit(solution)/shard_map/pallas_call | solution.py:322
  (9 shorter events, 0.0 us)
Async XLA Ops:
  7.2 133.1 %copy-start.18 = (f32[4,512]{1,0:T(4,128)S(1)}, f32[4,512]{1,0:T(4,128)}, u32[]{:S(2)}) copy-start(f32[4,512]{1,0:T(4,128)} %cw_ref.3) | copy-start | bytes 24580
  7.2 105.4 %all-gather.5.cloned.1.call-start = ((), (), s32[]{:S(2)}) async-start(), calls=%async_computation.2 | async-start | bytes 6389760 | tf_op jit(solution)/shard_map/all_gather | solution.py:361
  9.5 157.1 %all-gather.7.cloned.1.call-start = ((), (), s32[]{:S(2)}) async-start(), calls=%async_computation.3 | async-start | bytes 2359296 | tf_op jit(solution)/shard_map/all_gather | solution.py:363
  45.3 59.0 %collective-permute-start.2 = (bf16[4,192,512]{2,1,0:T(8,128)(2,1)}, bf16[4,192,512]{2,1,0:T(8,128)(2,1)}, u32[]{:S(2)}, u32[]{:S(2)}) collective-permute-start(bf16[4,192,512]{2,1,0:T(8,128)(2,1)} %bitcast.4.own_ref), channel_id=1, source_target_pairs={{0,1},{1,0},{2,3},{3,2},{4,5},{5,4},{6,7},{7,6},{8,9},{9,8},{10,11... | collective-permute-start | bytes 2359304 | tf_op jit(solution)/shard_map/ppermute | solution.py:365
  60.2 2.1 %collective-permute-start = (bf16[16,512]{1,0:T(8,128)(2,1)S(1)}, bf16[16,512]{1,0:T(8,128)(2,1)S(1)}, u32[]{:S(2)}, u32[]{:S(2)}) collective-permute-start(bf16[16,512]{1,0:T(8,128)(2,1)S(1)} %slice.9), channel_id=1, source_target_pairs={{0,8},{8,16},{16,24},{24,32},{32,40},{40,48},{48,56},{56,64},{64,7... | collective-permute-start | bytes 49160 | tf_op jit(solution)/shard_map/ppermute | solution.py:366
  62.3 0.9 copy-start
  63.2 0.9 copy-start.6
  64.1 0.9 copy-start.16
  65.1 0.7 copy-start.17
  65.8 0.7 copy-start.19
  66.5 95.6 %copy-start.1 = (bf16[192,512]{1,0:T(8,128)(2,1)S(1)}, bf16[192,512]{1,0:T(8,128)(2,1)}, u32[]{:S(2)}) copy-start(bf16[192,512]{1,0:T(8,128)(2,1)} %inw_ref.5) | copy-start | bytes 589828
  66.5 95.6 %copy-start.7 = (bf16[192,512]{1,0:T(8,128)(2,1)S(1)}, bf16[192,512]{1,0:T(8,128)(2,1)}, u32[]{:S(2)}) copy-start(bf16[192,512]{1,0:T(8,128)(2,1)} %rec_ref.3) | copy-start | bytes 589828
  66.5 95.6 %copy-start.8 = (bf16[192,512]{1,0:T(8,128)(2,1)S(1)}, bf16[192,512]{1,0:T(8,128)(2,1)}, u32[]{:S(2)}) copy-start(bf16[192,512]{1,0:T(8,128)(2,1)} %gate_ref.3) | copy-start | bytes 589828
  69.3 0.8 copy-start.2
  70.1 0.8 copy-start.4
  70.8 0.7 copy-start.9
  71.6 0.8 copy-start.13
  72.3 89.7 %copy-start.3 = (f32[192,512]{1,0:T(8,128)S(1)}, f32[192,512]{1,0:T(8,128)}, u32[]{:S(2)}) copy-start(f32[192,512]{1,0:T(8,128)} %copy-done.2) | copy-start | bytes 1179652
  72.3 89.7 %copy-start.5 = (f32[192,512]{1,0:T(8,128)S(1)}, f32[192,512]{1,0:T(8,128)}, u32[]{:S(2)}) copy-start(f32[192,512]{1,0:T(8,128)} %copy-done.4) | copy-start | bytes 1179652
  72.3 32.0 %all-to-all-start = ((f32[64,2,512]{2,1,0:T(2,128)}), f32[64,2,512]{2,1,0:T(2,128)S(1)}, u32[]{:S(2)}, u32[]{:S(2)}) async-start(f32[64,2,512]{2,1,0:T(2,128)} %get-tuple-element.27), calls=%async_computation | async-start | bytes 524288 | tf_op jit(solution)/shard_map/all_to_all | solution.py:377
  88.5 10.0 %collective-permute-start.1 = (f32[8,512]{1,0:T(8,128)S(1)}, f32[8,512]{1,0:T(8,128)S(1)}, u32[]{:S(2)}, u32[]{:S(2)}) collective-permute-start(f32[8,512]{1,0:T(8,128)S(1)} %get-tuple-element.28), channel_id=1, source_target_pairs={{8,0},{16,8},{24,16},{32,24},{40,32},{48,40},{56,48},{64,56},{72,6... | collective-permute-start | bytes 49160 | tf_op jit(solution)/shard_map/ppermute | solution.py:375
  119.2 21.1 %all-to-all-start.1 = ((f32[64,1,512]{2,1,0:T(1,128)}), f32[64,1,512]{2,1,0:T(1,128)S(1)}, u32[]{:S(2)}, u32[]{:S(2)}) async-start(f32[64,1,512]{2,1,0:T(1,128)} %get-tuple-element.32), calls=%async_computation.1 | async-start | bytes 262144 | tf_op jit(solution)/shard_map/all_to_all | solution.py:383
  128.6 5.4 %collective-permute-start.3 = (f32[8,512]{1,0:T(8,128)}, f32[8,512]{1,0:T(8,128)S(1)}, u32[]{:S(2)}, u32[]{:S(2)}) collective-permute-start(f32[8,512]{1,0:T(8,128)} %get-tuple-element.35), channel_id=1, source_target_pairs={{8,0},{16,8},{24,16},{32,24},{40,32},{48,40},{56,48},{64,56},{72,6... | collective-permute-start | bytes 49160 | tf_op jit(solution)/shard_map/ppermute | solution.py:382
  140.2 1.0 copy-start.14
  141.2 1.0 copy-start.15
  155.8 10.8 %collective-permute-start.4 = (bf16[4,192,512]{2,1,0:T(8,128)(2,1)}, bf16[4,192,512]{2,1,0:T(8,128)(2,1)}, u32[]{:S(2)}, u32[]{:S(2)}) collective-permute-start(bf16[4,192,512]{2,1,0:T(8,128)(2,1)} %bitcast.5.own_ref), channel_id=1, source_target_pairs={{0,1},{1,0},{2,3},{3,2},{4,5},{5,4},{6,7},{7,6},{8,9},{9,8},{10,11... | collective-permute-start | bytes 2359304 | tf_op jit(solution)/shard_map/ppermute | solution.py:386
  162.1 1.0 copy-start.10
  163.1 1.0 copy-start.11
  164.1 1.0 copy-start.12
Sparse Core Ops, SparseCore 0:
  11.6 100.9 all-gather.4
  114.7 40.6 all-gather.6

commit v7 on v5

--- a/solution.py
+++ b/solution.py
@@ -288,8 +288,8 @@
     def add(first, second):
         dims = (((1,), (1,)), ((), ()))
         acc[...] += lax.dot_general(
-            first, w_ref[:, :half], dims, preferred_element_type=F32
-        ) + lax.dot_general(second, w_ref[:, half:], dims, preferred_element_type=F32)
+            w_ref[:, :half], first, dims, preferred_element_type=F32
+        ) + lax.dot_general(w_ref[:, half:], second, dims, preferred_element_type=F32)
 
     @pl.when(core_ref[0] == 0)
     def _():
@@ -301,7 +301,7 @@
 
     @pl.when(step == pl.num_programs(0) - 1)
     def _():
-        out_ref[...] = acc[...].astype(BF16)
+        out_ref[...] = acc[...].T.astype(BF16)
 
 
 def input_grad(core, own, other, weights):
@@ -317,7 +317,7 @@
         ],
         out_specs=pl.BlockSpec((rows, weights.shape[0]), lambda i: (0, 0)),
         out_shape=jax.ShapeDtypeStruct((rows, weights.shape[0]), BF16),
-        scratch_shapes=[pltpu.VMEM((rows, weights.shape[0]), F32)],
+        scratch_shapes=[pltpu.VMEM((weights.shape[0], rows), F32)],
         compiler_params=pltpu.CompilerParams(vmem_limit_bytes=VMEM_WHOLE),
     )(core, own, other, weights)
 

time: 174 us -> 174 us (level)
  no operation moved by 1% of the time
where the time goes in v7:
time: 174 us; the launch traced here: 173 us
  blocking collectives  70.3 us (40%)
  starting transfers between devices  40.2 us (23%)
  waiting for transfers between devices  24 us (14%)
  Pallas kernels  16.4 us (9%)
  between operations  14.3 us (8%)
  local copies, waits for them, and re-layouts  7.92 us (5%)
    all_gather x1, blocking collectives, shards(): in_part = lax.all_gather(w_in, 'y', axis=0, tiled=True)  22.3 us
    all_to_all x1, blocking collectives, shards(): out_part = lax.all_to_all(spread, 'y', 0, 0).reshape(-1, w_out.shape[1])  22 us
    all_to_all x1, starting transfers between devices, shards(): carries = lax.all_to_all(carry, SEQ, 0, 0)  15.9 us
    all_gather x1, blocking collectives, shards(): out_own = lax.all_gather(d_out, 'x')  13.7 us
    all_gather x1, blocking collectives, shards(): own = lax.all_gather(d_branch, 'x')  12.3 us
    ppermute x1, starting transfers between devices, shards(): out_other = lax.ppermute(out_own, 'k', cores)  11.4 us
    ppermute x1, waiting for transfers between devices, shards(): next_a = lax.ppermute(front_a, SEQ, backward)  9.68 us
    ppermute x1, starting transfers between devices, shards(): other = lax.ppermute(own, 'k', cores)  8.96 us
  transfers between devices with their start and end apart: 8, of which 6 were waited for; matrix products, arithmetic and copies ran while one was open for 0% of the time, Pallas kernels for 6%

profile of v7, /device:TPU:1, one launch (start us, length us, event | category | flops | bytes accessed | tf_op | source)
XLA Modules:
  0.0 173.2 jit_solution(8070127960850664813)
XLA Ops:
  7.2 0.0 copy-start.13
  7.2 0.0 copy-start.18
  7.2 0.0 copy-start.16
  7.2 0.0 copy-start.7
  7.2 0.0 copy-start
  7.2 0.0 copy-start.14
  7.2 0.0 all-gather.5.cloned.1.call-start
  7.3 1.1 broadcast_in_dim.27
  8.3 22.0 %all_to_all.10 = bf16[8,8,4096]{2,1,0:T(8,128)(2,1)} all-to-all(bf16[8,8,4096]{2,1,0:T(8,128)(2,1)S(1)} %broadcast_in_dim.27), channel_id=1, replica_groups=mesh['z'=8,'y'=8,'x'=4,'k'=2] {'y'}, dimensions={0} | all-to-all | bytes 1048576 | tf_op jit(solution)/shard_map/all_to_all | solution.py:346
  30.3 0.0 all-gather.5.cloned.1.call-update
  30.4 0.0 all-gather.7.cloned.1.call-start
  30.4 22.3 %all_gather.24 = bf16[64,4096]{1,0:T(8,128)(2,1)} all-gather(bf16[8,4096]{1,0:T(8,128)(2,1)} %param.18), channel_id=1, replica_groups=mesh['z'=8,'y'=8,'x'=4,'k'=2] {'y'}, dimensions={0}, use_global_device_ids=true | all-gather | bytes 589824 | tf_op jit(solution)/shard_map/all_gather | solution.py:349
  52.7 0.0 all-gather.7.cloned.1.call-update
  52.7 13.7 %all-gather = bf16[768,512]{1,0:T(8,128)(2,1)S(1)} all-gather(bf16[192,512]{1,0:T(8,128)(2,1)} %param.10), channel_id=2, replica_groups=mesh['z'=8,'y'=8,'x'=4,'k'=2] {'x'}, dimensions={0}, use_global_device_ids=true | all-gather | bytes 983040 | tf_op jit(solution)/shard_map/all_gather | solution.py:351
  66.4 0.0 copy-start.17
  66.4 11.4 %collective-permute-start = (bf16[4,192,512]{2,1,0:T(8,128)(2,1)S(1)}, bf16[4,192,512]{2,1,0:T(8,128)(2,1)}, u32[]{:S(2)}, u32[]{:S(2)}) collective-permute-start(bf16[4,192,512]{2,1,0:T(8,128)(2,1)S(1)} %bitcast.10), channel_id=1, source_target_pairs={{0,1},{1,0},{2,3},{3,2},{4,5},{5,4},{6,7},{7,6},{8,9},{9,8},{10,11... | collective-permute-start | bytes 2359304 | tf_op jit(solution)/shard_map/ppermute | solution.py:352
  77.8 0.0 copy-done.13
  77.8 1.3 collective-permute-start.1
  79.2 0.0 copy-done.18
  79.2 0.1 select_reduce_fusion
  79.2 0.7 collective-permute-done.1.prev_ref
  80.0 0.0 copy-done.16
  80.0 0.0 copy-done.7
  80.0 0.0 copy-done
  80.0 0.0 copy-done.14
  80.0 2.4 %shard_map.129 = (f32[192,512]{1,0:T(8,128)S(1)}, f32[192,512]{1,0:T(8,128)S(1)}, f32[192,512]{1,0:T(8,128)S(1)}, f32[192,512]{1,0:T(8,128)S(1)}, f32[192,512]{1...) custom-call(bf16[192,512]{1,0:T(8,128)(2,1)S(1)} %copy-done.13, ...), custom_call_target="tpu_custom_call" | custom-call | tf_op jit(solution)/shard_map/pallas_call | solution.py:111
  82.4 0.0 copy-start.2
  82.4 0.7 copy-done.2
  83.1 0.0 copy-start.4
  83.1 0.7 copy-done.4
  83.9 0.0 copy-start.9
  83.9 0.8 copy-done.9
  84.6 0.0 copy-start.15
  84.6 0.6 copy-done.15
  85.2 1.3 collective-permute-start.2
  86.5 4.3 %collective-permute-done.2.front_b_ref = f32[8,512]{1,0:T(8,128)S(1)} collective-permute-done((f32[8,512]{1,0:T(8,128)S(1)}, f32[8,512]{1,0:T(8,128)S(1)}, u32[]{:S(2)}, u32[]{:S(2)}) %collective-permute-start.2) | collective-permute-done | bytes 16416 | tf_op jit(solution)/shard_map/ppermute | solution.py:361
  90.8 0.0 collective-permute-done.other_ref
  90.8 0.7 all-gather.5.cloned.1.call-done.w_ref
  91.5 0.0 copy-done.17
  91.5 0.0 copy-start.1
  91.5 0.0 copy-start.3
  91.5 0.0 copy-start.5
  91.5 0.0 copy-start.6
  91.5 6.9 %shard_map.130 = (f32[192,512]{1,0:T(8,128)}, f32[192,512]{1,0:T(8,128)}, f32[192,512]{1,0:T(8,128)}, f32[8,512]{1,0:T(8,128)}, f32[64,3,512]{2,1,0:T(4,128)}) custom-call(s32[1]{0:T(128)} %bitcast.core_ref, bf16[4,192,512]{2,1,0:T(8,128)(2,1)} %bitcast.11, bf16[4,192,512]{2,1,0:T(8,128)(2,1)} %collective-permute-done.other_ref, ...), custom_call_target="tpu_custom_call" | custom-call | tf_op jit(solution)/shard_map/pallas_call | solution.py:174
  98.4 15.9 %all-to-all-start.1 = ((f32[64,3,512]{2,1,0:T(4,128)}), f32[64,3,512]{2,1,0:T(4,128)S(1)}, u32[]{:S(2)}, u32[]{:S(2)}) async-start(f32[64,3,512]{2,1,0:T(4,128)} %get-tuple-element.34), calls=%async_computation.1 | async-start | bytes 1048576 | tf_op jit(solution)/shard_map/all_to_all | solution.py:368
  114.4 1.3 collective-permute-start.3
  115.7 9.7 %collective-permute-done.3.front_a_ref = f32[8,512]{1,0:T(8,128)S(1)} collective-permute-done((f32[8,512]{1,0:T(8,128)}, f32[8,512]{1,0:T(8,128)S(1)}, u32[]{:S(2)}, u32[]{:S(2)}) %collective-permute-start.3) | collective-permute-done | bytes 16416 | tf_op jit(solution)/shard_map/ppermute | solution.py:367
  125.4 4.7 %all-to-all-done.1.carry_ref = f32[64,3,512]{2,1,0:T(4,128)S(1)} async-done(((f32[64,3,512]{2,1,0:T(4,128)}), f32[64,3,512]{2,1,0:T(4,128)S(1)}, u32[]{:S(2)}, u32[]{:S(2)}) %all-to-all-start.1) | async-done | bytes 393248 | tf_op jit(solution)/shard_map/all_to_all | solution.py:368
  130.0 1.0 copy-done.8
  131.0 0.5 shard_map.131
  131.5 12.3 %all-gather.1 = bf16[768,512]{1,0:T(8,128)(2,1)} all-gather(bf16[192,512]{1,0:T(8,128)(2,1)S(1)} %get-tuple-element.39), channel_id=3, replica_groups=mesh['z'=8,'y'=8,'x'=4,'k'=2] {'x'}, dimensions={0}, use_global_device_ids=true | all-gather | bytes 983040 | tf_op jit(solution)/shard_map/all_gather | solution.py:370
  143.8 9.0 %collective-permute-start.4 = (bf16[4,192,512]{2,1,0:T(8,128)(2,1)}, bf16[4,192,512]{2,1,0:T(8,128)(2,1)}, u32[]{:S(2)}, u32[]{:S(2)}) collective-permute-start(bf16[4,192,512]{2,1,0:T(8,128)(2,1)} %bitcast.6.own_ref), channel_id=1, source_target_pairs={{0,1},{1,0},{2,3},{3,2},{4,5},{5,4},{6,7},{7,6},{8,9},{9,8},{10,11... | collective-permute-start | bytes 2359304 | tf_op jit(solution)/shard_map/ppermute | solution.py:371
  152.8 0.0 copy-done.1
  152.8 0.0 copy-done.3
  152.8 0.0 copy-done.5
  152.8 0.0 copy-done.6
  152.8 0.0 copy-start.10
  152.8 1.0 copy-done.10
  153.8 1.0 copy-done.11
  154.8 1.0 copy-done.12
  155.8 1.5 shard_map.133
  157.3 3.9 %all-gather.7.cloned.1.call-done.w_ref = bf16[512,4096]{1,0:T(8,128)(2,1)} async-done(((bf16[64,4096]{1,0:T(8,128)(2,1)}), bf16[512,4096]{1,0:T(8,128)(2,1)}) %all-gather.7.cloned.1.call-update) | async-done | bytes 4194320 | tf_op jit(solution)/shard_map/all_gather | solution.py:350
  161.2 0.0 collective-permute-done.4.other_ref
  161.2 5.2 %shard_map.132 = bf16[192,512]{1,0:T(8,128)(2,1)} custom-call(s32[1]{0:T(128)} %bitcast.core_ref, bf16[4,192,512]{2,1,0:T(8,128)(2,1)} %bitcast.6.own_ref, bf16[4,192,512]{2,1,0:T(8,128)(2,1)} %collective-permute-done.4.other_ref, bf16[512,4096]{1,0:T(8,128)(2,1)} %all-gather.7.cloned.1.call-done.w_ref), custom_call_target="tpu_custom_call" | custom-call | tf_op jit(solution)/shard_map/pallas_call | solution.py:309
  (5 shorter events, 0.0 us)
Async XLA Ops:
  7.2 70.7 %copy-start.13 = (bf16[192,512]{1,0:T(8,128)(2,1)S(1)}, bf16[192,512]{1,0:T(8,128)(2,1)}, u32[]{:S(2)}) copy-start(bf16[192,512]{1,0:T(8,128)(2,1)} %x_ref.1) | copy-start | bytes 589828
  7.2 72.0 %copy-start.18 = (s32[512]{0:T(512)S(1)}, s32[512]{0:T(512)}, u32[]{:S(2)}) copy-start(s32[512]{0:T(512)} %param.17) | copy-start | bytes 6148
  7.2 72.8 %copy-start.16 = (f32[512]{0:T(512)S(1)}, f32[512]{0:T(512)}, u32[]{:S(2)}) copy-start(f32[512]{0:T(512)} %param.16) | copy-start | bytes 6148
  7.2 72.8 %copy-start.7 = (bf16[192,512]{1,0:T(8,128)(2,1)S(1)}, bf16[192,512]{1,0:T(8,128)(2,1)}, u32[]{:S(2)}) copy-start(bf16[192,512]{1,0:T(8,128)(2,1)} %rec_ref.3) | copy-start | bytes 589828
  7.2 72.8 %copy-start = (bf16[192,512]{1,0:T(8,128)(2,1)S(1)}, bf16[192,512]{1,0:T(8,128)(2,1)}, u32[]{:S(2)}) copy-start(bf16[192,512]{1,0:T(8,128)(2,1)} %inw_ref.5) | copy-start | bytes 589828
  7.2 72.8 %copy-start.14 = (f32[4,512]{1,0:T(4,128)S(1)}, f32[4,512]{1,0:T(4,128)}, u32[]{:S(2)}) copy-start(f32[4,512]{1,0:T(4,128)} %cw_ref.3) | copy-start | bytes 24580
  7.2 84.3 %all-gather.5.cloned.1.call-start = ((), (), s32[]{:S(2)}) async-start(), calls=%async_computation.2 | async-start | bytes 4718592 | tf_op jit(solution)/shard_map/all_gather | solution.py:348
  30.4 130.8 %all-gather.7.cloned.1.call-start = ((), (), s32[]{:S(2)}) async-start(), calls=%async_computation.3 | async-start | bytes 4718592 | tf_op jit(solution)/shard_map/all_gather | solution.py:350
  66.4 25.1 %copy-start.17 = (bf16[768,512]{1,0:T(8,128)(2,1)}, bf16[768,512]{1,0:T(8,128)(2,1)S(1)}, u32[]{:S(2)}) copy-start(bf16[768,512]{1,0:T(8,128)(2,1)S(1)} %all-gather) | copy-start | bytes 2359300
  66.4 24.3 %collective-permute-start = (bf16[4,192,512]{2,1,0:T(8,128)(2,1)S(1)}, bf16[4,192,512]{2,1,0:T(8,128)(2,1)}, u32[]{:S(2)}, u32[]{:S(2)}) collective-permute-start(bf16[4,192,512]{2,1,0:T(8,128)(2,1)S(1)} %bitcast.10), channel_id=1, source_target_pairs={{0,1},{1,0},{2,3},{3,2},{4,5},{5,4},{6,7},{7,6},{8,9},{9,8},{10,11... | collective-permute-start | bytes 2359304 | tf_op jit(solution)/shard_map/ppermute | solution.py:352
  77.8 2.1 %collective-permute-start.1 = (bf16[16,512]{1,0:T(8,128)(2,1)S(1)}, bf16[16,512]{1,0:T(8,128)(2,1)S(1)}, u32[]{:S(2)}, u32[]{:S(2)}) collective-permute-start(bf16[16,512]{1,0:T(8,128)(2,1)S(1)} %slice.3), channel_id=1, source_target_pairs={{0,8},{8,16},{16,24},{24,32},{32,40},{40,48},{48,56},{56,64},{64,7... | collective-permute-start | bytes 49160 | tf_op jit(solution)/shard_map/ppermute | solution.py:353
  82.4 0.7 copy-start.2
  83.1 0.7 copy-start.4
  83.9 0.8 copy-start.9
  84.6 0.6 copy-start.15
  85.2 5.5 %collective-permute-start.2 = (f32[8,512]{1,0:T(8,128)S(1)}, f32[8,512]{1,0:T(8,128)S(1)}, u32[]{:S(2)}, u32[]{:S(2)}) collective-permute-start(f32[8,512]{1,0:T(8,128)S(1)} %get-tuple-element.31), channel_id=1, source_target_pairs={{8,0},{16,8},{24,16},{32,24},{40,32},{48,40},{56,48},{64,56},{72,6... | collective-permute-start | bytes 49160 | tf_op jit(solution)/shard_map/ppermute | solution.py:361
  91.5 61.3 %copy-start.1 = (bf16[192,512]{1,0:T(8,128)(2,1)S(1)}, bf16[192,512]{1,0:T(8,128)(2,1)}, u32[]{:S(2)}) copy-start(bf16[192,512]{1,0:T(8,128)(2,1)} %inw_ref.5) | copy-start | bytes 589828
  91.5 61.3 %copy-start.3 = (f32[192,512]{1,0:T(8,128)S(1)}, f32[192,512]{1,0:T(8,128)}, u32[]{:S(2)}) copy-start(f32[192,512]{1,0:T(8,128)} %copy-done.2) | copy-start | bytes 1179652
  91.5 61.3 %copy-start.5 = (f32[192,512]{1,0:T(8,128)S(1)}, f32[192,512]{1,0:T(8,128)}, u32[]{:S(2)}) copy-start(f32[192,512]{1,0:T(8,128)} %copy-done.4) | copy-start | bytes 1179652
  91.5 61.3 %copy-start.6 = (bf16[192,512]{1,0:T(8,128)(2,1)S(1)}, bf16[192,512]{1,0:T(8,128)(2,1)}, u32[]{:S(2)}) copy-start(bf16[192,512]{1,0:T(8,128)(2,1)} %gate_ref.3) | copy-start | bytes 589828
  98.4 31.6 %all-to-all-start.1 = ((f32[64,3,512]{2,1,0:T(4,128)}), f32[64,3,512]{2,1,0:T(4,128)S(1)}, u32[]{:S(2)}, u32[]{:S(2)}) async-start(f32[64,3,512]{2,1,0:T(4,128)} %get-tuple-element.34), calls=%async_computation.1 | async-start | bytes 1048576 | tf_op jit(solution)/shard_map/all_to_all | solution.py:368
  114.4 11.0 %collective-permute-start.3 = (f32[8,512]{1,0:T(8,128)}, f32[8,512]{1,0:T(8,128)S(1)}, u32[]{:S(2)}, u32[]{:S(2)}) collective-permute-start(f32[8,512]{1,0:T(8,128)} %get-tuple-element.37), channel_id=1, source_target_pairs={{8,0},{16,8},{24,16},{32,24},{40,32},{48,40},{56,48},{64,56},{72,6... | collective-permute-start | bytes 49160 | tf_op jit(solution)/shard_map/ppermute | solution.py:367
  130.0 1.0 copy-start.8
  143.8 17.4 %collective-permute-start.4 = (bf16[4,192,512]{2,1,0:T(8,128)(2,1)}, bf16[4,192,512]{2,1,0:T(8,128)(2,1)}, u32[]{:S(2)}, u32[]{:S(2)}) collective-permute-start(bf16[4,192,512]{2,1,0:T(8,128)(2,1)} %bitcast.6.own_ref), channel_id=1, source_target_pairs={{0,1},{1,0},{2,3},{3,2},{4,5},{5,4},{6,7},{7,6},{8,9},{9,8},{10,11... | collective-permute-start | bytes 2359304 | tf_op jit(solution)/shard_map/ppermute | solution.py:371
  152.8 1.0 copy-start.10
  153.8 1.0 copy-start.11
  154.8 1.0 copy-start.12
Sparse Core Ops, SparseCore 0:
  30.5 60.9 all-gather.4
  93.6 67.5 all-gather.6

commit v8 on v4

--- a/solution.py
+++ b/solution.py
@@ -1,3 +1,5 @@
+import functools
+
 import jax
 import jax.numpy as jnp
 from jax import lax
@@ -277,57 +279,55 @@
     )(place, carry, kappa, d_lru, *arrays)
 
 
-def input_kernel(core_ref, own_ref, other_ref, first_ref, rest_ref, out_ref, acc):
+def input_kernel(lead, core_ref, blocks_ref, first_ref, rest_ref, start_ref, out_ref, acc):
     step = pl.program_id(0)
     half = first_ref.shape[1] // 2
 
-    def product(left, right, w_ref):
-        dims = (((1,), (1,)), ((), ()))
-        return lax.dot_general(
-            left, w_ref[:, :half], dims, preferred_element_type=F32
-        ) + lax.dot_general(right, w_ref[:, half:], dims, preferred_element_type=F32)
-
-    def add(left, right):
-        @pl.when(step == 0)
+    @pl.when(step == 0)
+    def _():
+        acc[...] = start_ref[...]
+
+    def add(w_ref, at):
+        acc[...] += lax.dot_general(
+            blocks_ref[0], w_ref[:, at : at + half], (((1,), (1,)), ((), ())),
+            preferred_element_type=F32,
+        )
+
+    for core, at in ((0, 0), (1, half)):
+
+        @pl.when((core_ref[0] == core) & (step < lead))
         def _():
-            acc[...] = product(left[0], right[0], first_ref)
-
-        @pl.when(step != 0)
+            add(first_ref, at)
+
+        @pl.when((core_ref[0] == core) & (step >= lead))
         def _():
-            acc[...] += product(left[0], right[0], rest_ref)
-
-    @pl.when(core_ref[0] == 0)
-    def _():
-        add(own_ref, other_ref)
-
-    @pl.when(core_ref[0] != 0)
-    def _():
-        add(other_ref, own_ref)
+            add(rest_ref, at)
 
     @pl.when(step == pl.num_programs(0) - 1)
     def _():
-        out_ref[...] = acc[...].astype(BF16)
-
-
-def input_grad(core, own, other, first, rest):
-    steps, rows, width = own.shape
+        out_ref[...] = acc[...].astype(out_ref.dtype)
+
+
+def input_grad(core, blocks, first, rest, start, dtype):
+    steps, rows, width = blocks.shape
     feats = first.shape[0]
-    at = first.shape[1] // (2 * width) - 1
-    return pl.pallas_call(
-        input_kernel,
+    lead = steps - rest.shape[1] // (2 * width)
+    at = first.shape[1] // (2 * width) - lead
+    return pl.pallas_call(
+        functools.partial(input_kernel, lead),
         grid=(steps,),
         in_specs=[
             pl.BlockSpec(memory_space=pltpu.SMEM),
             pl.BlockSpec((1, rows, width), lambda i: (i, 0, 0)),
-            pl.BlockSpec((1, rows, width), lambda i: (i, 0, 0)),
-            pl.BlockSpec((feats, 2 * width), lambda i: (0, at)),
-            pl.BlockSpec((feats, 2 * width), lambda i: (0, jnp.maximum(i - 1, 0))),
+            pl.BlockSpec((feats, 2 * width), lambda i: (0, at + jnp.minimum(i, lead - 1))),
+            pl.BlockSpec((feats, 2 * width), lambda i: (0, jnp.maximum(i - lead, 0))),
+            pl.BlockSpec((rows, feats), lambda i: (0, 0)),
         ],
         out_specs=pl.BlockSpec((rows, feats), lambda i: (0, 0)),
-        out_shape=jax.ShapeDtypeStruct((rows, feats), BF16),
+        out_shape=jax.ShapeDtypeStruct((rows, feats), dtype),
         scratch_shapes=[pltpu.VMEM((rows, feats), F32)],
         compiler_params=pltpu.CompilerParams(vmem_limit_bytes=VMEM_WHOLE),
-    )(core, own, other, first, rest)
+    )(core, blocks, first, rest, start)
 
 
 def shards(
@@ -350,9 +350,10 @@
     backward = [(i + 1, i) for i in range(seq_count - 1)]
     cores = [(0, 1), (1, 0)]
 
-    first = jnp.concatenate([w_out, w_in[:, : 2 * width]], axis=1)
+    half = w_in.shape[1] // 2
+    first = jnp.concatenate([w_out, w_in[:, :half]], axis=1)
     first = lax.all_gather(first, SEQ, axis=0, tiled=True)
-    rest = lax.all_gather(w_in[:, 2 * width :], "y", axis=0, tiled=True)
+    rest = lax.all_gather(w_in[:, half:], "y", axis=0, tiled=True)
     in_rows = lax.all_gather(rest, "z", axis=0, tiled=True)
     out_own = lax.all_gather(d_out, "x")
     out_other = lax.ppermute(out_own, "k", cores)
@@ -379,7 +380,9 @@
         place, carries, kappa, d_lru, adj_local, post, cum_decay, local_states, decay,
         beta, conv_out, gate_branch, recurrence_gate, input_gate, log_decay,
     )
-    d_input = input_grad(core, own, other, first, in_rows)
+    start = jnp.zeros((tok_rows, first.shape[0]), F32)
+    start = input_grad(core, own, first, in_rows, start, F32)
+    d_input = input_grad(1 - core, other, first, in_rows, start, BF16)
     return (d_input, d_gate, d_recurrence_gate, d_input_gate)
 
 

time: 177 us -> 189 us (1.068)
  waiting for transfers between devices: 44.1 us -> 49.6 us
  Pallas kernels: 16.8 us -> 21.6 us
  local copies, waits for them, and re-layouts: 13.2 us -> 17.4 us
    pallas_call x1 -> x2, Pallas kernels: 5.55 us -> 10.5 us  [input_grad(): pl.pallas_call(functools.partial(input_kernel, lead), grid=(steps,), in_s...]
    all_gather x1, waiting for transfers between devices: 25.1 us -> 29.5 us  [shards(): first = lax.all_gather(first, SEQ, axis=0, tiled=True)]
    unnamed x42 -> x58, local copies, waits for them, and re-layouts: 11 us -> 15.1 us
  transfers between devices with their start and end apart: 8 -> 8, of which waited for: 6 -> 5; matrix products, arithmetic and copies ran while one was open for 1% -> 1% of each run, Pallas kernels for 6% -> 9%
where the time goes in v8:
time: 189 us; the launch traced here: 188 us
  waiting for transfers between devices  49.6 us (26%)
  blocking collectives  47 us (25%)
  starting transfers between devices  35.8 us (19%)
  Pallas kernels  21.6 us (11%)
  local copies, waits for them, and re-layouts  17.4 us (9%)
  between operations  14.2 us (8%)
  other arithmetic  2.27 us (1%)
    all_gather x1, waiting for transfers between devices, shards(): first = lax.all_gather(first, SEQ, axis=0, tiled=True)  29.5 us
    all_gather x1, blocking collectives, shards(): rest = lax.all_gather(w_in[:, half:], 'y', axis=0, tiled=True)  22.9 us
    unnamed x58, local copies, waits for them, and re-layouts  15.1 us
    ppermute x1, starting transfers between devices, shards(): out_other = lax.ppermute(out_own, 'k', cores)  14.5 us
    all_gather x1, blocking collectives, shards(): own = lax.all_gather(d_branch, 'x')  12.4 us
    all_gather x1, blocking collectives, shards(): out_own = lax.all_gather(d_out, 'x')  11.7 us
    pallas_call x2, Pallas kernels, input_grad(): pl.pallas_call(functools.partial(input_kernel, lead), grid=(steps,), in_s...  10.5 us
    ppermute x1, waiting for transfers between devices, shards(): next_a = lax.ppermute(front_a, SEQ, backward)  10.3 us
  transfers between devices with their start and end apart: 8, of which 5 were waited for; matrix products, arithmetic and copies ran while one was open for 1% of the time, Pallas kernels for 9%

profile of v8, /device:TPU:1, one launch (start us, length us, event | category | flops | bytes accessed | tf_op | source)
XLA Modules:
  0.0 187.9 jit_solution(14046849417547429205)
XLA Ops:
  7.2 0.0 all-gather.5.cloned.1.call-start
  7.2 0.8 fusion.1
  8.0 1.5 pad_maximum_fusion
  9.5 0.0 all-gather.5.cloned.1.call-update
  9.5 0.0 all-gather.7.cloned.1.call-start
  9.6 22.9 %all_gather.26 = bf16[64,2048]{1,0:T(8,128)(2,1)} all-gather(bf16[8,2048]{1,0:T(8,128)(2,1)S(1)} %get-tuple-element.46), channel_id=1, replica_groups=mesh['z'=8,'y'=8,'x'=4,'k'=2] {'y'}, dimensions={0}, use_global_device_ids=true | all-gather | bytes 294912 | tf_op jit(solution)/shard_map/all_gather | solution.py:356
  32.5 0.0 all-gather.7.cloned.1.call-update
  32.5 11.7 %all-gather = bf16[768,512]{1,0:T(8,128)(2,1)S(1)} all-gather(bf16[192,512]{1,0:T(8,128)(2,1)} %param.10), channel_id=2, replica_groups=mesh['z'=8,'y'=8,'x'=4,'k'=2] {'x'}, dimensions={0}, use_global_device_ids=true | all-gather | bytes 983040 | tf_op jit(solution)/shard_map/all_gather | solution.py:358
  44.2 14.5 %collective-permute-start = (bf16[4,192,512]{2,1,0:T(8,128)(2,1)S(1)}, bf16[4,192,512]{2,1,0:T(8,128)(2,1)S(1)}, u32[]{:S(2)}, u32[]{:S(2)}) collective-permute-start(bf16[4,192,512]{2,1,0:T(8,128)(2,1)S(1)} %bitcast.9), channel_id=1, source_target_pairs={{0,1},{1,0},{2,3},{3,2},{4,5},{5,4},{6,7},{7,6},{8,9},{9,8},{10,11... | collective-permute-start | bytes 2359304 | tf_op jit(solution)/shard_map/ppermute | solution.py:359
  58.7 0.7 slice.10
  59.4 1.3 collective-permute-start.1
  60.7 0.8 select_reduce_fusion
  61.5 0.1 collective-permute-done.1.prev_ref
  61.5 0.9 copy-done
  62.5 0.9 copy-done.6
  63.4 0.9 copy-done.16
  64.3 0.7 copy-done.17
  65.0 0.7 copy-done.24
  65.7 2.4 %shard_map.129 = (f32[192,512]{1,0:T(8,128)S(1)}, f32[192,512]{1,0:T(8,128)S(1)}, f32[192,512]{1,0:T(8,128)S(1)}, f32[192,512]{1,0:T(8,128)S(1)}, f32[192,512]{1...) custom-call(bf16[192,512]{1,0:T(8,128)(2,1)S(1)} %copy-done.16, ...), custom_call_target="tpu_custom_call" | custom-call | tf_op jit(solution)/shard_map/pallas_call | solution.py:113
  68.1 0.0 copy-done.19
  68.1 0.0 copy-start.2
  68.1 0.7 copy-done.2
  68.9 0.7 copy-done.4
  69.6 0.7 copy-done.10
  70.3 0.7 copy-done.12
  71.1 0.6 copy-done.23
  71.7 1.3 collective-permute-start.2
  73.0 4.2 %collective-permute-done.2.front_b_ref = f32[8,512]{1,0:T(8,128)S(1)} collective-permute-done((f32[8,512]{1,0:T(8,128)S(1)}, f32[8,512]{1,0:T(8,128)S(1)}, u32[]{:S(2)}, u32[]{:S(2)}) %collective-permute-start.2) | collective-permute-done | bytes 16416 | tf_op jit(solution)/shard_map/ppermute | solution.py:368
  77.1 0.6 copy-done.21
  77.7 0.0 collective-permute-done.other_ref
  77.7 29.5 %all-gather.5.cloned.1.call-done.w_ref.first_ref = bf16[512,6144]{1,0:T(8,128)(2,1)} async-done(((bf16[8,6144]{1,0:T(8,128)(2,1)}), bf16[512,6144]{1,0:T(8,128)(2,1)}) %all-gather.5.cloned.1.call-update) | async-done | bytes 6291472 | tf_op jit(solution)/shard_map/all_gather | solution.py:355
  107.3 0.0 copy-done.27
  107.3 0.0 copy-done.28
  107.3 6.8 %shard_map.130 = (f32[192,512]{1,0:T(8,128)}, f32[192,512]{1,0:T(8,128)}, f32[192,512]{1,0:T(8,128)}, f32[8,512]{1,0:T(8,128)}, f32[64,3,512]{2,1,0:T(4,128)}) custom-call(s32[1]{0:T(128)} %bitcast.core_ref, bf16[4,192,512]{2,1,0:T(8,128)(2,1)} %bitcast.10, bf16[4,192,512]{2,1,0:T(8,128)(2,1)} %copy-done.28, ...), custom_call_target="tpu_custom_call" | custom-call | tf_op jit(solution)/shard_map/pallas_call | solution.py:176
  114.1 9.1 %all-to-all-start = ((f32[64,3,512]{2,1,0:T(4,128)}), f32[64,3,512]{2,1,0:T(4,128)S(1)}, u32[]{:S(2)}, u32[]{:S(2)}) async-start(f32[64,3,512]{2,1,0:T(4,128)} %get-tuple-element.30), calls=%async_computation | async-start | bytes 1048576 | tf_op jit(solution)/shard_map/all_to_all | solution.py:375
  123.2 1.3 collective-permute-start.3
  124.5 10.3 %collective-permute-done.3.front_a_ref = f32[8,512]{1,0:T(8,128)S(1)} collective-permute-done((f32[8,512]{1,0:T(8,128)}, f32[8,512]{1,0:T(8,128)S(1)}, u32[]{:S(2)}, u32[]{:S(2)}) %collective-permute-start.3) | collective-permute-done | bytes 16416 | tf_op jit(solution)/shard_map/ppermute | solution.py:374
  134.8 5.5 %all-to-all-done.carry_ref = f32[64,3,512]{2,1,0:T(4,128)S(1)} async-done(((f32[64,3,512]{2,1,0:T(4,128)}), f32[64,3,512]{2,1,0:T(4,128)S(1)}, u32[]{:S(2)}, u32[]{:S(2)}) %all-to-all-start) | async-done | bytes 393248 | tf_op jit(solution)/shard_map/all_to_all | solution.py:375
  140.3 1.0 copy-done.9
  141.3 0.7 copy-done.18
  142.0 0.7 copy-done.22
  142.7 0.0 copy-start.8
  142.7 0.5 shard_map.131
  143.2 0.0 copy-start.25
  143.2 0.0 copy-start.11
  143.3 12.4 %all-gather.1 = bf16[768,512]{1,0:T(8,128)(2,1)} all-gather(bf16[192,512]{1,0:T(8,128)(2,1)S(1)} %get-tuple-element.35), channel_id=3, replica_groups=mesh['z'=8,'y'=8,'x'=4,'k'=2] {'x'}, dimensions={0}, use_global_device_ids=true | all-gather | bytes 983040 | tf_op jit(solution)/shard_map/all_gather | solution.py:377
  155.7 0.0 copy-done.25
  155.7 8.2 %collective-permute-start.4 = (bf16[4,192,512]{2,1,0:T(8,128)(2,1)}, bf16[4,192,512]{2,1,0:T(8,128)(2,1)}, u32[]{:S(2)}, u32[]{:S(2)}) collective-permute-start(bf16[4,192,512]{2,1,0:T(8,128)(2,1)} %bitcast.5.blocks_ref), channel_id=1, source_target_pairs={{0,1},{1,0},{2,3},{3,2},{4,5},{5,4},{6,7},{7,6},{8,9},{9,8},{10,11... | collective-permute-start | bytes 2359304 | tf_op jit(solution)/shard_map/ppermute | solution.py:378
  163.9 0.0 all-gather.7.cloned.1.call-done.rest_ref
  163.9 0.8 broadcast_in_dim.28.start_ref
  164.7 5.3 %shard_map.132.start_ref = f32[192,512]{1,0:T(8,128)} custom-call(s32[1]{0:T(128)} %bitcast.core_ref, bf16[4,192,512]{2,1,0:T(8,128)(2,1)} %bitcast.5.blocks_ref, bf16[512,6144]{1,0:T(8,128)(2,1)} %all-gather.5.cloned.1.call-done.w_ref.first_ref, bf16[512,2048]{1,0:T(8,128)(2,1)} %all-gather.7.cloned.1.call-done.rest_ref, f32[192,512]{1,0:T(8,128)} %broadcast_in_dim.28.start_ref), custom_call_target="tpu_custom_call" | custom-call | tf_op jit(solution)/shard_map/pallas_call | solution.py:316
  170.0 0.0 copy-done.5
  170.0 0.0 copy-done.7
  170.0 0.0 copy-done.8
  170.0 0.0 copy-done.11
  170.0 0.0 copy-start.13
  170.0 1.0 copy-done.13
  171.0 1.0 copy-done.14
  172.0 1.0 copy-done.15
  173.0 0.7 copy-done.20
  173.7 0.7 copy-done.26
  174.4 1.5 shard_map.134
  175.8 0.0 collective-permute-done.4.blocks_ref
  175.8 5.2 %shard_map.133 = bf16[192,512]{1,0:T(8,128)(2,1)} custom-call(s32[1]{0:T(128)S(6)} %sub.6.core_ref, bf16[4,192,512]{2,1,0:T(8,128)(2,1)} %collective-permute-done.4.blocks_ref, bf16[512,6144]{1,0:T(8,128)(2,1)} %all-gather.5.cloned.1.call-done.w_ref.first_ref, bf16[512,2048]{1,0:T(8,128)(2,1)} %all-gather.7.cloned.1.call-done.rest_ref, ...), custom_call_target="tpu_custom_call" | custom-call | tf_op jit(solution)/shard_map/pallas_call | solution.py:316
  (27 shorter events, 0.1 us)
Async XLA Ops:
  7.2 100.1 %all-gather.5.cloned.1.call-start = ((), (), s32[]{:S(2)}) async-start(), calls=%async_computation.1 | async-start | bytes 6389760 | tf_op jit(solution)/shard_map/all_gather | solution.py:355
  9.5 154.4 %all-gather.7.cloned.1.call-start = ((), (), s32[]{:S(2)}) async-start(), calls=%async_computation.2 | async-start | bytes 2359296 | tf_op jit(solution)/shard_map/all_gather | solution.py:357
  44.2 63.1 %copy-start.27 = (bf16[768,512]{1,0:T(8,128)(2,1)}, bf16[768,512]{1,0:T(8,128)(2,1)S(1)}, u32[]{:S(2)}) copy-start(bf16[768,512]{1,0:T(8,128)(2,1)S(1)} %all-gather) | copy-start | bytes 2359300
  44.2 33.6 %collective-permute-start = (bf16[4,192,512]{2,1,0:T(8,128)(2,1)S(1)}, bf16[4,192,512]{2,1,0:T(8,128)(2,1)S(1)}, u32[]{:S(2)}, u32[]{:S(2)}) collective-permute-start(bf16[4,192,512]{2,1,0:T(8,128)(2,1)S(1)} %bitcast.9), channel_id=1, source_target_pairs={{0,1},{1,0},{2,3},{3,2},{4,5},{5,4},{6,7},{7,6},{8,9},{9,8},{10,11... | collective-permute-start | bytes 2359304 | tf_op jit(solution)/shard_map/ppermute | solution.py:359
  59.4 2.1 %collective-permute-start.1 = (bf16[16,512]{1,0:T(8,128)(2,1)S(1)}, bf16[16,512]{1,0:T(8,128)(2,1)S(1)}, u32[]{:S(2)}, u32[]{:S(2)}) collective-permute-start(bf16[16,512]{1,0:T(8,128)(2,1)S(1)} %slice.10), channel_id=1, source_target_pairs={{0,8},{8,16},{16,24},{24,32},{32,40},{40,48},{48,56},{56,64},{64,7... | collective-permute-start | bytes 49160 | tf_op jit(solution)/shard_map/ppermute | solution.py:360
  61.5 6.6 %copy-start.19 = (f32[512]{0:T(512)}, f32[512]{0:T(512)S(1)}, u32[]{:S(2)}) copy-start(f32[512]{0:T(512)S(1)} %select_reduce_fusion) | copy-start | bytes 6148
  61.5 0.9 copy-start
  62.5 0.9 copy-start.6
  63.4 0.9 copy-start.16
  64.3 0.7 copy-start.17
  65.0 0.7 copy-start.24
  68.1 0.8 copy-start.2
  68.8 0.8 copy-start.4
  69.6 0.7 copy-start.10
  70.3 0.7 copy-start.12
  71.1 0.6 copy-start.23
  71.7 5.5 %collective-permute-start.2 = (f32[8,512]{1,0:T(8,128)S(1)}, f32[8,512]{1,0:T(8,128)S(1)}, u32[]{:S(2)}, u32[]{:S(2)}) collective-permute-start(f32[8,512]{1,0:T(8,128)S(1)} %get-tuple-element.28), channel_id=1, source_target_pairs={{8,0},{16,8},{24,16},{32,24},{40,32},{48,40},{56,48},{64,56},{72,6... | collective-permute-start | bytes 49160 | tf_op jit(solution)/shard_map/ppermute | solution.py:368
  77.1 0.6 copy-start.21
  77.7 29.5 %copy-start.28 = (bf16[4,192,512]{2,1,0:T(8,128)(2,1)}, bf16[4,192,512]{2,1,0:T(8,128)(2,1)S(1)}, u32[]{:S(2)}) copy-start(bf16[4,192,512]{2,1,0:T(8,128)(2,1)S(1)} %collective-permute-done.other_ref) | copy-start | bytes 2359300
  114.1 26.2 %all-to-all-start = ((f32[64,3,512]{2,1,0:T(4,128)}), f32[64,3,512]{2,1,0:T(4,128)S(1)}, u32[]{:S(2)}, u32[]{:S(2)}) async-start(f32[64,3,512]{2,1,0:T(4,128)} %get-tuple-element.30), calls=%async_computation | async-start | bytes 1048576 | tf_op jit(solution)/shard_map/all_to_all | solution.py:375
  123.2 11.6 %collective-permute-start.3 = (f32[8,512]{1,0:T(8,128)}, f32[8,512]{1,0:T(8,128)S(1)}, u32[]{:S(2)}, u32[]{:S(2)}) collective-permute-start(f32[8,512]{1,0:T(8,128)} %get-tuple-element.33), channel_id=1, source_target_pairs={{8,0},{16,8},{24,16},{32,24},{40,32},{48,40},{56,48},{64,56},{72,6... | collective-permute-start | bytes 49160 | tf_op jit(solution)/shard_map/ppermute | solution.py:374
  140.3 1.0 copy-start.9
  141.3 0.7 copy-start.18
  142.0 0.7 copy-start.22
  142.7 27.3 %copy-start.1 = (bf16[192,512]{1,0:T(8,128)(2,1)S(1)}, bf16[192,512]{1,0:T(8,128)(2,1)}, u32[]{:S(2)}) copy-start(bf16[192,512]{1,0:T(8,128)(2,1)} %inw_ref.5) | copy-start | bytes 589828
  142.7 27.3 %copy-start.3 = (f32[192,512]{1,0:T(8,128)S(1)}, f32[192,512]{1,0:T(8,128)}, u32[]{:S(2)}) copy-start(f32[192,512]{1,0:T(8,128)} %copy-done.2) | copy-start | bytes 1179652
  142.7 27.3 %copy-start.5 = (f32[192,512]{1,0:T(8,128)S(1)}, f32[192,512]{1,0:T(8,128)}, u32[]{:S(2)}) copy-start(f32[192,512]{1,0:T(8,128)} %copy-done.4) | copy-start | bytes 1179652
  142.7 27.3 %copy-start.7 = (bf16[192,512]{1,0:T(8,128)(2,1)S(1)}, bf16[192,512]{1,0:T(8,128)(2,1)}, u32[]{:S(2)}) copy-start(bf16[192,512]{1,0:T(8,128)(2,1)} %rec_ref.3) | copy-start | bytes 589828
  142.7 27.3 %copy-start.8 = (bf16[192,512]{1,0:T(8,128)(2,1)S(1)}, bf16[192,512]{1,0:T(8,128)(2,1)}, u32[]{:S(2)}) copy-start(bf16[192,512]{1,0:T(8,128)(2,1)} %gate_ref.3) | copy-start | bytes 589828
  143.2 12.4 %copy-start.25 = (f32[1,512]{1,0:T(1,128)}, f32[1,512]{1,0:T(1,128)S(1)}, u32[]{:S(2)}) copy-start(f32[1,512]{1,0:T(1,128)S(1)} %get-tuple-element.36.kappa_ref) | copy-start | bytes 6148
  143.2 26.8 %copy-start.11 = (f32[192,512]{1,0:T(8,128)S(1)}, f32[192,512]{1,0:T(8,128)}, u32[]{:S(2)}) copy-start(f32[192,512]{1,0:T(8,128)} %copy-done.10) | copy-start | bytes 1179652
  155.7 20.2 %collective-permute-start.4 = (bf16[4,192,512]{2,1,0:T(8,128)(2,1)}, bf16[4,192,512]{2,1,0:T(8,128)(2,1)}, u32[]{:S(2)}, u32[]{:S(2)}) collective-permute-start(bf16[4,192,512]{2,1,0:T(8,128)(2,1)} %bitcast.5.blocks_ref), channel_id=1, source_target_pairs={{0,1},{1,0},{2,3},{3,2},{4,5},{5,4},{6,7},{7,6},{8,9},{9,8},{10,11... | collective-permute-start | bytes 2359304 | tf_op jit(solution)/shard_map/ppermute | solution.py:378
  170.0 1.0 copy-start.13
  171.0 1.0 copy-start.14
  172.0 1.0 copy-start.15
  173.0 0.7 copy-start.20
  173.7 0.7 copy-start.26
Sparse Core Ops, SparseCore 0:
  11.6 95.6 all-gather.4
  109.3 48.9 all-gather.6
